TPU v7x, 256 devices: a whole 4x4x8 slice. The times are simulated.
256 devices in a mesh: replica: 8 (over z_lo, core), fsdp: 32 (over y, x, z_hi).
Axes of the slice: x: 4, y: 4, z: 8 (z_hi: 2, z_lo: 4; z = z_hi * 4 + z_lo), core: 2. Of those that a mesh axis runs over, the one named last changes fastest.
Arguments:
- activations: bfloat16 [8, 8192, 12288], P('replica', 'fsdp'), may hold values from -18 to 18
- norm_gain: bfloat16 [12288], replicated, may hold values from 0.25 to 1.75
- key_cotangent: bfloat16 [8, 8192, 512], P('replica', 'fsdp'), may hold values from -6 to 6
- key_weight: bfloat16 [8, 12288, 512], P('replica', 'fsdp'), may hold values from -6 to 6
- adam_first: float32 [8, 12288, 512], P('replica', 'fsdp'), may hold values from -6 to 6
- adam_second: float32 [8, 12288, 512], P('replica', 'fsdp'), may hold values from 0.05 to 1
- outer_codes: bfloat16 [8, 12288, 128], P('replica', 'fsdp'), may hold values from -127 to 127, as said below
- outer_scales: bfloat16 [8, 12288], P('replica', 'fsdp'), may hold values from 0.0009994507 to 0.0099487305
- global_fragment: float32 [12288, 128], P('fsdp'), may hold values from -6 to 6
- outer_momentum: float32 [12288, 128], P('fsdp'), may hold values from -4 to 4
- fragment_index: int32 [1], replicated, may hold values from 0 to 99999
Outputs:
- projected: bfloat16 [8, 8192, 512], P('replica', 'fsdp')
- new_weight: bfloat16 [8, 12288, 512], P('replica', 'fsdp')
- new_first: float32 [8, 12288, 512], P('replica', 'fsdp')
- new_second: float32 [8, 12288, 512], P('replica', 'fsdp')
- new_momentum: float32 [12288, 128], P('fsdp')
- new_global: float32 [12288, 128], P('fsdp')
Inputs may be any that keep to these rules, and one draw needn't show every extreme that they name: `outer_codes`: whole numbers held as bfloat16.
All inputs are finite; a program needn't handle non-finite values.
Results may differ from a plain program's by a relative error of at most 0.018.
Values may be sent and summed in bfloat16 or wider, within the bound.
No kernel may reach another device: no remote copies, remote signals or barrier semaphores. Data moves between devices by JAX's collectives and lax.ppermute only.
A program may use at most 128 MiB of HBM per device.

v0:
```python
import jax
import jax.numpy as jnp
from jax import lax
from jax.sharding import PartitionSpec as P

norm_epsilon = 1e-05
adam_epsilon = 1e-08
beta_one = 0.9
beta_two = 0.95
inner_rate = 0.02
decay_rate = 0.1
outer_beta = 0.9
outer_rate = 0.7
mix_weight = 0.5


def normalize(token_rows, norm_gain):
    widened = token_rows.astype(jnp.float32)
    mean_square = jnp.mean(widened * widened, axis=-1, keepdims=True)
    return (widened * lax.rsqrt(mean_square + norm_epsilon) * norm_gain.astype(jnp.float32)).astype(
        jnp.bfloat16
    )


def per_device(
    activations,
    norm_gain,
    key_cotangent,
    key_weight,
    adam_first,
    adam_second,
    outer_codes,
    outer_scales,
    global_fragment,
    outer_momentum,
    fragment_index,
):
    token_rows = activations[0]
    cotangent = key_cotangent[0]
    weight_shard = key_weight[0]
    feature_count = token_rows.shape[1]
    key_count = weight_shard.shape[1]
    factor = feature_count ** (-0.5)
    normed = normalize(token_rows, norm_gain)
    columns = normed
    summed = jnp.dot(
        columns,
        lax.all_gather(weight_shard, "fsdp", axis=0, tiled=True),
        preferred_element_type=jnp.float32,
    )
    projected = (factor * summed).astype(jnp.bfloat16)
    columns = normed
    gradient = lax.psum_scatter(
        (
            factor
            * lax.dot_general(
                columns, cotangent, (((0,), (0,)), ((), ())), preferred_element_type=jnp.float32
            )
        ).astype(jnp.bfloat16),
        "fsdp",
        scatter_dimension=0,
        tiled=True,
    ).astype(jnp.float32)
    moment_one = beta_one * adam_first[0] + (1.0 - beta_one) * gradient
    moment_two = beta_two * adam_second[0] + (1.0 - beta_two) * gradient * gradient
    master = weight_shard.astype(jnp.float32)
    stepped = master - inner_rate * (
        moment_one / (jnp.sqrt(moment_two) + adam_epsilon) + decay_rate * master
    )
    replicas = lax.axis_size("replica")
    every_code, every_scale = (
        lax.all_gather(outer_codes, "replica", axis=0, tiled=True),
        lax.all_gather(outer_scales, "replica", axis=0, tiled=True),
    )
    outer_delta = (
        jnp.sum(
            every_code.astype(jnp.float32) * every_scale.astype(jnp.float32)[:, :, None], axis=0
        )
        / replicas
    )
    momentum = outer_beta * outer_momentum + outer_delta
    refreshed = global_fragment - outer_rate * (outer_delta + outer_beta * momentum)
    head_width = global_fragment.shape[1]
    head_count = key_count // head_width
    offset = jnp.remainder(fragment_index[0], head_count) * head_width
    current = lax.dynamic_slice_in_dim(stepped, offset, head_width, 1)
    blended = mix_weight * current + (1.0 - mix_weight) * refreshed
    merged = lax.dynamic_update_slice_in_dim(stepped, blended, offset, 1)
    return (
        projected[None],
        merged.astype(jnp.bfloat16)[None],
        moment_one[None],
        moment_two[None],
        momentum,
        refreshed,
    )


def solution(mesh):
    in_specs = (
        P("replica", "fsdp", None),
        P(),
        P("replica", "fsdp", None),
        P("replica", "fsdp", None),
        P("replica", "fsdp", None),
        P("replica", "fsdp", None),
        P("replica", "fsdp", None),
        P("replica", "fsdp"),
        P("fsdp", None),
        P("fsdp", None),
        P(),
    )
    out_specs = (
        P("replica", "fsdp", None),
        P("replica", "fsdp", None),
        P("replica", "fsdp", None),
        P("replica", "fsdp", None),
        P("fsdp", None),
        P("fsdp", None),
    )
    return jax.shard_map(
        per_device, mesh=mesh, in_specs=in_specs, out_specs=out_specs, check_vma=False
    )
```

profile of v0, /device:TPU:32, one launch (start us, length us, event | category | flops | bytes accessed | tf_op | source)
XLA Modules:
  0.0 535.6 jit_solution(12291051265713133893)
XLA Ops:
  7.2 0.0 copy-start
  7.2 0.0 all-gather.4.cloned.1.call-start
  7.2 0.7 all-gather.4.cloned.1.call-update
  7.9 0.0 reduce-scatter.2.cloned.1.call-start
  8.0 0.7 convert_element_type.43
  8.7 4.1 fusion.2
  12.8 10.9 %multiply_convert_fusion = bf16[12288,512]{1,0:T(8,128)(2,1)} fusion(bf16[1,256,12288]{2,1,0:T(8,128)(2,1)} %param.11, f32[12288]{0:T(1024)S(1)} %convert_element_type.43, f32[256]{0:T(256)S(1)} %add_rsqrt_fusion, bf16[1,256,512]{2,1,0:T(8,128)(2,1)S(1)} %copy-done), kind=kOutput, calls=%fused_computation | convolution fusion | flops 3246391296 | bytes 19186688 | tf_op jit(solution)/shard_map/dot_general | solution.py:56
  23.7 0.0 reduce-scatter.2.cloned.1.call-update
  24.4 13.8 %all-gather.1 = bf16[8,1,384]{2,1,0:T(2,128)(2,1)S(1)} all-gather(bf16[1,1,384]{2,1,0:T(2,128)(2,1)S(1)} %bitcast.66), channel_id=1, replica_groups=mesh['replica'=8,'fsdp'=32] {'replica'}, dimensions={0}, use_global_device_ids=true | all-gather | bytes 6912 | tf_op jit(solution)/shard_map/all_gather | solution.py:73
  38.3 0.0 copy-done.6
  38.3 14.5 %all_gather.10 = bf16[8,384,128]{2,1,0:T(8,128)(2,1)S(1)} all-gather(bf16[1,384,128]{2,1,0:T(8,128)(2,1)S(1)} %copy-done.6), channel_id=1, replica_groups=mesh['replica'=8,'fsdp'=32] {'replica'}, dimensions={0}, use_global_device_ids=true | all-gather | bytes 884736 | tf_op jit(solution)/shard_map/all_gather | solution.py:72
  52.7 0.5 multiply_reduce_fusion
  53.2 0.0 copy-start.1
  53.2 0.0 copy-start.2
  53.2 0.0 copy-start.3
  53.2 0.0 copy-start.4
  53.3 0.0 copy-start.5
  53.3 158.5 %all-gather.4.cloned.1.call-done = bf16[1,12288,512]{2,1,0:T(8,128)(2,1)} async-done(((bf16[1,384,512]{2,1,0:T(8,128)(2,1)}), bf16[1,12288,512]{2,1,0:T(8,128)(2,1)}) %all-gather.4.cloned.1.call-update) | async-done | bytes 12582928 | tf_op jit(solution)/shard_map/all_gather | solution.py:48
  211.8 10.6 %fusion.26 = bf16[1,256,512]{2,1,0:T(8,128)(2,1)} fusion(bf16[1,12288,512]{2,1,0:T(8,128)(2,1)} %all-gather.4.cloned.1.call-done, bf16[1,256,12288]{2,1,0:T(8,128)(2,1)} %param.11, f32[12288]{0:T(1024)S(1)} %convert_element_type.43, f32[256]{0:T(256)S(1)} %add_rsqrt_fusion), kind=kOutput, calls=%fused_computation.21 | convolution fusion | flops 3234070528 | bytes 19186688 | tf_op jit(solution)/shard_map/dot_general | solution.py:46
  222.3 302.1 %reduce-scatter.2.cloned.1.call-done = bf16[384,512]{1,0:T(8,128)(2,1)} async-done(((bf16[12288,512]{1,0:T(8,128)(2,1)}), bf16[384,512]{1,0:T(8,128)(2,1)}) %reduce-scatter.2.cloned.1.call-update) | async-done | bytes 393232 | tf_op jit(solution)/shard_map/reduce_scatter | solution.py:53
  524.5 0.0 copy-done.1
  524.5 2.7 fusion.36
  527.2 0.8 multiply_dynamic-update-slice_fusion
  528.0 0.8 convert_bitcast_fusion.1
  (10 shorter events, 0.0 us)
Async XLA Ops:
  7.2 5.7 %copy-start = (bf16[1,256,512]{2,1,0:T(8,128)(2,1)S(1)}, bf16[1,256,512]{2,1,0:T(8,128)(2,1)}, u32[]{:S(2)}) copy-start(bf16[1,256,512]{2,1,0:T(8,128)(2,1)} %param.13) | copy-start | bytes 786436
  7.2 204.6 %all-gather.4.cloned.1.call-start = ((), (), s32[]{:S(2)}) async-start(), calls=%async_computation.2 | async-start | bytes 12976128 | tf_op jit(solution)/shard_map/all_gather | solution.py:48
  7.9 516.5 %reduce-scatter.2.cloned.1.call-start = ((), (), s32[]{:S(2)}) async-start(), calls=%async_computation.1 | async-start | bytes 12976128 | tf_op jit(solution)/shard_map/reduce_scatter | solution.py:53
  23.7 0.7 copy-start.7
  23.7 14.6 %copy-start.6 = (bf16[1,384,128]{2,1,0:T(8,128)(2,1)S(1)}, bf16[1,384,128]{2,1,0:T(8,128)(2,1)}, u32[]{:S(2)}) copy-start(bf16[1,384,128]{2,1,0:T(8,128)(2,1)} %param.17) | copy-start | bytes 294916
  53.2 471.2 %copy-start.1 = (bf16[1,384,512]{2,1,0:T(8,128)(2,1)S(1)}, bf16[1,384,512]{2,1,0:T(8,128)(2,1)}, u32[]{:S(2)}) copy-start(bf16[1,384,512]{2,1,0:T(8,128)(2,1)} %param.14) | copy-start | bytes 1179652
  53.2 471.2 %copy-start.2 = (f32[1,384,512]{2,1,0:T(8,128)S(1)}, f32[1,384,512]{2,1,0:T(8,128)}, u32[]{:S(2)}) copy-start(f32[1,384,512]{2,1,0:T(8,128)} %param.16) | copy-start | bytes 2359300
  53.2 471.2 %copy-start.3 = (f32[1,384,512]{2,1,0:T(8,128)S(1)}, f32[1,384,512]{2,1,0:T(8,128)}, u32[]{:S(2)}) copy-start(f32[1,384,512]{2,1,0:T(8,128)} %param.15) | copy-start | bytes 2359300
  53.2 473.9 %copy-start.4 = (f32[384,128]{1,0:T(8,128)S(1)}, f32[384,128]{1,0:T(8,128)}, u32[]{:S(2)}) copy-start(f32[384,128]{1,0:T(8,128)} %param.19) | copy-start | bytes 589828
  53.3 473.9 %copy-start.5 = (f32[384,128]{1,0:T(8,128)S(1)}, f32[384,128]{1,0:T(8,128)}, u32[]{:S(2)}) copy-start(f32[384,128]{1,0:T(8,128)} %param.20) | copy-start | bytes 589828
Sparse Core Ops, SparseCore 0:
  11.5 200.2 all-gather.3
  217.5 306.8 reduce-scatter.1
where the time goes:
time: 536 us
  waiting for transfers between devices  461 us (86%)
  blocking collectives  28.3 us (5%)
  matrix products  21.4 us (4%)
  between operations  14.8 us (3%)
  other arithmetic  9.69 us (2%)
    reduce_scatter x1, waiting for transfers between devices, per_device(): lax.psum_scatter((factor * lax.dot_general(columns, cotangent, (((0,), (0...  302 us
    all_gather x1, waiting for transfers between devices, per_device(): lax.all_gather(weight_shard, 'fsdp', axis=0, tiled=True)  159 us
    all_gather x1, blocking collectives, per_device(): lax.all_gather(outer_codes, 'replica', axis=0, tiled=True)  14.5 us
    all_gather x1, blocking collectives, per_device(): lax.all_gather(outer_scales, 'replica', axis=0, tiled=True)  13.8 us
    dot_general x1, matrix products, per_device(): lax.dot_general(columns, cotangent, (((0,), (0,)), ((), ())), preferred_e...  10.9 us
  transfers between devices with their start and end apart: 2, of which 2 were waited for; matrix products, arithmetic and copies ran while one was open for 5% of the time, Pallas kernels for 0%

commit v1 on v0

v1 whole, which is shorter than its diff:
```python
import functools

import jax
import jax.numpy as jnp
from jax import lax
from jax.experimental import pallas as pl
from jax.experimental.pallas import tpu as pltpu
from jax.sharding import PartitionSpec as P

norm_epsilon = 1e-05
adam_epsilon = 1e-08
beta_one = 0.9
beta_two = 0.95
inner_rate = 0.02
decay_rate = 0.1
outer_beta = 0.9
outer_rate = 0.7
mix_weight = 0.5

NY, NX, NZ = 4, 4, 2
ROWS = 32
VMEM_LIMIT = 48 * 1024 * 1024


def place(y, x, z):
    return ((y % NY) * NX + x % NX) * NZ + z % NZ


def shift(value, dy, dx, dz):
    pairs = [
        (place(y, x, z), place(y + dy, x + dx, z + dz))
        for y in range(NY)
        for x in range(NX)
        for z in range(NZ)
    ]
    return lax.ppermute(value, "fsdp", pairs)


def whole_blocks(count):
    return [pl.BlockSpec(memory_space=pltpu.VMEM)] * count


def norm_kernel(width, layout, column_ref, rows_ref, gain_ref, *outs):
    features = rows_ref.shape[1]
    rows = rows_ref.shape[0]

    def add_squares(step, total):
        part = rows_ref[:, pl.ds(pl.multiple_of(step * width, 128), width)].astype(jnp.float32)
        return total + part * part

    total = lax.fori_loop(
        0, features // width, add_squares, jnp.zeros((rows, width), jnp.float32), unroll=4
    )
    scale = lax.rsqrt(jnp.sum(total, axis=1, keepdims=True) / features + norm_epsilon)
    for out, blocks in zip(outs, layout):
        for position, block in enumerate(blocks):
            column = pl.multiple_of(column_ref[block], 128)
            part = rows_ref[:, pl.ds(column, width)].astype(jnp.float32)
            gain = gain_ref[:, pl.ds(column, width)]
            out[:, position * width : (position + 1) * width] = (part * scale * gain).astype(
                jnp.bfloat16
            )


def normalize(token_rows, gain, columns, layout, width):
    tokens, features = token_rows.shape
    return pl.pallas_call(
        functools.partial(norm_kernel, width, layout),
        grid_spec=pltpu.PrefetchScalarGridSpec(
            num_scalar_prefetch=1,
            grid=(tokens // ROWS,),
            in_specs=[
                pl.BlockSpec((ROWS, features), lambda i, c: (i, 0)),
                pl.BlockSpec((1, features), lambda i, c: (0, 0)),
            ],
            out_specs=[
                pl.BlockSpec((ROWS, width * len(blocks)), lambda i, c: (i, 0)) for blocks in layout
            ],
        ),
        out_shape=[
            jax.ShapeDtypeStruct((tokens, width * len(blocks)), jnp.bfloat16) for blocks in layout
        ],
        compiler_params=pltpu.CompilerParams(vmem_limit_bytes=VMEM_LIMIT),
        cost_estimate=pl.CostEstimate(
            flops=6 * tokens * features, bytes_accessed=4 * tokens * features, transcendentals=0
        ),
        name="norm",
    )(columns, token_rows, gain)


def gradient_kernel(sources, factor, *refs):
    cots, rows, outs = refs[:sources], refs[sources : 2 * sources], refs[2 * sources :]
    width = outs[0].shape[1]
    for j, out in enumerate(outs):
        total = None
        for cot, row in zip(cots, rows):
            term = jnp.dot(
                cot[...], row[:, j * width : (j + 1) * width], preferred_element_type=jnp.float32
            )
            total = term if total is None else total + term
        out[...] = (factor * total).astype(jnp.bfloat16)


def gradient_blocks(cots, rows, width, factor):
    count = rows[0].shape[1] // width
    keys, tokens = cots[0].shape
    work = len(cots) * keys * tokens * width * count
    return pl.pallas_call(
        functools.partial(gradient_kernel, len(cots), factor),
        in_specs=whole_blocks(2 * len(cots)),
        out_specs=whole_blocks(count),
        out_shape=[jax.ShapeDtypeStruct((keys, width), jnp.bfloat16)] * count,
        compiler_params=pltpu.CompilerParams(vmem_limit_bytes=VMEM_LIMIT),
        cost_estimate=pl.CostEstimate(
            flops=2 * work, bytes_accessed=8 * 2**20, transcendentals=0
        ),
        name="gradient",
    )(*cots, *rows)


def project_kernel(sources, pieces, factor, has_start, *refs):
    refs = list(refs)
    starts = [refs.pop(0) for _ in range(sources)] if has_start else [None] * sources
    rows = [[refs.pop(0) for _ in range(sources)] for _ in range(len(pieces))]
    weights = [refs.pop(0) for _ in range(len(refs) - sources)]
    outs = refs
    for source, (start, out) in enumerate(zip(starts, outs)):
        total = None if start is None else start[...]
        for group, blocks in zip(rows, pieces):
            for position, (weight, low, high) in enumerate(blocks):
                width = high - low
                term = jnp.dot(
                    group[source][:, position * width : (position + 1) * width],
                    weights[weight][low:high, :],
                    preferred_element_type=jnp.float32,
                )
                total = term if total is None else total + term
        if has_start:
            total = factor * total
        out[...] = total.astype(out.dtype)


def project(starts, rows, weights, pieces, out_types, factor):
    sources = len(rows[0])
    tokens = rows[0][0].shape[0]
    keys = weights[0].shape[1]
    depth = sum(group[0].shape[1] for group in rows)
    flat = list(starts or []) + [r for group in rows for r in group] + list(weights)
    return pl.pallas_call(
        functools.partial(project_kernel, sources, pieces, factor, starts is not None),
        in_specs=whole_blocks(len(flat)),
        out_specs=whole_blocks(sources),
        out_shape=[jax.ShapeDtypeStruct((tokens, keys), t) for t in out_types],
        compiler_params=pltpu.CompilerParams(vmem_limit_bytes=VMEM_LIMIT),
        cost_estimate=pl.CostEstimate(
            flops=2 * sources * tokens * keys * depth,
            bytes_accessed=8 * 2**20,
            transcendentals=0,
        ),
        name="project",
    )(*flat)


def update_kernel(
    offset_ref, own, one, two, three, far, weight, first, second, fresh, merged_out, first_out, second_out
):
    summed = own[...].astype(jnp.float32)
    for other in (one, two, three, far):
        summed = summed + other[...].astype(jnp.float32)
    gradient = summed.T
    moment_one = beta_one * first[...] + (1.0 - beta_one) * gradient
    moment_two = beta_two * second[...] + (1.0 - beta_two) * gradient * gradient
    first_out[...] = moment_one
    second_out[...] = moment_two
    master = weight[...].astype(jnp.float32)
    stepped = master - inner_rate * (
        moment_one / (jnp.sqrt(moment_two) + adam_epsilon) + decay_rate * master
    )
    head = fresh.shape[1]
    for position in range(master.shape[1] // head):
        part = stepped[:, position * head : (position + 1) * head]
        blended = mix_weight * part + (1.0 - mix_weight) * fresh[...]
        merged_out[:, position * head : (position + 1) * head] = jnp.where(
            offset_ref[0] == position, blended, part
        ).astype(jnp.bfloat16)


def update(head_index, terms, weight, first, second, fresh):
    rows, keys = weight.shape
    head = fresh.shape[1]
    block = 128
    return pl.pallas_call(
        update_kernel,
        grid_spec=pltpu.PrefetchScalarGridSpec(
            num_scalar_prefetch=1,
            grid=(rows // block,),
            in_specs=[pl.BlockSpec((keys, block), lambda i, o: (0, i))] * 5
            + [pl.BlockSpec((block, keys), lambda i, o: (i, 0))] * 3
            + [pl.BlockSpec((block, head), lambda i, o: (i, 0))],
            out_specs=[pl.BlockSpec((block, keys), lambda i, o: (i, 0))] * 3,
        ),
        out_shape=[
            jax.ShapeDtypeStruct((rows, keys), jnp.bfloat16),
            jax.ShapeDtypeStruct((rows, keys), jnp.float32),
            jax.ShapeDtypeStruct((rows, keys), jnp.float32),
        ],
        compiler_params=pltpu.CompilerParams(vmem_limit_bytes=VMEM_LIMIT),
        cost_estimate=pl.CostEstimate(
            flops=20 * rows * keys, bytes_accessed=6 * 2**20, transcendentals=0
        ),
        name="update",
    )(head_index, *terms, weight, first, second, fresh)


def per_device(
    activations,
    norm_gain,
    key_cotangent,
    key_weight,
    adam_first,
    adam_second,
    outer_codes,
    outer_scales,
    global_fragment,
    outer_momentum,
    fragment_index,
):
    token_rows = activations[0]
    weight_shard = key_weight[0]
    features = token_rows.shape[1]
    factor = features ** (-0.5)
    width = weight_shard.shape[0]
    replicas = lax.axis_size("replica")

    me = lax.axis_index("fsdp")
    my_y, my_x, my_z = me // (NX * NZ), (me // NZ) % NX, me % NZ

    cot = key_cotangent[0].T
    cots = [cot] + [shift(cot, 0, d, 0) for d in (1, 2, 3)]

    pair = jnp.concatenate([weight_shard, shift(weight_shard, 0, 0, 1)], axis=0)
    pairs = [pair] + [shift(pair, -e, 0, 0) for e in (1, 2, 3)]

    table = [(d, e, z) for d in range(NX) for e in range(NY) for z in range(NZ)]
    columns = jnp.stack(
        [
            ((((my_y + e) % NY) * NX + (my_x + d) % NX) * NZ + (my_z + z) % NZ) * width
            for d, e, z in table
        ]
    ).astype(jnp.int32)
    at = {key: number for number, key in enumerate(table)}
    far_z = [[at[d, e, 1] for e in range(NY)] for d in range(NX)]
    near_z = [[at[d, e, 0] for e in range(1, NY)] for d in range(NX)]
    own_z = [[at[d, 0, 0]] for d in range(NX)]
    parts = normalize(
        token_rows,
        norm_gain.astype(jnp.float32)[None],
        columns,
        far_z + near_z + own_z,
        width,
    )
    chunks = [parts[0:NX], parts[NX : 2 * NX], parts[2 * NX :]]
    chunks = [[c[0]] + [shift(c[d], 0, d, 0) for d in (1, 2, 3)] for c in chunks]

    far = gradient_blocks(cots, chunks[0], width, factor)
    far = [far[0]] + [shift(far[e], e, 0, 0) for e in (1, 2, 3)]
    far = sum(f.astype(jnp.float32) for f in far).astype(jnp.bfloat16)
    far = shift(far, 0, 0, 1)
    near = gradient_blocks(cots, chunks[1], width, factor)
    near = [shift(near[e - 1], e, 0, 0) for e in (1, 2, 3)]
    own = gradient_blocks(cots, chunks[2], width, factor)

    early = project(
        None,
        chunks[:2],
        pairs,
        [
            [(e, width, 2 * width) for e in range(NY)],
            [(e, 0, width) for e in range(1, NY)],
        ],
        [jnp.float32] * NX,
        factor,
    )
    late = project(
        early,
        chunks[2:],
        [weight_shard],
        [[(0, 0, width)]],
        [jnp.float32] + [jnp.bfloat16] * (NX - 1),
        factor,
    )
    back = [shift(late[d], 0, -d, 0) for d in (1, 2, 3)]
    projected = (late[0] + sum(b.astype(jnp.float32) for b in back)).astype(jnp.bfloat16)

    delta = outer_codes[0].astype(jnp.float32) * outer_scales[0].astype(jnp.float32)[:, None]
    step = 1
    while step < replicas:
        delta = delta + lax.ppermute(
            delta, "replica", [(r, r ^ step) for r in range(replicas)]
        )
        step *= 2
    outer_delta = delta / replicas
    momentum = outer_beta * outer_momentum + outer_delta
    refreshed = global_fragment - outer_rate * (outer_delta + outer_beta * momentum)

    heads = weight_shard.shape[1] // global_fragment.shape[1]
    head_index = jnp.remainder(fragment_index, heads).astype(jnp.int32)
    merged, moment_one, moment_two = update(
        head_index,
        list(own) + near + [far],
        weight_shard,
        adam_first[0],
        adam_second[0],
        refreshed,
    )
    return (
        projected[None],
        merged[None],
        moment_one[None],
        moment_two[None],
        momentum,
        refreshed,
    )


def solution(mesh):
    in_specs = (
        P("replica", "fsdp", None),
        P(),
        P("replica", "fsdp", None),
        P("replica", "fsdp", None),
        P("replica", "fsdp", None),
        P("replica", "fsdp", None),
        P("replica", "fsdp", None),
        P("replica", "fsdp"),
        P("fsdp", None),
        P("fsdp", None),
        P(),
    )
    out_specs = (
        P("replica", "fsdp", None),
        P("replica", "fsdp", None),
        P("replica", "fsdp", None),
        P("replica", "fsdp", None),
        P("fsdp", None),
        P("fsdp", None),
    )
    return jax.shard_map(
        per_device, mesh=mesh, in_specs=in_specs, out_specs=out_specs, check_vma=False
    )
```

time: 536 us -> 168 us (0.31)
  waiting for transfers between devices: 461 us -> 81.1 us
  starting transfers between devices: 0.08 us -> 57 us
  blocking collectives: 28.3 us -> 0 us
  Pallas kernels: 0 us -> 22.7 us
  matrix products: 21.4 us -> 0 us
  between operations: 14.8 us -> 1.54 us
  other arithmetic: 9.69 us -> 2.84 us
    reduce_scatter x1 -> x0, waiting for transfers between devices: 302 us -> none  [per_device(): lax.psum_scatter((factor * lax.dot_general(columns, cotangent, (((0,), (0...]
    all_gather x1 -> x0, waiting for transfers between devices: 159 us -> none  [per_device(): lax.all_gather(weight_shard, 'fsdp', axis=0, tiled=True)]
    ppermute x0 -> x29, waiting for transfers between devices: none -> 81.1 us  [the longest x26 75.3 us: shift(): return lax.ppermute(value, 'fsdp', pairs)]
    ppermute x0 -> x29, starting transfers between devices: none -> 57 us  [the longest x26 53.6 us: shift(): return lax.ppermute(value, 'fsdp', pairs)]
    all_gather x2 -> x0, blocking collectives: 28.3 us -> none  [the longest x1 14.5 us: per_device(): lax.all_gather(outer_codes, 'replica', axis=0, tiled=True)]
    pallas_call x0 -> x7, Pallas kernels: none -> 22.7 us  [the longest x1 8.32 us: normalize(): pl.pallas_call(functools.partial(norm_kernel, width, layout), grid_spec=p...]
    dot_general x2 -> x0, matrix products: 21.4 us -> none  [the longest x1 10.9 us: per_device(): lax.dot_general(columns, cotangent, (((0,), (0,)), ((), ())), preferred_e...]
  transfers between devices with their start and end apart: 2 -> 29, of which waited for: 2 -> 10; matrix products, arithmetic and copies ran while one was open for 5% -> 2% of each run, Pallas kernels for 0% -> 12%
where the time goes in v1:
time: 168 us; the launch traced here: 167 us
  waiting for transfers between devices  81.1 us (48%)
  starting transfers between devices  57 us (34%)
  Pallas kernels  22.7 us (14%)
  other arithmetic  2.84 us (2%)
  local copies, waits for them, and re-layouts  2.13 us (1%)
    ppermute x26, waiting for transfers between devices, shift(): return lax.ppermute(value, 'fsdp', pairs)  75.3 us
    ppermute x26, starting transfers between devices, shift(): return lax.ppermute(value, 'fsdp', pairs)  53.6 us
    pallas_call x1, Pallas kernels, normalize(): pl.pallas_call(functools.partial(norm_kernel, width, layout), grid_spec=p...  8.32 us
    pallas_call x2, Pallas kernels, project(): pl.pallas_call(functools.partial(project_kernel, sources, pieces, factor,...  6.97 us
    ppermute x3, waiting for transfers between devices, per_device(): lax.ppermute(delta, 'replica', [(r, r ^ step) for r in range(replicas)])  5.74 us
    pallas_call x3, Pallas kernels, gradient_blocks(): pl.pallas_call(functools.partial(gradient_kernel, len(cots), factor), in_...  4.84 us
    ppermute x3, starting transfers between devices, per_device(): lax.ppermute(delta, 'replica', [(r, r ^ step) for r in range(replicas)])  3.37 us
  transfers between devices with their start and end apart: 29, of which 10 were waited for; matrix products, arithmetic and copies ran while one was open for 2% of the time, Pallas kernels for 12%

profile of v1, /device:TPU:32, one launch (start us, length us, event | category | flops | bytes accessed | tf_op | source)
XLA Modules:
  0.0 167.2 jit_solution(16056551004627848189)
XLA Ops:
  3.3 2.7 %collective-permute-start.17 = (bf16[512,256]{1,0:T(8,128)(2,1)S(1)}, bf16[512,256]{1,0:T(8,128)(2,1)S(1)}, u32[]{:S(2)}, u32[]{:S(2)}) collective-permute-start(bf16[512,256]{1,0:T(8,128)(2,1)S(1)} %bitcast.55), channel_id=1, source_target_pairs={{0,4},{1,5},{2,6},{3,7},{4,0},{5,1},{6,2},{7,3},{8,12},{9,13},{10,... | collective-permute-start | bytes 786440 | tf_op jit(solution)/shard_map/ppermute | solution.py:36
  6.9 8.3 %norm.1 = (bf16[256,1536]{1,0:T(8,128)(2,1)S(1)}, bf16[256,1536]{1,0:T(8,128)(2,1)S(1)}, bf16[256,1536]{1,0:T(8,128)(2,1)S(1)}, bf16[256,1536]{1,0:T(8,128)(2,1)...) custom-call(s32[32]{0:T(128)S(1)} %stack.131.column_ref, ...), custom_call_target="tpu_custom_call" | custom-call | flops 18874368 | bytes 12582912 | tf_op jit(solution)/shard_map/norm/pallas_call | solution.py:67
  15.2 2.9 %collective-permute-start.11 = (bf16[256,384]{1,0:T(8,128)(2,1)S(1)}, bf16[256,384]{1,0:T(8,128)(2,1)S(1)}, u32[]{:S(2)}, u32[]{:S(2)}) collective-permute-start(bf16[256,384]{1,0:T(8,128)(2,1)S(1)} %get-tuple-element.50), channel_id=1, source_target_pairs={{0,4},{1,5},{2,6},{3,7},{4,0},{5,1},{6,2},{7,3},{8,12},{9,13},{10,... | collective-permute-start | bytes 589832 | tf_op jit(solution)/shard_map/ppermute | solution.py:36
  18.8 7.9 %collective-permute-done.10.refs_5_ = bf16[256,384]{1,0:T(8,128)(2,1)S(1)} collective-permute-done((bf16[256,384]{1,0:T(8,128)(2,1)S(1)}, bf16[256,384]{1,0:T(8,128)(2,1)S(1)}, u32[]{:S(2)}, u32[]{:S(2)}) %collective-permute-start.10) | collective-permute-done | bytes 196640 | tf_op jit(solution)/shard_map/ppermute | solution.py:36
  28.8 2.4 %collective-permute-start.1 = (bf16[256,1536]{1,0:T(8,128)(2,1)S(1)}, bf16[256,1536]{1,0:T(8,128)(2,1)S(1)}, u32[]{:S(2)}, u32[]{:S(2)}) collective-permute-start(bf16[256,1536]{1,0:T(8,128)(2,1)S(1)} %get-tuple-element.38), channel_id=1, source_target_pairs={{0,4},{1,5},{2,6},{3,7},{4,0},{5,1},{6,2},{7,3},{8,12},{9,13},{10,... | collective-permute-start | bytes 2359304 | tf_op jit(solution)/shard_map/ppermute | solution.py:36
  31.6 6.3 %collective-permute-start.6 = (bf16[384,512]{1,0:T(8,128)(2,1)S(1)}, bf16[384,512]{1,0:T(8,128)(2,1)S(1)}, u32[]{:S(2)}, u32[]{:S(2)}) collective-permute-start(bf16[384,512]{1,0:T(8,128)(2,1)S(1)} %bitcast.50), channel_id=1, source_target_pairs={{0,1},{1,0},{2,3},{3,2},{4,5},{5,4},{6,7},{7,6},{8,9},{9,8},{10,11... | collective-permute-start | bytes 1179656 | tf_op jit(solution)/shard_map/ppermute | solution.py:36
  39.6 15.7 %collective-permute-done.6 = bf16[384,512]{1,0:T(8,128)(2,1)S(1)} collective-permute-done((bf16[384,512]{1,0:T(8,128)(2,1)S(1)}, bf16[384,512]{1,0:T(8,128)(2,1)S(1)}, u32[]{:S(2)}, u32[]{:S(2)}) %collective-permute-start.6) | collective-permute-done | bytes 393248 | tf_op jit(solution)/shard_map/ppermute | solution.py:36
  55.4 5.7 %collective-permute-done.27 = f32[384,128]{1,0:T(8,128)S(1)} collective-permute-done((f32[384,128]{1,0:T(8,128)S(1)}, f32[384,128]{1,0:T(8,128)S(1)}, u32[]{:S(2)}, u32[]{:S(2)}) %collective-permute-start.27) | collective-permute-done | bytes 196640 | tf_op jit(solution)/shard_map/ppermute | solution.py:298
  61.1 3.0 %collective-permute-start.7 = (bf16[768,512]{1,0:T(8,128)(2,1)S(1)}, bf16[768,512]{1,0:T(8,128)(2,1)S(1)}, u32[]{:S(2)}, u32[]{:S(2)}) collective-permute-start(bf16[768,512]{1,0:T(8,128)(2,1)S(1)} %pad_maximum_fusion.refs_8_), channel_id=1, source_target_pairs={{0,24},{1,25},{2,26},{3,27},{4,28},{5,29},{6,30},{7,31},{8,0},{9,1... | collective-permute-start | bytes 2359304 | tf_op jit(solution)/shard_map/ppermute | solution.py:36
  64.1 13.4 %collective-permute-done.3.refs_5_ = bf16[256,1152]{1,0:T(8,128)(2,1)S(1)} collective-permute-done((bf16[256,1152]{1,0:T(8,128)(2,1)S(1)}, bf16[256,1152]{1,0:T(8,128)(2,1)S(1)}, u32[]{:S(2)}, u32[]{:S(2)}) %collective-permute-start.3) | collective-permute-done | bytes 589856 | tf_op jit(solution)/shard_map/ppermute | solution.py:36
  77.5 3.2 %collective-permute-start.8 = (bf16[768,512]{1,0:T(8,128)(2,1)S(1)}, bf16[768,512]{1,0:T(8,128)(2,1)S(1)}, u32[]{:S(2)}, u32[]{:S(2)}) collective-permute-start(bf16[768,512]{1,0:T(8,128)(2,1)S(1)} %pad_maximum_fusion.refs_8_), channel_id=1, source_target_pairs={{0,16},{1,17},{2,18},{3,19},{4,20},{5,21},{6,22},{7,23},{8,24},{9,... | collective-permute-start | bytes 2359304 | tf_op jit(solution)/shard_map/ppermute | solution.py:36
  82.1 2.4 %collective-permute-start.5 = (bf16[256,1152]{1,0:T(8,128)(2,1)S(1)}, bf16[256,1152]{1,0:T(8,128)(2,1)S(1)}, u32[]{:S(2)}, u32[]{:S(2)}) collective-permute-start(bf16[256,1152]{1,0:T(8,128)(2,1)S(1)} %get-tuple-element.43), channel_id=1, source_target_pairs={{0,6},{1,7},{2,0},{3,1},{4,2},{5,3},{6,4},{7,5},{8,14},{9,15},{10,... | collective-permute-start | bytes 1769480 | tf_op jit(solution)/shard_map/ppermute | solution.py:36
  88.3 7.8 %collective-permute-done.4.refs_6_ = bf16[256,1152]{1,0:T(8,128)(2,1)S(1)} collective-permute-done((bf16[256,1152]{1,0:T(8,128)(2,1)S(1)}, bf16[256,1152]{1,0:T(8,128)(2,1)S(1)}, u32[]{:S(2)}, u32[]{:S(2)}) %collective-permute-start.4) | collective-permute-done | bytes 589856 | tf_op jit(solution)/shard_map/ppermute | solution.py:36
  96.1 2.6 %collective-permute-start.24 = (bf16[512,384]{1,0:T(8,128)(2,1)S(1)}, bf16[512,384]{1,0:T(8,128)(2,1)S(1)}, u32[]{:S(2)}, u32[]{:S(2)}) collective-permute-start(bf16[512,384]{1,0:T(8,128)(2,1)S(1)} %get-tuple-element.62), channel_id=1, source_target_pairs={{0,24},{1,25},{2,26},{3,27},{4,28},{5,29},{6,30},{7,31},{8,0},{9,1... | collective-permute-start | bytes 1179656 | tf_op jit(solution)/shard_map/ppermute | solution.py:36
  98.7 8.5 %collective-permute-done.5.refs_7_ = bf16[256,1152]{1,0:T(8,128)(2,1)S(1)} collective-permute-done((bf16[256,1152]{1,0:T(8,128)(2,1)S(1)}, bf16[256,1152]{1,0:T(8,128)(2,1)S(1)}, u32[]{:S(2)}, u32[]{:S(2)}) %collective-permute-start.5) | collective-permute-done | bytes 589856 | tf_op jit(solution)/shard_map/ppermute | solution.py:36
  112.4 3.4 %collective-permute-start.28 = (f32[384,128]{1,0:T(8,128)S(1)}, f32[384,128]{1,0:T(8,128)S(1)}, u32[]{:S(2)}, u32[]{:S(2)}) collective-permute-start(f32[384,128]{1,0:T(8,128)S(1)} %add.477), channel_id=1, source_target_pairs={{0,128},{32,160},{64,192},{96,224},{128,0},{160,32},{192,64},{224,... | collective-permute-start | bytes 589832 | tf_op jit(solution)/shard_map/ppermute | solution.py:298
  118.9 6.3 %project.2 = (f32[256,512]{1,0:T(8,128)S(1)}, f32[256,512]{1,0:T(8,128)S(1)}, f32[256,512]{1,0:T(8,128)S(1)}, f32[256,512]{1,0:T(8,128)S(1)}) custom-call(bf16[256,1536]{1,0:T(8,128)(2,1)S(1)} %get-tuple-element.36.refs_0_.refs_4_, bf16[256,1536]{1,0:T(8,128)(2,1)S(1)} %collective-permute-done.refs_1_.refs_5_, bf16[256,1536]{1,0:T(8,128)(2,1)} %copy-done.4, ...), custom_call_target="tpu_custom_call" | custom-call | flops 2818572288 | bytes 8388608 | tf_op jit(solution)/shard_map/project/pallas_call | solution.py:149
  128.3 4.1 %collective-permute-done.22 = bf16[512,384]{1,0:T(8,128)(2,1)S(1)} collective-permute-done((bf16[512,384]{1,0:T(8,128)(2,1)S(1)}, bf16[512,384]{1,0:T(8,128)(2,1)S(1)}, u32[]{:S(2)}, u32[]{:S(2)}) %collective-permute-start.22) | collective-permute-done | bytes 393248 | tf_op jit(solution)/shard_map/ppermute | solution.py:36
  133.5 3.0 %collective-permute-start.20 = (bf16[512,384]{1,0:T(8,128)(2,1)S(1)}, bf16[512,384]{1,0:T(8,128)(2,1)S(1)}, u32[]{:S(2)}, u32[]{:S(2)}) collective-permute-start(bf16[512,384]{1,0:T(8,128)(2,1)S(1)} %get-tuple-element.57), channel_id=1, source_target_pairs={{0,16},{1,17},{2,18},{3,19},{4,20},{5,21},{6,22},{7,23},{8,24},{9,... | collective-permute-start | bytes 1179656 | tf_op jit(solution)/shard_map/ppermute | solution.py:36
  136.6 2.7 %collective-permute-done.15 = bf16[256,512]{1,0:T(8,128)(2,1)S(1)} collective-permute-done((bf16[256,512]{1,0:T(8,128)(2,1)S(1)}, bf16[256,512]{1,0:T(8,128)(2,1)S(1)}, u32[]{:S(2)}, u32[]{:S(2)}) %collective-permute-start.15) | collective-permute-done | bytes 262176 | tf_op jit(solution)/shard_map/ppermute | solution.py:36
  139.2 2.9 %collective-permute-start.21 = (bf16[512,384]{1,0:T(8,128)(2,1)S(1)}, bf16[512,384]{1,0:T(8,128)(2,1)S(1)}, u32[]{:S(2)}, u32[]{:S(2)}) collective-permute-start(bf16[512,384]{1,0:T(8,128)(2,1)S(1)} %get-tuple-element.58), channel_id=1, source_target_pairs={{0,24},{1,25},{2,26},{3,27},{4,28},{5,29},{6,30},{7,31},{8,0},{9,1... | collective-permute-start | bytes 1179656 | tf_op jit(solution)/shard_map/ppermute | solution.py:36
  142.2 6.3 %collective-permute-start.25 = (bf16[512,384]{1,0:T(8,128)(2,1)S(1)}, bf16[512,384]{1,0:T(8,128)(2,1)S(1)}, u32[]{:S(2)}, u32[]{:S(2)}) collective-permute-start(bf16[512,384]{1,0:T(8,128)(2,1)S(1)} %add_convert_fusion), channel_id=1, source_target_pairs={{0,1},{1,0},{2,3},{3,2},{4,5},{5,4},{6,7},{7,6},{8,9},{9,8},{10,11... | collective-permute-start | bytes 1179656 | tf_op jit(solution)/shard_map/ppermute | solution.py:36
  150.1 14.6 %collective-permute-done.25.far = bf16[512,384]{1,0:T(8,128)(2,1)S(1)} collective-permute-done((bf16[512,384]{1,0:T(8,128)(2,1)S(1)}, bf16[512,384]{1,0:T(8,128)(2,1)S(1)}, u32[]{:S(2)}, u32[]{:S(2)}) %collective-permute-start.25) | collective-permute-done | bytes 393248 | tf_op jit(solution)/shard_map/ppermute | solution.py:36
  164.7 2.5 %update.1 = (bf16[384,512]{1,0:T(8,128)(2,1)}, f32[384,512]{1,0:T(8,128)}, f32[384,512]{1,0:T(8,128)}) custom-call(s32[1]{0:T(128)S(6)} %select_n.250.offset_ref, bf16[512,384]{1,0:T(8,128)(2,1)S(1)} %gradient.3.own, bf16[512,384]{1,0:T(8,128)(2,1)S(1)} %collective-permute-done.19.one, bf16[512,384]{1,0:T(8,128)(2,1)S(1)} %collective-permute-done.20.two, ...), custom_call_target="tpu_custom_call" | custom-call | flops 3932160 | bytes 6291456 | tf_op jit(solution)/shard_map/update/pallas_call | solution.py:192
  (80 shorter events, 27.1 us)
Async XLA Ops:
  1.7 29.4 %collective-permute-start.16 = (bf16[512,256]{1,0:T(8,128)(2,1)S(1)}, bf16[512,256]{1,0:T(8,128)(2,1)S(1)}, u32[]{:S(2)}, u32[]{:S(2)}) collective-permute-start(bf16[512,256]{1,0:T(8,128)(2,1)S(1)} %bitcast.54), channel_id=1, source_target_pairs={{0,2},{1,3},{2,4},{3,5},{4,6},{5,7},{6,0},{7,1},{8,10},{9,11},{10,... | collective-permute-start | bytes 786440 | tf_op jit(solution)/shard_map/ppermute | solution.py:36
  3.3 28.3 %collective-permute-start.17 = (bf16[512,256]{1,0:T(8,128)(2,1)S(1)}, bf16[512,256]{1,0:T(8,128)(2,1)S(1)}, u32[]{:S(2)}, u32[]{:S(2)}) collective-permute-start(bf16[512,256]{1,0:T(8,128)(2,1)S(1)} %bitcast.55), channel_id=1, source_target_pairs={{0,4},{1,5},{2,6},{3,7},{4,0},{5,1},{6,2},{7,3},{8,12},{9,13},{10,... | collective-permute-start | bytes 786440 | tf_op jit(solution)/shard_map/ppermute | solution.py:36
  15.2 11.5 %collective-permute-start.10 = (bf16[256,384]{1,0:T(8,128)(2,1)S(1)}, bf16[256,384]{1,0:T(8,128)(2,1)S(1)}, u32[]{:S(2)}, u32[]{:S(2)}) collective-permute-start(bf16[256,384]{1,0:T(8,128)(2,1)S(1)} %get-tuple-element.49), channel_id=1, source_target_pairs={{0,2},{1,3},{2,4},{3,5},{4,6},{5,7},{6,0},{7,1},{8,10},{9,11},{10,... | collective-permute-start | bytes 589832 | tf_op jit(solution)/shard_map/ppermute | solution.py:36
  15.2 11.5 %collective-permute-start.11 = (bf16[256,384]{1,0:T(8,128)(2,1)S(1)}, bf16[256,384]{1,0:T(8,128)(2,1)S(1)}, u32[]{:S(2)}, u32[]{:S(2)}) collective-permute-start(bf16[256,384]{1,0:T(8,128)(2,1)S(1)} %get-tuple-element.50), channel_id=1, source_target_pairs={{0,4},{1,5},{2,6},{3,7},{4,0},{5,1},{6,2},{7,3},{8,12},{9,13},{10,... | collective-permute-start | bytes 589832 | tf_op jit(solution)/shard_map/ppermute | solution.py:36
  27.8 52.9 %collective-permute-start = (bf16[256,1536]{1,0:T(8,128)(2,1)S(1)}, bf16[256,1536]{1,0:T(8,128)(2,1)S(1)}, u32[]{:S(2)}, u32[]{:S(2)}) collective-permute-start(bf16[256,1536]{1,0:T(8,128)(2,1)S(1)} %get-tuple-element.37), channel_id=1, source_target_pairs={{0,2},{1,3},{2,4},{3,5},{4,6},{5,7},{6,0},{7,1},{8,10},{9,11},{10,... | collective-permute-start | bytes 2359304 | tf_op jit(solution)/shard_map/ppermute | solution.py:36
  28.8 52.6 %collective-permute-start.1 = (bf16[256,1536]{1,0:T(8,128)(2,1)S(1)}, bf16[256,1536]{1,0:T(8,128)(2,1)S(1)}, u32[]{:S(2)}, u32[]{:S(2)}) collective-permute-start(bf16[256,1536]{1,0:T(8,128)(2,1)S(1)} %get-tuple-element.38), channel_id=1, source_target_pairs={{0,4},{1,5},{2,6},{3,7},{4,0},{5,1},{6,2},{7,3},{8,12},{9,13},{10,... | collective-permute-start | bytes 2359304 | tf_op jit(solution)/shard_map/ppermute | solution.py:36
  31.2 51.0 %collective-permute-start.2 = (bf16[256,1536]{1,0:T(8,128)(2,1)}, bf16[256,1536]{1,0:T(8,128)(2,1)S(1)}, u32[]{:S(2)}, u32[]{:S(2)}) collective-permute-start(bf16[256,1536]{1,0:T(8,128)(2,1)} %get-tuple-element.39), channel_id=1, source_target_pairs={{0,6},{1,7},{2,0},{3,1},{4,2},{5,3},{6,4},{7,5},{8,14},{9,15},{10,... | collective-permute-start | bytes 2359304 | tf_op jit(solution)/shard_map/ppermute | solution.py:36
  31.6 23.7 %collective-permute-start.6 = (bf16[384,512]{1,0:T(8,128)(2,1)S(1)}, bf16[384,512]{1,0:T(8,128)(2,1)S(1)}, u32[]{:S(2)}, u32[]{:S(2)}) collective-permute-start(bf16[384,512]{1,0:T(8,128)(2,1)S(1)} %bitcast.50), channel_id=1, source_target_pairs={{0,1},{1,0},{2,3},{3,2},{4,5},{5,4},{6,7},{7,6},{8,9},{9,8},{10,11... | collective-permute-start | bytes 1179656 | tf_op jit(solution)/shard_map/ppermute | solution.py:36
  37.8 39.6 %collective-permute-start.3 = (bf16[256,1152]{1,0:T(8,128)(2,1)S(1)}, bf16[256,1152]{1,0:T(8,128)(2,1)S(1)}, u32[]{:S(2)}, u32[]{:S(2)}) collective-permute-start(bf16[256,1152]{1,0:T(8,128)(2,1)S(1)} %get-tuple-element.41), channel_id=1, source_target_pairs={{0,2},{1,3},{2,4},{3,5},{4,6},{5,7},{6,0},{7,1},{8,10},{9,11},{10,... | collective-permute-start | bytes 1769480 | tf_op jit(solution)/shard_map/ppermute | solution.py:36
  61.1 47.9 %collective-permute-start.7 = (bf16[768,512]{1,0:T(8,128)(2,1)S(1)}, bf16[768,512]{1,0:T(8,128)(2,1)S(1)}, u32[]{:S(2)}, u32[]{:S(2)}) collective-permute-start(bf16[768,512]{1,0:T(8,128)(2,1)S(1)} %pad_maximum_fusion.refs_8_), channel_id=1, source_target_pairs={{0,24},{1,25},{2,26},{3,27},{4,28},{5,29},{6,30},{7,31},{8,0},{9,1... | collective-permute-start | bytes 2359304 | tf_op jit(solution)/shard_map/ppermute | solution.py:36
  77.5 34.9 %collective-permute-start.8 = (bf16[768,512]{1,0:T(8,128)(2,1)S(1)}, bf16[768,512]{1,0:T(8,128)(2,1)S(1)}, u32[]{:S(2)}, u32[]{:S(2)}) collective-permute-start(bf16[768,512]{1,0:T(8,128)(2,1)S(1)} %pad_maximum_fusion.refs_8_), channel_id=1, source_target_pairs={{0,16},{1,17},{2,18},{3,19},{4,20},{5,21},{6,22},{7,23},{8,24},{9,... | collective-permute-start | bytes 2359304 | tf_op jit(solution)/shard_map/ppermute | solution.py:36
  80.7 35.7 %collective-permute-start.9 = (bf16[768,512]{1,0:T(8,128)(2,1)S(1)}, bf16[768,512]{1,0:T(8,128)(2,1)S(1)}, u32[]{:S(2)}, u32[]{:S(2)}) collective-permute-start(bf16[768,512]{1,0:T(8,128)(2,1)S(1)} %pad_maximum_fusion.refs_8_), channel_id=1, source_target_pairs={{0,8},{1,9},{2,10},{3,11},{4,12},{5,13},{6,14},{7,15},{8,16},{9,17... | collective-permute-start | bytes 2359304 | tf_op jit(solution)/shard_map/ppermute | solution.py:36
  81.4 14.8 %collective-permute-start.4 = (bf16[256,1152]{1,0:T(8,128)(2,1)S(1)}, bf16[256,1152]{1,0:T(8,128)(2,1)S(1)}, u32[]{:S(2)}, u32[]{:S(2)}) collective-permute-start(bf16[256,1152]{1,0:T(8,128)(2,1)S(1)} %get-tuple-element.42), channel_id=1, source_target_pairs={{0,4},{1,5},{2,6},{3,7},{4,0},{5,1},{6,2},{7,3},{8,12},{9,13},{10,... | collective-permute-start | bytes 1769480 | tf_op jit(solution)/shard_map/ppermute | solution.py:36
  82.1 25.0 %collective-permute-start.5 = (bf16[256,1152]{1,0:T(8,128)(2,1)S(1)}, bf16[256,1152]{1,0:T(8,128)(2,1)S(1)}, u32[]{:S(2)}, u32[]{:S(2)}) collective-permute-start(bf16[256,1152]{1,0:T(8,128)(2,1)S(1)} %get-tuple-element.43), channel_id=1, source_target_pairs={{0,6},{1,7},{2,0},{3,1},{4,2},{5,3},{6,4},{7,5},{8,14},{9,15},{10,... | collective-permute-start | bytes 1769480 | tf_op jit(solution)/shard_map/ppermute | solution.py:36
  96.1 29.8 %collective-permute-start.24 = (bf16[512,384]{1,0:T(8,128)(2,1)S(1)}, bf16[512,384]{1,0:T(8,128)(2,1)S(1)}, u32[]{:S(2)}, u32[]{:S(2)}) collective-permute-start(bf16[512,384]{1,0:T(8,128)(2,1)S(1)} %get-tuple-element.62), channel_id=1, source_target_pairs={{0,24},{1,25},{2,26},{3,27},{4,28},{5,29},{6,30},{7,31},{8,0},{9,1... | collective-permute-start | bytes 1179656 | tf_op jit(solution)/shard_map/ppermute | solution.py:36
  107.2 19.3 %collective-permute-start.23 = (bf16[512,384]{1,0:T(8,128)(2,1)S(1)}, bf16[512,384]{1,0:T(8,128)(2,1)S(1)}, u32[]{:S(2)}, u32[]{:S(2)}) collective-permute-start(bf16[512,384]{1,0:T(8,128)(2,1)S(1)} %get-tuple-element.61), channel_id=1, source_target_pairs={{0,16},{1,17},{2,18},{3,19},{4,20},{5,21},{6,22},{7,23},{8,24},{9,... | collective-permute-start | bytes 1179656 | tf_op jit(solution)/shard_map/ppermute | solution.py:36
  109.0 23.4 %collective-permute-start.22 = (bf16[512,384]{1,0:T(8,128)(2,1)S(1)}, bf16[512,384]{1,0:T(8,128)(2,1)S(1)}, u32[]{:S(2)}, u32[]{:S(2)}) collective-permute-start(bf16[512,384]{1,0:T(8,128)(2,1)S(1)} %get-tuple-element.60), channel_id=1, source_target_pairs={{0,8},{1,9},{2,10},{3,11},{4,12},{5,13},{6,14},{7,15},{8,16},{9,17... | collective-permute-start | bytes 1179656 | tf_op jit(solution)/shard_map/ppermute | solution.py:36
  112.4 21.1 %collective-permute-start.28 = (f32[384,128]{1,0:T(8,128)S(1)}, f32[384,128]{1,0:T(8,128)S(1)}, u32[]{:S(2)}, u32[]{:S(2)}) collective-permute-start(f32[384,128]{1,0:T(8,128)S(1)} %add.477), channel_id=1, source_target_pairs={{0,128},{32,160},{64,192},{96,224},{128,0},{160,32},{192,64},{224,... | collective-permute-start | bytes 589832 | tf_op jit(solution)/shard_map/ppermute | solution.py:298
  117.3 32.7 %collective-permute-start.19 = (bf16[512,384]{1,0:T(8,128)(2,1)S(1)}, bf16[512,384]{1,0:T(8,128)(2,1)S(1)}, u32[]{:S(2)}, u32[]{:S(2)}) collective-permute-start(bf16[512,384]{1,0:T(8,128)(2,1)S(1)} %get-tuple-element.56), channel_id=1, source_target_pairs={{0,8},{1,9},{2,10},{3,11},{4,12},{5,13},{6,14},{7,15},{8,16},{9,17... | collective-permute-start | bytes 1179656 | tf_op jit(solution)/shard_map/ppermute | solution.py:36
  125.9 13.3 %collective-permute-start.15 = (bf16[256,512]{1,0:T(8,128)(2,1)S(1)}, bf16[256,512]{1,0:T(8,128)(2,1)S(1)}, u32[]{:S(2)}, u32[]{:S(2)}) collective-permute-start(bf16[256,512]{1,0:T(8,128)(2,1)S(1)} %get-tuple-element.55), channel_id=1, source_target_pairs={{0,2},{1,3},{2,4},{3,5},{4,6},{5,7},{6,0},{7,1},{8,10},{9,11},{10,... | collective-permute-start | bytes 786440 | tf_op jit(solution)/shard_map/ppermute | solution.py:36
  126.5 15.7 %collective-permute-start.14 = (bf16[256,512]{1,0:T(8,128)(2,1)S(1)}, bf16[256,512]{1,0:T(8,128)(2,1)S(1)}, u32[]{:S(2)}, u32[]{:S(2)}) collective-permute-start(bf16[256,512]{1,0:T(8,128)(2,1)S(1)} %get-tuple-element.54), channel_id=1, source_target_pairs={{0,4},{1,5},{2,6},{3,7},{4,0},{5,1},{6,2},{7,3},{8,12},{9,13},{10,... | collective-permute-start | bytes 786440 | tf_op jit(solution)/shard_map/ppermute | solution.py:36
  132.4 16.8 %collective-permute-start.13 = (bf16[256,512]{1,0:T(8,128)(2,1)S(1)}, bf16[256,512]{1,0:T(8,128)(2,1)S(1)}, u32[]{:S(2)}, u32[]{:S(2)}) collective-permute-start(bf16[256,512]{1,0:T(8,128)(2,1)S(1)} %get-tuple-element.53), channel_id=1, source_target_pairs={{0,6},{1,7},{2,0},{3,1},{4,2},{5,3},{6,4},{7,5},{8,14},{9,15},{10,... | collective-permute-start | bytes 786440 | tf_op jit(solution)/shard_map/ppermute | solution.py:36
  133.5 16.5 %collective-permute-start.20 = (bf16[512,384]{1,0:T(8,128)(2,1)S(1)}, bf16[512,384]{1,0:T(8,128)(2,1)S(1)}, u32[]{:S(2)}, u32[]{:S(2)}) collective-permute-start(bf16[512,384]{1,0:T(8,128)(2,1)S(1)} %get-tuple-element.57), channel_id=1, source_target_pairs={{0,16},{1,17},{2,18},{3,19},{4,20},{5,21},{6,22},{7,23},{8,24},{9,... | collective-permute-start | bytes 1179656 | tf_op jit(solution)/shard_map/ppermute | solution.py:36
  142.2 22.5 %collective-permute-start.25 = (bf16[512,384]{1,0:T(8,128)(2,1)S(1)}, bf16[512,384]{1,0:T(8,128)(2,1)S(1)}, u32[]{:S(2)}, u32[]{:S(2)}) collective-permute-start(bf16[512,384]{1,0:T(8,128)(2,1)S(1)} %add_convert_fusion), channel_id=1, source_target_pairs={{0,1},{1,0},{2,3},{3,2},{4,5},{5,4},{6,7},{7,6},{8,9},{9,8},{10,11... | collective-permute-start | bytes 1179656 | tf_op jit(solution)/shard_map/ppermute | solution.py:36
  (19 other events, 267.6 us)

commit v2 on v0

v2 whole, which is shorter than its diff:
```python
import functools

import jax
import jax.numpy as jnp
from jax import lax
from jax.experimental import pallas as pl
from jax.experimental.pallas import tpu as pltpu
from jax.sharding import PartitionSpec as P

norm_epsilon = 1e-05
adam_epsilon = 1e-08
beta_one = 0.9
beta_two = 0.95
inner_rate = 0.02
decay_rate = 0.1
outer_beta = 0.9
outer_rate = 0.7
mix_weight = 0.5

NY, NX, NZ = 4, 4, 2
ROWS = 32
VMEM_LIMIT = 60 * 1024 * 1024


def place(y, x, z):
    return ((y % NY) * NX + x % NX) * NZ + z % NZ


def shift(value, dy, dx, dz):
    pairs = [
        (place(y, x, z), place(y + dy, x + dx, z + dz))
        for y in range(NY)
        for x in range(NX)
        for z in range(NZ)
    ]
    return lax.ppermute(value, "fsdp", pairs)


def in_memory(count):
    return [pl.BlockSpec(memory_space=pl.ANY)] * count


def call_options(work=1, limit=VMEM_LIMIT):
    return dict(
        compiler_params=pltpu.CompilerParams(vmem_limit_bytes=limit),
        cost_estimate=pl.CostEstimate(flops=work, bytes_accessed=1, transcendentals=0),
    )


def norm_kernel(width, blocks, extra, column_ref, rows_hbm, gain_ref, cot_hbm, *refs):
    outs, (held, ready, cot, came, gone, cot_came, cot_gone) = refs[:-7], refs[-7:]
    tokens, features = held.shape
    depth = width * len(blocks)
    lanes = 128
    bands = tokens // ROWS

    def fetch(band):
        rows = pl.ds(pl.multiple_of(band * ROWS, ROWS), ROWS)
        return pltpu.make_async_copy(rows_hbm.at[rows], held.at[rows], came.at[band])

    def store(band, x):
        rows = pl.ds(pl.multiple_of(band * ROWS, ROWS), ROWS)
        if len(outs) == 1:
            target = outs[0].at[x, rows, pl.ds(0, depth)]
        else:
            target = outs[x].at[rows]
        return pltpu.make_async_copy(ready.at[x, rows], target, gone.at[band, x])

    for band in range(bands):
        fetch(band).start()
    cot_copies = []
    if extra:
        cot_fetch = pltpu.make_async_copy(cot_hbm, cot, cot_came)
        cot_fetch.start()
        cot_copies = [
            pltpu.make_async_copy(cot, outs[0].at[x, :, pl.ds(depth, extra)], cot_gone.at[x])
            for x in range(NX)
        ]
    columns = [column_ref[number] for number in range(NX * len(blocks))]
    if extra:
        cot_fetch.wait()
        for copy in cot_copies:
            copy.start()

    @pl.loop(0, bands)
    def _(band):
        fetch(band).wait()
        rows = pl.ds(pl.multiple_of(band * ROWS, ROWS), ROWS)
        sums = [jnp.zeros((ROWS, lanes), jnp.float32) for _ in range(2)]
        for k in range(features // lanes):
            part = held[rows, k * lanes : (k + 1) * lanes].astype(jnp.float32)
            sums[k % 2] = sums[k % 2] + part * part
        total = jnp.sum(sums[0] + sums[1], axis=1, keepdims=True)
        scale = lax.rsqrt(total / features + norm_epsilon)
        scale = jnp.broadcast_to(scale, (ROWS, lanes))
        for x in range(NX):
            for position in range(len(blocks)):
                start = columns[x * len(blocks) + position]
                for k in range(0, width, lanes):
                    column = pl.multiple_of(start + k, lanes)
                    part = held[rows, pl.ds(column, lanes)].astype(jnp.float32)
                    gain = gain_ref[:, pl.ds(column, lanes)]
                    low = position * width + k
                    ready[x, rows, low : low + lanes] = (part * scale * gain).astype(jnp.bfloat16)
            store(band, x).start()

    for copy in cot_copies:
        copy.wait()
    for band in range(bands):
        for x in range(NX):
            store(band, x).wait()


def normalize(token_rows, gain, cot, columns, blocks, width, extra, work):
    tokens, features = token_rows.shape
    depth = width * len(blocks)
    bands = tokens // ROWS
    if extra:
        out_shape = [jax.ShapeDtypeStruct((NX, tokens, depth + extra), jnp.bfloat16)]
    else:
        out_shape = [jax.ShapeDtypeStruct((tokens, depth), jnp.bfloat16)] * NX
    return pl.pallas_call(
        functools.partial(norm_kernel, width, blocks, extra),
        in_specs=[
            pl.BlockSpec(memory_space=pltpu.SMEM),
            pl.BlockSpec(memory_space=pl.ANY),
            pl.BlockSpec(memory_space=pltpu.VMEM),
            pl.BlockSpec(memory_space=pl.ANY),
        ],
        out_specs=in_memory(len(out_shape)),
        out_shape=out_shape,
        scratch_shapes=[
            pltpu.VMEM((tokens, features), jnp.bfloat16),
            pltpu.VMEM((NX, tokens, depth), jnp.bfloat16),
            pltpu.VMEM(cot.shape, jnp.bfloat16),
            pltpu.SemaphoreType.DMA((bands,)),
            pltpu.SemaphoreType.DMA((bands, NX)),
            pltpu.SemaphoreType.DMA,
            pltpu.SemaphoreType.DMA((NX,)),
        ],
        name="norm",
        **call_options(work),
    )(columns, token_rows, gain, cot)


def gradient_kernel(factor, width, count, skip, turn, sources_ref, cots_hbm, *refs):
    rows_count = 1 if turn else NX
    rows_hbm, refs = refs[:rows_count], refs[rows_count:]
    outs, refs = refs[: count - NY + 2], refs[count - NY + 2 :]
    cots, rows, ready, raw, cots_came, came, gone, turned_gone = refs
    sources, tokens, keys = raw.shape
    fetches, stores = [], []
    if turn:
        cots_copy = pltpu.make_async_copy(
            cots_hbm.at[:, :, pl.ds(count * width, keys)], raw, cots_came
        )
    else:
        cots_copy = pltpu.make_async_copy(cots_hbm, cots, cots_came)
    cots_copy.start()
    for j in range(count):
        span = pl.ds((skip + j) * width, width)
        if turn:
            pieces = [pltpu.make_async_copy(rows_hbm[0].at[:, :, span], rows.at[j], came.at[j, 0])]
        else:
            pieces = [
                pltpu.make_async_copy(
                    rows_hbm[s].at[:, span], rows.at[j, sources_ref[s]], came.at[j, s]
                )
                for s in range(sources)
            ]
        fetches.append(pieces)
        target = outs[0].at[sources_ref[j]] if j < NY else outs[1 + j - NY]
        stores.append(pltpu.make_async_copy(ready.at[j], target, gone.at[j]))
        for piece in pieces:
            piece.start()
    cots_copy.wait()
    if turn:
        for source in range(sources):
            cots[:, source * tokens : (source + 1) * tokens] = raw[source].T
        turned_copy = pltpu.make_async_copy(cots, outs[-1], turned_gone)
        turned_copy.start()
        stores.append(turned_copy)
    for j in range(count):
        for piece in fetches[j]:
            piece.wait()
        total = jnp.dot(
            cots[...],
            rows[j].reshape(sources * tokens, width),
            preferred_element_type=jnp.float32,
        )
        ready[j] = (factor * total).astype(jnp.bfloat16)
        stores[j].start()
    for store in stores:
        store.wait()


def gradient_blocks(
    sources, cots, rows, keys, width, factor, turn, work, skip=0, count=None
):
    tokens = rows[0].shape[-2]
    if count is None:
        count = (rows[0].shape[-1] - (keys if turn else 0)) // width - skip
    out_shape = [jax.ShapeDtypeStruct((NY, keys, width), jnp.bfloat16)]
    out_shape += [jax.ShapeDtypeStruct((keys, width), jnp.bfloat16)] * (count - NY)
    if turn:
        out_shape.append(jax.ShapeDtypeStruct((keys, NX * tokens), jnp.bfloat16))
    return pl.pallas_call(
        functools.partial(gradient_kernel, factor, width, count, skip, turn),
        in_specs=[pl.BlockSpec(memory_space=pltpu.SMEM)] + in_memory(1 + len(rows)),
        out_specs=in_memory(len(out_shape)),
        out_shape=out_shape,
        scratch_shapes=[
            pltpu.VMEM((keys, NX * tokens), jnp.bfloat16),
            pltpu.VMEM((count, NX, tokens, width), jnp.bfloat16),
            pltpu.VMEM((count, keys, width), jnp.bfloat16),
            pltpu.VMEM((NX, tokens, keys), jnp.bfloat16),
            pltpu.SemaphoreType.DMA,
            pltpu.SemaphoreType.DMA((count, NX)),
            pltpu.SemaphoreType.DMA((count,)),
            pltpu.SemaphoreType.DMA,
        ],
        name="gradient",
        **call_options(work),
    )(sources, cots, *rows)


def project_kernel(factor, count, has_start, sources_ref, *refs):
    refs = list(refs)
    start_hbm = refs.pop(0) if has_start else None
    rows_hbm = [refs.pop(0) for _ in range(NX if has_start else 1)]
    weights_hbm = [refs.pop(0) for _ in range(count)]
    out_hbm, rows, weights, ready, start, weights_came, came, gone, start_came = refs
    sources = rows.shape[0]
    width = weights.shape[0] // count
    weight_copies = [
        pltpu.make_async_copy(
            weights_hbm[j], weights.at[pl.ds(j * width, width)], weights_came.at[j]
        )
        for j in range(count)
    ]
    fetches, stores, starts = [], [], []
    for s in range(sources):
        if has_start:
            fetches.append(pltpu.make_async_copy(rows_hbm[s], rows.at[s], came.at[s]))
            place_at = sources_ref[s]
            starts.append(
                pltpu.make_async_copy(start_hbm.at[place_at], start.at[s], start_came.at[s])
            )
        else:
            span = pl.ds(0, count * width)
            fetches.append(
                pltpu.make_async_copy(rows_hbm[0].at[s, :, span], rows.at[s], came.at[s])
            )
            place_at = s
        stores.append(pltpu.make_async_copy(ready.at[s], out_hbm.at[place_at], gone.at[s]))
    for copy in weight_copies + fetches + starts:
        copy.start()
    for copy in weight_copies:
        copy.wait()
    for s in range(sources):
        fetches[s].wait()
        total = jnp.dot(rows[s], weights[...], preferred_element_type=jnp.float32)
        if has_start:
            starts[s].wait()
            total = factor * (total + start[s])
        ready[s] = total.astype(ready.dtype)
        stores[s].start()
    for store in stores:
        store.wait()


def project(sources, start, rows, weights, out_type, factor):
    tokens = rows[0].shape[-2]
    width, keys = weights[0].shape
    count = len(weights)
    has_start = start is not None
    flat = ([start] if has_start else []) + list(rows) + list(weights)
    return pl.pallas_call(
        functools.partial(project_kernel, factor, count, has_start),
        in_specs=[pl.BlockSpec(memory_space=pltpu.SMEM)] + in_memory(len(flat)),
        out_specs=pl.BlockSpec(memory_space=pl.ANY),
        out_shape=jax.ShapeDtypeStruct((NX, tokens, keys), out_type),
        scratch_shapes=[
            pltpu.VMEM((NX, tokens, count * width), jnp.bfloat16),
            pltpu.VMEM((count * width, keys), jnp.bfloat16),
            pltpu.VMEM((NX, tokens, keys), out_type),
            pltpu.VMEM((NX, tokens, keys), jnp.float32),
            pltpu.SemaphoreType.DMA((count,)),
            pltpu.SemaphoreType.DMA((NX,)),
            pltpu.SemaphoreType.DMA((NX,)),
            pltpu.SemaphoreType.DMA((NX,)),
        ],
        name="project",
        **call_options(),
    )(sources, *flat)


def near_gradient_kernel(factor, width, skip, sources_ref, cots, *refs):
    rows, outs = refs[:NX], refs[NX:]
    keys, all_tokens = cots.shape
    tokens = all_tokens // NX
    for j, out in enumerate(outs):
        span = slice((skip + j) * width, (skip + j + 1) * width)
        total = None
        for number, row in enumerate(rows):
            left = cots[:, pl.ds(pl.multiple_of(sources_ref[number] * tokens, 128), tokens)]
            term = jnp.dot(left, row[:, span], preferred_element_type=jnp.float32)
            total = term if total is None else total + term
        out[...] = (factor * total).astype(jnp.bfloat16)


def near_gradient(sources, cots, rows, width, factor, skip, count, work):
    keys = cots.shape[0]
    vmem = pl.BlockSpec(memory_space=pltpu.VMEM)
    return pl.pallas_call(
        functools.partial(near_gradient_kernel, factor, width, skip),
        in_specs=[pl.BlockSpec(memory_space=pltpu.SMEM)] + [vmem] * (1 + NX),
        out_specs=[vmem] * count,
        out_shape=[jax.ShapeDtypeStruct((keys, width), jnp.bfloat16)] * count,
        name="near_gradient",
        **call_options(work, VMEM_LIMIT // 2),
    )(sources, cots, *rows)


def near_project_kernel(factor, sources_ref, start, *refs):
    rows, weights, out = refs[:NX], refs[NX:-1], refs[-1]
    width = weights[0].shape[0]
    for number, row in enumerate(rows):
        total = start[sources_ref[number]]
        for j, weight in enumerate(weights):
            total = total + jnp.dot(
                row[:, j * width : (j + 1) * width],
                weight[...],
                preferred_element_type=jnp.float32,
            )
        out[sources_ref[number]] = (factor * total).astype(jnp.bfloat16)


def near_project(sources, start, rows, weights, factor):
    vmem = pl.BlockSpec(memory_space=pltpu.VMEM)
    return pl.pallas_call(
        functools.partial(near_project_kernel, factor),
        in_specs=[pl.BlockSpec(memory_space=pltpu.SMEM)] + [vmem] * (1 + NX + len(weights)),
        out_specs=vmem,
        out_shape=jax.ShapeDtypeStruct(start.shape, jnp.bfloat16),
        name="near_project",
        **call_options(1, VMEM_LIMIT // 2),
    )(sources, start, *rows, *weights)


def update_kernel(
    offset_ref, own, one, two, three, far, weight, first, second, fresh, merged_out, first_out, second_out
):
    summed = own[...].astype(jnp.float32)
    for other in (one, two, three, far):
        summed = summed + other[...].astype(jnp.float32)
    gradient = summed.T
    moment_one = beta_one * first[...] + (1.0 - beta_one) * gradient
    moment_two = beta_two * second[...] + (1.0 - beta_two) * gradient * gradient
    first_out[...] = moment_one
    second_out[...] = moment_two
    master = weight[...].astype(jnp.float32)
    stepped = master - inner_rate * (
        moment_one / (jnp.sqrt(moment_two) + adam_epsilon) + decay_rate * master
    )
    head = fresh.shape[1]
    for position in range(master.shape[1] // head):
        part = stepped[:, position * head : (position + 1) * head]
        blended = mix_weight * part + (1.0 - mix_weight) * fresh[...]
        merged_out[:, position * head : (position + 1) * head] = jnp.where(
            offset_ref[0] == position, blended, part
        ).astype(jnp.bfloat16)


def update(head_index, terms, weight, first, second, fresh):
    rows, keys = weight.shape
    head = fresh.shape[1]
    block = 128
    return pl.pallas_call(
        update_kernel,
        grid_spec=pltpu.PrefetchScalarGridSpec(
            num_scalar_prefetch=1,
            grid=(rows // block,),
            in_specs=[pl.BlockSpec((keys, block), lambda i, o: (0, i))] * 5
            + [pl.BlockSpec((block, keys), lambda i, o: (i, 0))] * 3
            + [pl.BlockSpec((block, head), lambda i, o: (i, 0))],
            out_specs=[pl.BlockSpec((block, keys), lambda i, o: (i, 0))] * 3,
        ),
        out_shape=[
            jax.ShapeDtypeStruct((rows, keys), jnp.bfloat16),
            jax.ShapeDtypeStruct((rows, keys), jnp.float32),
            jax.ShapeDtypeStruct((rows, keys), jnp.float32),
        ],
        name="update",
        **call_options(limit=VMEM_LIMIT // 4),
    )(head_index, *terms, weight, first, second, fresh)


def per_device(
    activations,
    norm_gain,
    key_cotangent,
    key_weight,
    adam_first,
    adam_second,
    outer_codes,
    outer_scales,
    global_fragment,
    outer_momentum,
    fragment_index,
):
    token_rows = activations[0]
    weight_shard = key_weight[0]
    features = token_rows.shape[1]
    factor = features ** (-0.5)
    width = weight_shard.shape[0]
    replicas = lax.axis_size("replica")

    def swap_x(value):
        return lax.all_to_all(value, "fsdp", 0, 0, axis_index_groups=along_x, tiled=True)

    def add_replica(value, step):
        return value + lax.ppermute(value, "replica", [(r, r ^ step) for r in range(replicas)])

    me = lax.axis_index("fsdp")
    my_y, my_x, my_z = me // (NX * NZ), (me // NZ) % NX, me % NZ

    along_y = [[place(y, x, z) for y in range(NY)] for x in range(NX) for z in range(NZ)]
    along_x = [[place(y, x, z) for x in range(NX)] for y in range(NY) for z in range(NZ)]

    def swap_x(value):
        return lax.all_to_all(value, "fsdp", 0, 0, axis_index_groups=along_x, tiled=True)

    def swap_x(value):
        return lax.all_to_all(value, "fsdp", 0, 0, axis_index_groups=along_x, tiled=True)

    def columns_of(relative_x, blocks):
        return jnp.stack(
            [
                place(my_y + y, (0 if relative_x is None else my_x) + x, my_z + z) * width
                for x in range(NX)
                for y, z in blocks
            ]
        ).astype(jnp.int32)

    gain = norm_gain.astype(jnp.float32)[None]
    cot = key_cotangent[0]
    keys = cot.shape[1]
    sources = jnp.stack([(my_x - d) % NX for d in range(NX)]).astype(jnp.int32)
    heavy = 10**11

    blocks = [(0, 1), (1, 1), (2, 1), (3, 1), (2, 0)]
    (part_one,) = normalize(
        token_rows, gain, cot, columns_of(None, blocks), blocks, width, keys, 1
    )
    chunk_one = swap_x(part_one)

    near_weights = [weight_shard] + [shift(weight_shard, -e, 0, 0) for e in range(1, NY)]
    far_weight = shift(weight_shard, 0, 0, 1)
    delta = outer_codes[0].astype(jnp.float32) * outer_scales[0].astype(jnp.float32)[:, None]
    delta = add_replica(delta, 1)
    delta = add_replica(delta, 2)

    token_rows, far_weight, near_weights = lax.optimization_barrier(
        (token_rows, far_weight, near_weights)
    )
    blocks = [(1, 0), (3, 0), (0, 0)]
    part_two = normalize(
        token_rows, gain, cot, columns_of(my_x, blocks), blocks, width, 0, 1
    )
    far_weights = [far_weight] + [shift(far_weight, -e, 0, 0) for e in range(1, NY)]
    delta = add_replica(delta, 4)
    part_two, far_weights, delta = lax.optimization_barrier((part_two, far_weights, delta))
    chunk_two = [part_two[0]] + [shift(part_two[d], 0, d, 0) for d in range(1, NX)]
    chunk_one, _ = lax.optimization_barrier((chunk_one, part_two))

    targets = jnp.stack([(my_y + e) % NY for e in range(NY)]).astype(jnp.int32)
    *first, cots = gradient_blocks(
        targets, chunk_one, [chunk_one], keys, width, factor, True, heavy
    )
    far = lax.all_to_all(first[0], "fsdp", 0, 0, axis_index_groups=along_y, tiled=True)
    near_two = shift(first[1], 2, 0, 0)
    partial = project(
        sources, None, [chunk_one], far_weights + [near_weights[2]], jnp.float32, factor
    )
    far = jnp.sum(far.astype(jnp.float32), axis=0).astype(jnp.bfloat16)
    cots, far, delta, partial = lax.optimization_barrier((cots, far, delta, partial))
    far = shift(far, 0, 0, 1)
    second = near_gradient(sources, cots, chunk_two, width, factor, 0, 2, heavy)
    near_one = shift(second[0], 1, 0, 0)
    near_three = shift(second[1], 3, 0, 0)

    partial, _ = lax.optimization_barrier((partial, second[1]))
    partial = near_project(
        sources, partial, chunk_two, [near_weights[1], near_weights[3], weight_shard], factor
    )
    partial, cots, far = lax.optimization_barrier((partial, cots, far))
    (own,) = near_gradient(sources, cots, chunk_two, width, factor, 2, 1, heavy)
    terms = [own, near_one, near_two, near_three, far]
    back = swap_x(partial)
    projected = jnp.sum(back.astype(jnp.float32), axis=0).astype(jnp.bfloat16)

    outer_delta = delta / replicas
    momentum = outer_beta * outer_momentum + outer_delta
    refreshed = global_fragment - outer_rate * (outer_delta + outer_beta * momentum)

    heads = weight_shard.shape[1] // global_fragment.shape[1]
    head_index = jnp.remainder(fragment_index, heads).astype(jnp.int32)
    merged, moment_one, moment_two = update(
        head_index,
        terms,
        weight_shard,
        adam_first[0],
        adam_second[0],
        refreshed,
    )
    return (
        projected[None],
        merged[None],
        moment_one[None],
        moment_two[None],
        momentum,
        refreshed,
    )


def solution(mesh):
    in_specs = (
        P("replica", "fsdp", None),
        P(),
        P("replica", "fsdp", None),
        P("replica", "fsdp", None),
        P("replica", "fsdp", None),
        P("replica", "fsdp", None),
        P("replica", "fsdp", None),
        P("replica", "fsdp"),
        P("fsdp", None),
        P("fsdp", None),
        P(),
    )
    out_specs = (
        P("replica", "fsdp", None),
        P("replica", "fsdp", None),
        P("replica", "fsdp", None),
        P("replica", "fsdp", None),
        P("fsdp", None),
        P("fsdp", None),
    )
    return jax.shard_map(
        per_device, mesh=mesh, in_specs=in_specs, out_specs=out_specs, check_vma=False
    )
```

time: 536 us -> 151 us (0.28)
  waiting for transfers between devices: 461 us -> 50.7 us
  starting transfers between devices: 0.08 us -> 44.8 us
  Pallas kernels: 0 us -> 38.6 us
  blocking collectives: 28.3 us -> 0 us
  matrix products: 21.4 us -> 0 us
  between operations: 14.8 us -> 1.76 us
  local copies, waits for them, and re-layouts: 0.05 us -> 5.41 us
    reduce_scatter x1 -> x0, waiting for transfers between devices: 302 us -> none  [per_device(): lax.psum_scatter((factor * lax.dot_general(columns, cotangent, (((0,), (0...]
    all_gather x1 -> x0, waiting for transfers between devices: 159 us -> none  [per_device(): lax.all_gather(weight_shard, 'fsdp', axis=0, tiled=True)]
    pallas_call x0 -> x8, Pallas kernels: none -> 38.6 us  [the longest x2 13.1 us: normalize(): pl.pallas_call(functools.partial(norm_kernel, width, blocks, extra), in_s...]
    ppermute x0 -> x17, waiting for transfers between devices: none -> 31 us  [the longest x14 29.6 us: shift(): return lax.ppermute(value, 'fsdp', pairs)]
    ppermute x0 -> x17, starting transfers between devices: none -> 30.9 us  [the longest x14 28.1 us: shift(): return lax.ppermute(value, 'fsdp', pairs)]
    all_gather x2 -> x0, blocking collectives: 28.3 us -> none  [the longest x1 14.5 us: per_device(): lax.all_gather(outer_codes, 'replica', axis=0, tiled=True)]
    dot_general x2 -> x0, matrix products: 21.4 us -> none  [the longest x1 10.9 us: per_device(): lax.dot_general(columns, cotangent, (((0,), (0,)), ((), ())), preferred_e...]
    all_to_all x0 -> x3, waiting for transfers between devices: none -> 19.7 us  [the longest x2 12.2 us: swap_x(): lax.all_to_all(value, 'fsdp', 0, 0, axis_index_groups=along_x, tiled=True)]
  transfers between devices with their start and end apart: 2 -> 20, of which waited for: 2 -> 10; matrix products, arithmetic and copies ran while one was open for 5% -> 4% of each run, Pallas kernels for 0% -> 15%
where the time goes in v2:
time: 151 us; the launch traced here: 150 us
  waiting for transfers between devices  50.7 us (34%)
  starting transfers between devices  44.8 us (30%)
  Pallas kernels  38.6 us (26%)
  other arithmetic  8.86 us (6%)
  local copies, waits for them, and re-layouts  5.41 us (4%)
  between operations  1.76 us (1%)
    ppermute x14, waiting for transfers between devices, shift(): return lax.ppermute(value, 'fsdp', pairs)  29.6 us
    ppermute x14, starting transfers between devices, shift(): return lax.ppermute(value, 'fsdp', pairs)  28.1 us
    pallas_call x2, Pallas kernels, normalize(): pl.pallas_call(functools.partial(norm_kernel, width, blocks, extra), in_s...  13.1 us
    all_to_all x2, waiting for transfers between devices, swap_x(): lax.all_to_all(value, 'fsdp', 0, 0, axis_index_groups=along_x, tiled=True)  12.2 us
    all_to_all x2, starting transfers between devices, swap_x(): lax.all_to_all(value, 'fsdp', 0, 0, axis_index_groups=along_x, tiled=True)  9.39 us
    pallas_call x1, Pallas kernels, gradient_blocks(): pl.pallas_call(functools.partial(gradient_kernel, factor, width, count, s...  7.76 us
    all_to_all x1, waiting for transfers between devices, per_device(): lax.all_to_all(first[0], 'fsdp', 0, 0, axis_index_groups=along_y, tiled=T...  7.48 us
    pallas_call x1, Pallas kernels, project(): pl.pallas_call(functools.partial(project_kernel, factor, count, has_start...  6.79 us
  transfers between devices with their start and end apart: 20, of which 10 were waited for; matrix products, arithmetic and copies ran while one was open for 4% of the time, Pallas kernels for 15%

profile of v2, /device:TPU:32, one launch (start us, length us, event | category | flops | bytes accessed | tf_op | source)
XLA Modules:
  0.0 150.1 jit_solution(5612022003536901873)
XLA Ops:
  2.8 7.7 %norm.2 = bf16[4,256,2432]{2,1,0:T(8,128)(2,1)} custom-call(s32[20]{0:T(128)} %stack.162.column_ref, bf16[256,12288]{1,0:T(8,128)(2,1)} %bitcast.63, f32[1,12288]{1,0:T(1,128)} %bitcast.67, bf16[256,512]{1,0:T(8,128)(2,1)} %bitcast.65), custom_call_target="tpu_custom_call" | custom-call | flops 1 | bytes 1 | tf_op jit(solution)/shard_map/norm/pallas_call | solution.py:122
  10.5 5.1 %all-to-all-start = ((bf16[4,256,2432]{2,1,0:T(8,128)(2,1)}), bf16[4,256,2432]{2,1,0:T(8,128)(2,1)}, u32[]{:S(2)}, u32[]{:S(2)}) async-start(bf16[4,256,2432]{2,1,0:T(8,128)(2,1)} %norm.2), calls=%async_computation | async-start | bytes 9961472 | tf_op jit(solution)/shard_map/all_to_all | solution.py:435
  15.9 6.4 %collective-permute-start = (bf16[384,512]{1,0:T(8,128)(2,1)S(1)}, bf16[384,512]{1,0:T(8,128)(2,1)S(1)}, u32[]{:S(2)}, u32[]{:S(2)}) collective-permute-start(bf16[384,512]{1,0:T(8,128)(2,1)S(1)} %bitcast.55), channel_id=1, source_target_pairs={{0,1},{1,0},{2,3},{3,2},{4,5},{5,4},{6,7},{7,6},{8,9},{9,8},{10,11... | collective-permute-start | bytes 1179656 | tf_op jit(solution)/shard_map/ppermute | solution.py:36
  22.3 3.0 %collective-permute-start.1 = (bf16[384,512]{1,0:T(8,128)(2,1)S(1)}, bf16[384,512]{1,0:T(8,128)(2,1)S(1)}, u32[]{:S(2)}, u32[]{:S(2)}) collective-permute-start(bf16[384,512]{1,0:T(8,128)(2,1)S(1)} %bitcast.56), channel_id=1, source_target_pairs={{0,24},{1,25},{2,26},{3,27},{4,28},{5,29},{6,30},{7,31},{8,0},{9,1... | collective-permute-start | bytes 1179656 | tf_op jit(solution)/shard_map/ppermute | solution.py:36
  28.1 12.6 %collective-permute-done.refs_1_ = bf16[384,512]{1,0:T(8,128)(2,1)S(1)} collective-permute-done((bf16[384,512]{1,0:T(8,128)(2,1)S(1)}, bf16[384,512]{1,0:T(8,128)(2,1)S(1)}, u32[]{:S(2)}, u32[]{:S(2)}) %collective-permute-start) | collective-permute-done | bytes 393248 | tf_op jit(solution)/shard_map/ppermute | solution.py:36
  43.2 2.9 %collective-permute-done.3.refs_5_ = bf16[384,512]{1,0:T(8,128)(2,1)S(1)} collective-permute-done((bf16[384,512]{1,0:T(8,128)(2,1)S(1)}, bf16[384,512]{1,0:T(8,128)(2,1)S(1)}, u32[]{:S(2)}, u32[]{:S(2)}) %collective-permute-start.3) | collective-permute-done | bytes 393248 | tf_op jit(solution)/shard_map/ppermute | solution.py:36
  51.8 5.4 %norm.3 = (bf16[256,1152]{1,0:T(8,128)(2,1)}, bf16[256,1152]{1,0:T(8,128)(2,1)}, bf16[256,1152]{1,0:T(8,128)(2,1)}, bf16[256,1152]{1,0:T(8,128)(2,1)}) custom-call(s32[12]{0:T(128)} %stack.175.column_ref, bf16[256,12288]{1,0:T(8,128)(2,1)} %bitcast.64, f32[1,12288]{1,0:T(1,128)} %bitcast.68, bf16[256,512]{1,0:T(8,128)(2,1)} %bitcast.66), custom_call_target="tpu_custom_call" | custom-call | flops 1 | bytes 1 | tf_op jit(solution)/shard_map/norm/pallas_call | solution.py:122
  61.3 6.7 %collective-permute-done.6.refs_4_ = bf16[384,512]{1,0:T(8,128)(2,1)S(1)} collective-permute-done((bf16[384,512]{1,0:T(8,128)(2,1)S(1)}, bf16[384,512]{1,0:T(8,128)(2,1)S(1)}, u32[]{:S(2)}, u32[]{:S(2)}) %collective-permute-start.6) | collective-permute-done | bytes 393248 | tf_op jit(solution)/shard_map/ppermute | solution.py:36
  68.0 5.3 %all-to-all-done.cots_hbm.refs_0_ = bf16[4,256,2432]{2,1,0:T(8,128)(2,1)} async-done(((bf16[4,256,2432]{2,1,0:T(8,128)(2,1)}), bf16[4,256,2432]{2,1,0:T(8,128)(2,1)}, u32[]{:S(2)}, u32[]{:S(2)}) %all-to-all-start) | async-done | bytes 4980768 | tf_op jit(solution)/shard_map/all_to_all | solution.py:435
  73.2 7.8 %gradient.1 = (bf16[4,512,384]{2,1,0:T(8,128)(2,1)}, bf16[512,384]{1,0:T(8,128)(2,1)}, bf16[512,1024]{1,0:T(8,128)(2,1)}) custom-call(s32[4]{0:T(128)} %pad_add_fusion.1.sources_ref, bf16[4,256,2432]{2,1,0:T(8,128)(2,1)} %all-to-all-done.cots_hbm.refs_0_, bf16[4,256,2432]{2,1,0:T(8,128)(2,1)} %all-to-all-done.cots_hbm.refs_0_), custom_call_target="tpu_custom_call" | custom-call | flops 99999997952 | bytes 1 | tf_op jit(solution)/shard_map/gradient/pallas_call | solution.py:207
  81.0 4.5 %all-to-all-start.1 = ((bf16[4,512,384]{2,1,0:T(8,128)(2,1)}), bf16[4,512,384]{2,1,0:T(8,128)(2,1)}, u32[]{:S(2)}, u32[]{:S(2)}) async-start(bf16[4,512,384]{2,1,0:T(8,128)(2,1)} %get-tuple-element.53), calls=%async_computation.1 | async-start | bytes 3145728 | tf_op jit(solution)/shard_map/all_to_all | solution.py:481
  86.1 2.1 %collective-permute-start.11 = (bf16[256,1152]{1,0:T(8,128)(2,1)}, bf16[256,1152]{1,0:T(8,128)(2,1)S(1)}, u32[]{:S(2)}, u32[]{:S(2)}) collective-permute-start(bf16[256,1152]{1,0:T(8,128)(2,1)} %get-tuple-element.49), channel_id=1, source_target_pairs={{0,4},{1,5},{2,6},{3,7},{4,0},{5,1},{6,2},{7,3},{8,12},{9,13},{10,... | collective-permute-start | bytes 1769480 | tf_op jit(solution)/shard_map/ppermute | solution.py:36
  90.3 3.3 %collective-permute-start.15 = (bf16[512,384]{1,0:T(8,128)(2,1)}, bf16[512,384]{1,0:T(8,128)(2,1)}, u32[]{:S(2)}, u32[]{:S(2)}) collective-permute-start(bf16[512,384]{1,0:T(8,128)(2,1)} %get-tuple-element.70), channel_id=1, source_target_pairs={{0,16},{1,17},{2,18},{3,19},{4,20},{5,21},{6,22},{7,23},{8,24},{9,... | collective-permute-start | bytes 1179656 | tf_op jit(solution)/shard_map/ppermute | solution.py:36
  93.5 6.8 %project.1.start = f32[4,256,512]{2,1,0:T(8,128)} custom-call(s32[4]{0:T(128)} %pad_add_fusion.sources_ref, bf16[4,256,2432]{2,1,0:T(8,128)(2,1)} %all-to-all-done.cots_hbm.refs_0_, bf16[384,512]{1,0:T(8,128)(2,1)} %copy-done.14, bf16[384,512]{1,0:T(8,128)(2,1)} %copy-done.16, bf16[384,512]{1,0:T(8,128)(2,1)} %copy-done.17, bf16[384,512]{1,0:T(8,128)(2,1)} %copy-done.18, ...), custom_call_target="tpu_custom_call" | custom-call | flops 1 | bytes 1 | tf_op jit(solution)/shard_map/project/pallas_call | solution.py:278
  100.3 7.5 %all-to-all-done.1 = bf16[4,512,384]{2,1,0:T(8,128)(2,1)} async-done(((bf16[4,512,384]{2,1,0:T(8,128)(2,1)}), bf16[4,512,384]{2,1,0:T(8,128)(2,1)}, u32[]{:S(2)}, u32[]{:S(2)}) %all-to-all-start.1) | async-done | bytes 1572896 | tf_op jit(solution)/shard_map/all_to_all | solution.py:481
  107.8 2.5 %reduce_sum.24 = bf16[512,384]{1,0:T(8,128)(2,1)} reduce(bf16[4,512,384]{2,1,0:T(8,128)(2,1)} %all-to-all-done.1, bf16[]{:T(256)} %constant.275.clone.1), dimensions={0}, to_apply=%region_0.1 | reduce | flops 589824 | bytes 1966082 | tf_op jit(solution)/shard_map/reduce_sum | solution.py:486
  110.3 6.3 %collective-permute-start.13 = (bf16[512,384]{1,0:T(8,128)(2,1)}, bf16[512,384]{1,0:T(8,128)(2,1)S(1)}, u32[]{:S(2)}, u32[]{:S(2)}) collective-permute-start(bf16[512,384]{1,0:T(8,128)(2,1)} %reduce_sum.24), channel_id=1, source_target_pairs={{0,1},{1,0},{2,3},{3,2},{4,5},{5,4},{6,7},{7,6},{8,9},{9,8},{10,11... | collective-permute-start | bytes 1179656 | tf_op jit(solution)/shard_map/ppermute | solution.py:36
  117.9 2.5 %near_gradient.2 = (bf16[512,384]{1,0:T(8,128)(2,1)}, bf16[512,384]{1,0:T(8,128)(2,1)}) custom-call(s32[4]{0:T(128)S(1)} %copy-done.10, bf16[512,1024]{1,0:T(8,128)(2,1)S(1)} %copy-done.11, bf16[256,1152]{1,0:T(8,128)(2,1)S(1)} %copy-done.5, bf16[256,1152]{1,0:T(8,128)(2,1)S(1)} %collective-permute-done.10.refs_1_, ...), custom_call_target="tpu_custom_call" | custom-call | flops 99999997952 | bytes 1 | tf_op jit(solution)/shard_map/near_gradient/pallas_call | solution.py:315
  122.5 3.3 %near_project.1 = bf16[4,256,512]{2,1,0:T(8,128)(2,1)} custom-call(s32[4]{0:T(128)S(1)} %copy-done.10, f32[4,256,512]{2,1,0:T(8,128)S(1)} %copy-done, bf16[256,1152]{1,0:T(8,128)(2,1)S(1)} %copy-done.5, bf16[256,1152]{1,0:T(8,128)(2,1)S(1)} %collective-permute-done.10.refs_1_, bf16[256,1152]{1,0:T(8,128)(2,1)S(1)} %collective-permute-done.11.refs_2_, ...), custom_call_target="tpu_custom_call" | custom-call | flops 1 | bytes 1 | tf_op jit(solution)/shard_map/near_project/pallas_call | solution.py:341
  126.5 3.8 %collective-permute-done.13.far = bf16[512,384]{1,0:T(8,128)(2,1)S(1)} collective-permute-done((bf16[512,384]{1,0:T(8,128)(2,1)}, bf16[512,384]{1,0:T(8,128)(2,1)S(1)}, u32[]{:S(2)}, u32[]{:S(2)}) %collective-permute-start.13) | collective-permute-done | bytes 393248 | tf_op jit(solution)/shard_map/ppermute | solution.py:36
  130.3 4.2 %all-to-all-start.2 = ((bf16[4,256,512]{2,1,0:T(8,128)(2,1)}), bf16[4,256,512]{2,1,0:T(8,128)(2,1)}, u32[]{:S(2)}, u32[]{:S(2)}) async-start(bf16[4,256,512]{2,1,0:T(8,128)(2,1)} %near_project.1), calls=%async_computation.2 | async-start | bytes 2097152 | tf_op jit(solution)/shard_map/all_to_all | solution.py:435
  137.1 3.8 %update.1 = (bf16[384,512]{1,0:T(8,128)(2,1)}, f32[384,512]{1,0:T(8,128)}, f32[384,512]{1,0:T(8,128)}) custom-call(s32[1]{0:T(128)S(6)} %select_n.235.offset_ref, bf16[512,384]{1,0:T(8,128)(2,1)S(1)} %near_gradient.3.own, bf16[512,384]{1,0:T(8,128)(2,1)} %collective-permute-done.14.one, bf16[512,384]{1,0:T(8,128)(2,1)} %collective-permute-done.15.two, ...), custom_call_target="tpu_custom_call" | custom-call | flops 1 | bytes 1 | tf_op jit(solution)/shard_map/update/pallas_call | solution.py:379
  141.0 7.0 %all-to-all-done.2 = bf16[4,256,512]{2,1,0:T(8,128)(2,1)} async-done(((bf16[4,256,512]{2,1,0:T(8,128)(2,1)}), bf16[4,256,512]{2,1,0:T(8,128)(2,1)}, u32[]{:S(2)}, u32[]{:S(2)}) %all-to-all-start.2) | async-done | bytes 1048608 | tf_op jit(solution)/shard_map/all_to_all | solution.py:435
  147.9 2.2 %reduce_sum.25 = bf16[256,512]{1,0:T(8,128)(2,1)} reduce(bf16[4,256,512]{2,1,0:T(8,128)(2,1)} %all-to-all-done.2, bf16[]{:T(256)} %constant.275.clone.1), dimensions={0}, to_apply=%region_1.2 | reduce | flops 393216 | bytes 1310722 | tf_op jit(solution)/shard_map/reduce_sum | solution.py:501
  (83 shorter events, 25.8 us)
Async XLA Ops:
  10.5 62.7 %all-to-all-start = ((bf16[4,256,2432]{2,1,0:T(8,128)(2,1)}), bf16[4,256,2432]{2,1,0:T(8,128)(2,1)}, u32[]{:S(2)}, u32[]{:S(2)}) async-start(bf16[4,256,2432]{2,1,0:T(8,128)(2,1)} %norm.2), calls=%async_computation | async-start | bytes 9961472 | tf_op jit(solution)/shard_map/all_to_all | solution.py:435
  15.8 11.1 %collective-permute-start.7 = (f32[384,128]{1,0:T(8,128)S(1)}, f32[384,128]{1,0:T(8,128)S(1)}, u32[]{:S(2)}, u32[]{:S(2)}) collective-permute-start(f32[384,128]{1,0:T(8,128)S(1)} %convert_multiply_fusion), channel_id=1, source_target_pairs={{0,32},{32,0},{64,96},{96,64},{128,160},{160,128},{192,224},{224,1... | collective-permute-start | bytes 589832 | tf_op jit(solution)/shard_map/ppermute | solution.py:423
  15.9 24.8 %collective-permute-start = (bf16[384,512]{1,0:T(8,128)(2,1)S(1)}, bf16[384,512]{1,0:T(8,128)(2,1)S(1)}, u32[]{:S(2)}, u32[]{:S(2)}) collective-permute-start(bf16[384,512]{1,0:T(8,128)(2,1)S(1)} %bitcast.55), channel_id=1, source_target_pairs={{0,1},{1,0},{2,3},{3,2},{4,5},{5,4},{6,7},{7,6},{8,9},{9,8},{10,11... | collective-permute-start | bytes 1179656 | tf_op jit(solution)/shard_map/ppermute | solution.py:36
  22.3 20.1 %collective-permute-start.1 = (bf16[384,512]{1,0:T(8,128)(2,1)S(1)}, bf16[384,512]{1,0:T(8,128)(2,1)S(1)}, u32[]{:S(2)}, u32[]{:S(2)}) collective-permute-start(bf16[384,512]{1,0:T(8,128)(2,1)S(1)} %bitcast.56), channel_id=1, source_target_pairs={{0,24},{1,25},{2,26},{3,27},{4,28},{5,29},{6,30},{7,31},{8,0},{9,1... | collective-permute-start | bytes 1179656 | tf_op jit(solution)/shard_map/ppermute | solution.py:36
  25.3 17.9 %collective-permute-start.2 = (bf16[384,512]{1,0:T(8,128)(2,1)S(1)}, bf16[384,512]{1,0:T(8,128)(2,1)S(1)}, u32[]{:S(2)}, u32[]{:S(2)}) collective-permute-start(bf16[384,512]{1,0:T(8,128)(2,1)S(1)} %bitcast.57), channel_id=1, source_target_pairs={{0,16},{1,17},{2,18},{3,19},{4,20},{5,21},{6,22},{7,23},{8,24},{9,... | collective-permute-start | bytes 1179656 | tf_op jit(solution)/shard_map/ppermute | solution.py:36
  26.0 20.2 %collective-permute-start.3 = (bf16[384,512]{1,0:T(8,128)(2,1)S(1)}, bf16[384,512]{1,0:T(8,128)(2,1)S(1)}, u32[]{:S(2)}, u32[]{:S(2)}) collective-permute-start(bf16[384,512]{1,0:T(8,128)(2,1)S(1)} %bitcast.58), channel_id=1, source_target_pairs={{0,8},{1,9},{2,10},{3,11},{4,12},{5,13},{6,14},{7,15},{8,16},{9,17... | collective-permute-start | bytes 1179656 | tf_op jit(solution)/shard_map/ppermute | solution.py:36
  27.1 21.9 %collective-permute-start.8 = (f32[384,128]{1,0:T(8,128)S(1)}, f32[384,128]{1,0:T(8,128)S(1)}, u32[]{:S(2)}, u32[]{:S(2)}) collective-permute-start(f32[384,128]{1,0:T(8,128)S(1)} %fusion), channel_id=1, source_target_pairs={{0,64},{32,96},{64,0},{96,32},{128,192},{160,224},{192,128},{224,1... | collective-permute-start | bytes 589832 | tf_op jit(solution)/shard_map/ppermute | solution.py:423
  40.7 40.3 %copy-start.14 = (bf16[384,512]{1,0:T(8,128)(2,1)}, bf16[384,512]{1,0:T(8,128)(2,1)S(1)}, u32[]{:S(2)}) copy-start(bf16[384,512]{1,0:T(8,128)(2,1)S(1)} %collective-permute-done.refs_1_) | copy-start | bytes 1179652
  43.2 37.8 %copy-start.15 = (bf16[384,512]{1,0:T(8,128)(2,1)}, bf16[384,512]{1,0:T(8,128)(2,1)S(1)}, u32[]{:S(2)}) copy-start(bf16[384,512]{1,0:T(8,128)(2,1)S(1)} %collective-permute-done.2.refs_5_) | copy-start | bytes 1179652
  46.9 12.4 %collective-permute-start.4 = (bf16[384,512]{1,0:T(8,128)(2,1)S(1)}, bf16[384,512]{1,0:T(8,128)(2,1)S(1)}, u32[]{:S(2)}, u32[]{:S(2)}) collective-permute-start(bf16[384,512]{1,0:T(8,128)(2,1)S(1)} %collective-permute-done.refs_1_), channel_id=1, source_target_pairs={{0,24},{1,25},{2,26},{3,27},{4,28},{5,29},{6,30},{7,31},{8,0},{9,1... | collective-permute-start | bytes 1179656 | tf_op jit(solution)/shard_map/ppermute | solution.py:36
  47.7 13.6 %collective-permute-start.5 = (bf16[384,512]{1,0:T(8,128)(2,1)S(1)}, bf16[384,512]{1,0:T(8,128)(2,1)S(1)}, u32[]{:S(2)}, u32[]{:S(2)}) collective-permute-start(bf16[384,512]{1,0:T(8,128)(2,1)S(1)} %collective-permute-done.refs_1_), channel_id=1, source_target_pairs={{0,16},{1,17},{2,18},{3,19},{4,20},{5,21},{6,22},{7,23},{8,24},{9,... | collective-permute-start | bytes 1179656 | tf_op jit(solution)/shard_map/ppermute | solution.py:36
  48.1 19.8 %collective-permute-start.6 = (bf16[384,512]{1,0:T(8,128)(2,1)S(1)}, bf16[384,512]{1,0:T(8,128)(2,1)S(1)}, u32[]{:S(2)}, u32[]{:S(2)}) collective-permute-start(bf16[384,512]{1,0:T(8,128)(2,1)S(1)} %collective-permute-done.refs_1_), channel_id=1, source_target_pairs={{0,8},{1,9},{2,10},{3,11},{4,12},{5,13},{6,14},{7,15},{8,16},{9,17... | collective-permute-start | bytes 1179656 | tf_op jit(solution)/shard_map/ppermute | solution.py:36
  49.0 9.6 %collective-permute-start.9 = (f32[384,128]{1,0:T(8,128)S(1)}, f32[384,128]{1,0:T(8,128)S(1)}, u32[]{:S(2)}, u32[]{:S(2)}) collective-permute-start(f32[384,128]{1,0:T(8,128)S(1)} %add.459), channel_id=1, source_target_pairs={{0,128},{32,160},{64,192},{96,224},{128,0},{160,32},{192,64},{224,... | collective-permute-start | bytes 589832 | tf_op jit(solution)/shard_map/ppermute | solution.py:423
  81.0 26.8 %all-to-all-start.1 = ((bf16[4,512,384]{2,1,0:T(8,128)(2,1)}), bf16[4,512,384]{2,1,0:T(8,128)(2,1)}, u32[]{:S(2)}, u32[]{:S(2)}) async-start(bf16[4,512,384]{2,1,0:T(8,128)(2,1)} %get-tuple-element.53), calls=%async_computation.1 | async-start | bytes 3145728 | tf_op jit(solution)/shard_map/all_to_all | solution.py:481
  85.5 31.1 %collective-permute-start.10 = (bf16[256,1152]{1,0:T(8,128)(2,1)}, bf16[256,1152]{1,0:T(8,128)(2,1)S(1)}, u32[]{:S(2)}, u32[]{:S(2)}) collective-permute-start(bf16[256,1152]{1,0:T(8,128)(2,1)} %get-tuple-element.48), channel_id=1, source_target_pairs={{0,2},{1,3},{2,4},{3,5},{4,6},{5,7},{6,0},{7,1},{8,10},{9,11},{10,... | collective-permute-start | bytes 1769480 | tf_op jit(solution)/shard_map/ppermute | solution.py:36
  86.1 30.5 %collective-permute-start.11 = (bf16[256,1152]{1,0:T(8,128)(2,1)}, bf16[256,1152]{1,0:T(8,128)(2,1)S(1)}, u32[]{:S(2)}, u32[]{:S(2)}) collective-permute-start(bf16[256,1152]{1,0:T(8,128)(2,1)} %get-tuple-element.49), channel_id=1, source_target_pairs={{0,4},{1,5},{2,6},{3,7},{4,0},{5,1},{6,2},{7,3},{8,12},{9,13},{10,... | collective-permute-start | bytes 1769480 | tf_op jit(solution)/shard_map/ppermute | solution.py:36
  88.1 28.5 %collective-permute-start.12 = (bf16[256,1152]{1,0:T(8,128)(2,1)}, bf16[256,1152]{1,0:T(8,128)(2,1)S(1)}, u32[]{:S(2)}, u32[]{:S(2)}) collective-permute-start(bf16[256,1152]{1,0:T(8,128)(2,1)} %get-tuple-element.50), channel_id=1, source_target_pairs={{0,6},{1,7},{2,0},{3,1},{4,2},{5,3},{6,4},{7,5},{8,14},{9,15},{10,... | collective-permute-start | bytes 1769480 | tf_op jit(solution)/shard_map/ppermute | solution.py:36
  90.3 26.4 %copy-start.5 = (bf16[256,1152]{1,0:T(8,128)(2,1)S(1)}, bf16[256,1152]{1,0:T(8,128)(2,1)}, u32[]{:S(2)}) copy-start(bf16[256,1152]{1,0:T(8,128)(2,1)} %get-tuple-element.47.refs_0_) | copy-start | bytes 1769476
  90.3 26.4 %copy-start.10 = (s32[4]{0:T(128)S(1)}, s32[4]{0:T(128)}, u32[]{:S(2)}) copy-start(s32[4]{0:T(128)} %pad_add_fusion.sources_ref) | copy-start | bytes 52
  90.3 46.8 %collective-permute-start.15 = (bf16[512,384]{1,0:T(8,128)(2,1)}, bf16[512,384]{1,0:T(8,128)(2,1)}, u32[]{:S(2)}, u32[]{:S(2)}) collective-permute-start(bf16[512,384]{1,0:T(8,128)(2,1)} %get-tuple-element.70), channel_id=1, source_target_pairs={{0,16},{1,17},{2,18},{3,19},{4,20},{5,21},{6,22},{7,23},{8,24},{9,... | collective-permute-start | bytes 1179656 | tf_op jit(solution)/shard_map/ppermute | solution.py:36
  110.3 20.0 %collective-permute-start.13 = (bf16[512,384]{1,0:T(8,128)(2,1)}, bf16[512,384]{1,0:T(8,128)(2,1)S(1)}, u32[]{:S(2)}, u32[]{:S(2)}) collective-permute-start(bf16[512,384]{1,0:T(8,128)(2,1)} %reduce_sum.24), channel_id=1, source_target_pairs={{0,1},{1,0},{2,3},{3,2},{4,5},{5,4},{6,7},{7,6},{8,9},{9,8},{10,11... | collective-permute-start | bytes 1179656 | tf_op jit(solution)/shard_map/ppermute | solution.py:36
  120.4 16.6 %collective-permute-start.16 = (bf16[512,384]{1,0:T(8,128)(2,1)}, bf16[512,384]{1,0:T(8,128)(2,1)}, u32[]{:S(2)}, u32[]{:S(2)}) collective-permute-start(bf16[512,384]{1,0:T(8,128)(2,1)} %get-tuple-element.62), channel_id=1, source_target_pairs={{0,24},{1,25},{2,26},{3,27},{4,28},{5,29},{6,30},{7,31},{8,0},{9,1... | collective-permute-start | bytes 1179656 | tf_op jit(solution)/shard_map/ppermute | solution.py:36
  121.6 15.5 %collective-permute-start.14 = (bf16[512,384]{1,0:T(8,128)(2,1)}, bf16[512,384]{1,0:T(8,128)(2,1)}, u32[]{:S(2)}, u32[]{:S(2)}) collective-permute-start(bf16[512,384]{1,0:T(8,128)(2,1)} %get-tuple-element.69), channel_id=1, source_target_pairs={{0,8},{1,9},{2,10},{3,11},{4,12},{5,13},{6,14},{7,15},{8,16},{9,17... | collective-permute-start | bytes 1179656 | tf_op jit(solution)/shard_map/ppermute | solution.py:36
  130.3 17.6 %all-to-all-start.2 = ((bf16[4,256,512]{2,1,0:T(8,128)(2,1)}), bf16[4,256,512]{2,1,0:T(8,128)(2,1)}, u32[]{:S(2)}, u32[]{:S(2)}) async-start(bf16[4,256,512]{2,1,0:T(8,128)(2,1)} %near_project.1), calls=%async_computation.2 | async-start | bytes 2097152 | tf_op jit(solution)/shard_map/all_to_all | solution.py:435
  (19 other events, 140.1 us)

commit v3 on v2

v3 whole, which is shorter than its diff:
```python
import functools

import jax
import jax.numpy as jnp
from jax import lax
from jax.experimental import pallas as pl
from jax.experimental.pallas import tpu as pltpu
from jax.sharding import PartitionSpec as P

norm_epsilon = 1e-05
adam_epsilon = 1e-08
beta_one = 0.9
beta_two = 0.95
inner_rate = 0.02
decay_rate = 0.1
outer_beta = 0.9
outer_rate = 0.7
mix_weight = 0.5

NY, NX, NZ = 4, 4, 2
ROWS = 32
AHEAD = 3
VMEM_LIMIT = 60 * 1024 * 1024
HEAVY = 10**11


def place(y, x, z):
    return ((y % NY) * NX + x % NX) * NZ + z % NZ


def shift(value, dy, dx, dz):
    pairs = [
        (place(y, x, z), place(y + dy, x + dx, z + dz))
        for y in range(NY)
        for x in range(NX)
        for z in range(NZ)
    ]
    return lax.ppermute(value, "fsdp", pairs)


def in_memory(count):
    return [pl.BlockSpec(memory_space=pl.ANY)] * count


def call_options(work=1, limit=VMEM_LIMIT):
    return dict(
        compiler_params=pltpu.CompilerParams(vmem_limit_bytes=limit),
        cost_estimate=pl.CostEstimate(flops=work, bytes_accessed=1, transcendentals=0),
    )


def norm_kernel(width, blocks, relative, extra, rows_hbm, gain_ref, cot_hbm, *refs):
    outs, (held, ready, cot, gains, came, gone, cot_came, cot_gone) = refs[:-8], refs[-8:]
    tokens, features = held.shape
    depth = width * len(blocks)
    lanes = 128
    bands = tokens // ROWS
    me = lax.axis_index("fsdp")
    my_y, my_x, my_z = me // (NX * NZ), (me // NZ) % NX, me % NZ

    def fetch(band):
        rows = pl.ds(pl.multiple_of(band * ROWS, ROWS), ROWS)
        return pltpu.make_async_copy(rows_hbm.at[rows], held.at[rows], came.at[band])

    def store(band, x):
        rows = pl.ds(pl.multiple_of(band * ROWS, ROWS), ROWS)
        if len(outs) == 1:
            target = outs[0].at[x, rows, pl.ds(0, depth)]
        else:
            target = outs[x].at[rows]
        return pltpu.make_async_copy(ready.at[x, rows], target, gone.at[band, x])

    for band in range(AHEAD):
        fetch(band).start()
    cot_copies = []
    if extra:
        cot_fetch = pltpu.make_async_copy(cot_hbm, cot, cot_came)
        cot_fetch.start()
        cot_copies = [
            pltpu.make_async_copy(cot, outs[0].at[x, :, pl.ds(depth, extra)], cot_gone.at[x])
            for x in range(NX)
        ]
    gains[...] = gain_ref[...].astype(jnp.float32)
    starts = [
        [
            place(my_y + y, (my_x if relative else 0) + x, my_z + z) * (width // lanes)
            for y, z in blocks
        ]
        for x in range(NX)
    ]

    @pl.loop(0, bands)
    def _(band):
        @pl.when(band + AHEAD < bands)
        def _():
            fetch(band + AHEAD).start()

        fetch(band).wait()
        rows = pl.ds(pl.multiple_of(band * ROWS, ROWS), ROWS)
        sums = [jnp.zeros((ROWS, lanes), jnp.float32) for _ in range(2)]
        for k in range(features // lanes):
            part = held[rows, k * lanes : (k + 1) * lanes].astype(jnp.float32)
            sums[k % 2] = sums[k % 2] + part * part
        total = jnp.sum(sums[0] + sums[1], axis=1, keepdims=True)
        scale = lax.rsqrt(total / features + norm_epsilon)
        scale = jnp.broadcast_to(scale, (ROWS, lanes))
        for x in range(NX):
            for position in range(len(blocks)):
                for k in range(width // lanes):
                    tile = starts[x][position] + k
                    column = pl.multiple_of(tile * lanes, lanes)
                    part = held[rows, pl.ds(column, lanes)].astype(jnp.float32)
                    gain = gains[pl.ds(tile, 1), :]
                    low = position * width + k * lanes
                    ready[x, rows, low : low + lanes] = (part * scale * gain).astype(jnp.bfloat16)
            store(band, x).start()

    if extra:
        cot_fetch.wait()
        for copy in cot_copies:
            copy.start()
        for copy in cot_copies:
            copy.wait()
    for band in range(bands):
        for x in range(NX):
            store(band, x).wait()


def normalize(token_rows, gain, cot, blocks, relative, width, extra):
    tokens, features = token_rows.shape
    depth = width * len(blocks)
    bands = tokens // ROWS
    if extra:
        out_shape = [jax.ShapeDtypeStruct((NX, tokens, depth + extra), jnp.bfloat16)]
    else:
        out_shape = [jax.ShapeDtypeStruct((tokens, depth), jnp.bfloat16)] * NX
    return pl.pallas_call(
        functools.partial(norm_kernel, width, blocks, relative, extra),
        in_specs=[
            pl.BlockSpec(memory_space=pl.ANY),
            pl.BlockSpec(memory_space=pltpu.VMEM),
            pl.BlockSpec(memory_space=pl.ANY),
        ],
        out_specs=in_memory(len(out_shape)),
        out_shape=out_shape,
        scratch_shapes=[
            pltpu.VMEM((tokens, features), jnp.bfloat16),
            pltpu.VMEM((NX, tokens, depth), jnp.bfloat16),
            pltpu.VMEM(cot.shape, jnp.bfloat16),
            pltpu.VMEM(gain.shape, jnp.float32),
            pltpu.SemaphoreType.DMA((bands,)),
            pltpu.SemaphoreType.DMA((bands, NX)),
            pltpu.SemaphoreType.DMA,
            pltpu.SemaphoreType.DMA((NX,)),
        ],
        name="norm",
        **call_options(),
    )(token_rows, gain, cot)


VMEM = pl.BlockSpec(memory_space=pltpu.VMEM)
SMEM = pl.BlockSpec(memory_space=pltpu.SMEM)


def far_gradient_kernel(factor, width, targets_ref, chunk, far_hbm, cots, ready, gone):
    sources, tokens, depth = chunk.shape
    keys = cots.shape[0]
    for source in range(sources):
        cots[:, source * tokens : (source + 1) * tokens] = chunk[source, :, depth - keys :].T
    copies = []
    for j in range(NY):
        total = None
        for source in range(sources):
            term = jnp.dot(
                cots[:, source * tokens : (source + 1) * tokens],
                chunk[source, :, j * width : (j + 1) * width],
                preferred_element_type=jnp.float32,
            )
            total = term if total is None else total + term
        ready[j] = (factor * total).astype(jnp.bfloat16)
        copies.append(
            pltpu.make_async_copy(ready.at[j], far_hbm.at[targets_ref[j]], gone.at[j])
        )
        copies[j].start()
    for copy in copies:
        copy.wait()


def far_gradient(targets, chunk, keys, width, factor):
    sources, tokens, _ = chunk.shape
    return pl.pallas_call(
        functools.partial(far_gradient_kernel, factor, width),
        in_specs=[SMEM, VMEM],
        out_specs=[pl.BlockSpec(memory_space=pl.ANY), VMEM],
        out_shape=[
            jax.ShapeDtypeStruct((NY, keys, width), jnp.bfloat16),
            jax.ShapeDtypeStruct((keys, sources * tokens), jnp.bfloat16),
        ],
        scratch_shapes=[
            pltpu.VMEM((NY, keys, width), jnp.bfloat16),
            pltpu.SemaphoreType.DMA((NY,)),
        ],
        name="far_gradient",
        **call_options(HEAVY, VMEM_LIMIT // 3),
    )(targets, chunk)


def add_up_kernel(terms, out):
    total = terms[0].astype(jnp.float32)
    for number in range(1, terms.shape[0]):
        total = total + terms[number].astype(jnp.float32)
    out[...] = total.astype(out.dtype)


def add_up(terms):
    return pl.pallas_call(
        add_up_kernel,
        in_specs=[VMEM],
        out_specs=VMEM,
        out_shape=jax.ShapeDtypeStruct(terms.shape[1:], terms.dtype),
        name="add_up",
        **call_options(1, VMEM_LIMIT // 3),
    )(terms)


def far_project_kernel(sources_ref, chunk, *refs):
    weights, outs = refs[:-NX], refs[-NX:]
    width = weights[0].shape[0]
    for out_number, out in enumerate(outs):
        total = None
        for j, weight in enumerate(weights):
            term = jnp.dot(
                chunk[sources_ref[out_number], :, j * width : (j + 1) * width],
                weight[...],
                preferred_element_type=jnp.float32,
            )
            total = term if total is None else total + term
        out[...] = total


def far_project(sources, chunk, weights):
    count, tokens, _ = chunk.shape
    keys = weights[0].shape[1]
    return pl.pallas_call(
        far_project_kernel,
        in_specs=[SMEM] + [VMEM] * (1 + len(weights)),
        out_specs=[VMEM] * count,
        out_shape=[jax.ShapeDtypeStruct((tokens, keys), jnp.float32)] * count,
        name="far_project",
        **call_options(HEAVY, VMEM_LIMIT // 3),
    )(sources, chunk, *weights)


def near_gradient_kernel(factor, width, skip, sources_ref, cots, *refs):
    rows, outs = refs[:NX], refs[NX:]
    keys, all_tokens = cots.shape
    tokens = all_tokens // NX
    for j, out in enumerate(outs):
        span = slice((skip + j) * width, (skip + j + 1) * width)
        total = None
        for number, row in enumerate(rows):
            left = cots[:, pl.ds(pl.multiple_of(sources_ref[number] * tokens, 128), tokens)]
            term = jnp.dot(left, row[:, span], preferred_element_type=jnp.float32)
            total = term if total is None else total + term
        out[...] = (factor * total).astype(jnp.bfloat16)


def near_gradient(sources, cots, rows, width, factor, skip, count):
    keys = cots.shape[0]
    vmem = pl.BlockSpec(memory_space=pltpu.VMEM)
    return pl.pallas_call(
        functools.partial(near_gradient_kernel, factor, width, skip),
        in_specs=[pl.BlockSpec(memory_space=pltpu.SMEM)] + [vmem] * (1 + NX),
        out_specs=[vmem] * count,
        out_shape=[jax.ShapeDtypeStruct((keys, width), jnp.bfloat16)] * count,
        name="near_gradient",
        **call_options(HEAVY, VMEM_LIMIT // 3),
    )(sources, cots, *rows)


def near_project_kernel(factor, count, *refs):
    starts, rows, refs = refs[:count], refs[count : 2 * count], refs[2 * count :]
    weights, outs = refs[:-count], refs[-count:]
    width = weights[0].shape[0]
    for start, row, out in zip(starts, rows, outs):
        total = start[...]
        for j, weight in enumerate(weights):
            total = total + jnp.dot(
                row[:, j * width : (j + 1) * width],
                weight[...],
                preferred_element_type=jnp.float32,
            )
        out[...] = (factor * total).astype(out.dtype)


def near_project(starts, rows, weights, out_types, factor):
    count = len(rows)
    return pl.pallas_call(
        functools.partial(near_project_kernel, factor, count),
        in_specs=[VMEM] * (2 * count + len(weights)),
        out_specs=[VMEM] * count,
        out_shape=[jax.ShapeDtypeStruct(starts[0].shape, t) for t in out_types],
        name="near_project",
        **call_options(1, VMEM_LIMIT // 3),
    )(*starts, *rows, *weights)


def update_kernel(
    offset_ref, own, one, two, three, far, weight, first, second, fresh, merged_out, first_out, second_out
):
    summed = own[...].astype(jnp.float32)
    for other in (one, two, three, far):
        summed = summed + other[...].astype(jnp.float32)
    gradient = summed.T
    moment_one = beta_one * first[...] + (1.0 - beta_one) * gradient
    moment_two = beta_two * second[...] + (1.0 - beta_two) * gradient * gradient
    first_out[...] = moment_one
    second_out[...] = moment_two
    master = weight[...].astype(jnp.float32)
    stepped = master - inner_rate * (
        moment_one / (jnp.sqrt(moment_two) + adam_epsilon) + decay_rate * master
    )
    head = fresh.shape[1]
    for position in range(master.shape[1] // head):
        part = stepped[:, position * head : (position + 1) * head]
        blended = mix_weight * part + (1.0 - mix_weight) * fresh[...]
        merged_out[:, position * head : (position + 1) * head] = jnp.where(
            offset_ref[0] == position, blended, part
        ).astype(jnp.bfloat16)


def update(head_index, terms, weight, first, second, fresh):
    rows, keys = weight.shape
    head = fresh.shape[1]
    block = 128
    return pl.pallas_call(
        update_kernel,
        grid_spec=pltpu.PrefetchScalarGridSpec(
            num_scalar_prefetch=1,
            grid=(rows // block,),
            in_specs=[pl.BlockSpec((keys, block), lambda i, o: (0, i))] * 5
            + [pl.BlockSpec((block, keys), lambda i, o: (i, 0))] * 3
            + [pl.BlockSpec((block, head), lambda i, o: (i, 0))],
            out_specs=[pl.BlockSpec((block, keys), lambda i, o: (i, 0))] * 3,
        ),
        out_shape=[
            jax.ShapeDtypeStruct((rows, keys), jnp.bfloat16),
            jax.ShapeDtypeStruct((rows, keys), jnp.float32),
            jax.ShapeDtypeStruct((rows, keys), jnp.float32),
        ],
        name="update",
        **call_options(limit=VMEM_LIMIT // 4),
    )(head_index, *terms, weight, first, second, fresh)


def per_device(
    activations,
    norm_gain,
    key_cotangent,
    key_weight,
    adam_first,
    adam_second,
    outer_codes,
    outer_scales,
    global_fragment,
    outer_momentum,
    fragment_index,
):
    token_rows = activations[0]
    weight_shard = key_weight[0]
    features = token_rows.shape[1]
    factor = features ** (-0.5)
    width = weight_shard.shape[0]
    replicas = lax.axis_size("replica")

    def swap_x(value):
        return lax.all_to_all(value, "fsdp", 0, 0, axis_index_groups=along_x, tiled=True)

    def add_replica(value, step):
        return value + lax.ppermute(value, "replica", [(r, r ^ step) for r in range(replicas)])

    me = lax.axis_index("fsdp")
    my_y, my_x, my_z = me // (NX * NZ), (me // NZ) % NX, me % NZ

    along_y = [[place(y, x, z) for y in range(NY)] for x in range(NX) for z in range(NZ)]
    along_x = [[place(y, x, z) for x in range(NX)] for y in range(NY) for z in range(NZ)]

    def swap_x(value):
        return lax.all_to_all(value, "fsdp", 0, 0, axis_index_groups=along_x, tiled=True)

    def swap_x(value):
        return lax.all_to_all(value, "fsdp", 0, 0, axis_index_groups=along_x, tiled=True)

    gain = norm_gain.reshape(-1, 128)
    cot = key_cotangent[0]
    keys = cot.shape[1]
    sources = jnp.stack([(my_x - d) % NX for d in range(NX)]).astype(jnp.int32)
    targets = jnp.stack([(my_y + e) % NY for e in range(NY)]).astype(jnp.int32)

    blocks = [(e, 1) for e in range(NY)]
    (part_one,) = normalize(token_rows, gain, cot, blocks, False, width, keys)
    chunk_one = swap_x(part_one)

    near_weights = [weight_shard] + [shift(weight_shard, -e, 0, 0) for e in range(1, NY)]
    far_weight = shift(weight_shard, 0, 0, 1)
    delta = outer_codes[0].astype(jnp.float32) * outer_scales[0].astype(jnp.float32)[:, None]
    delta = add_replica(delta, 1)

    token_rows, far_weight, delta, near_weights = lax.optimization_barrier(
        (token_rows, far_weight, delta, near_weights)
    )
    blocks = [(1, 0), (2, 0), (3, 0), (0, 0)]
    part_two = normalize(token_rows, gain, cot, blocks, True, width, 0)
    far_weights = [far_weight] + [shift(far_weight, -e, 0, 0) for e in range(1, NY)]
    delta = add_replica(add_replica(delta, 2), 4)
    chunk_two = [part_two[0]] + [shift(part_two[d], 0, d, 0) for d in range(1, NX)]
    chunk_one, part_two, far_weights, delta = lax.optimization_barrier(
        (chunk_one, part_two, far_weights, delta)
    )

    far, cots = far_gradient(targets, chunk_one, keys, width, factor)
    far = lax.all_to_all(far, "fsdp", 0, 0, axis_index_groups=along_y, tiled=True)
    partial = far_project(sources, chunk_one, far_weights)
    far = add_up(far)
    cots, far, partial = lax.optimization_barrier((cots, far, partial))
    far = shift(far, 0, 0, 1)
    second = near_gradient(sources, cots, chunk_two, width, factor, 0, 3)
    near = [shift(second[e - 1], e, 0, 0) for e in range(1, NY)]

    weights = near_weights[1:] + [weight_shard]
    (back_two,) = near_project([partial[2]], [chunk_two[2]], weights, [jnp.bfloat16], factor)
    back_two = shift(back_two, 0, -2, 0)
    rest, _ = lax.optimization_barrier(([partial[d] for d in (0, 1, 3)], second))
    own_part, back_one, back_three = near_project(
        rest,
        [chunk_two[d] for d in (0, 1, 3)],
        weights,
        [jnp.float32, jnp.bfloat16, jnp.bfloat16],
        factor,
    )
    cots, far, own_part, _ = lax.optimization_barrier((cots, far, own_part, back_one))
    (own,) = near_gradient(sources, cots, chunk_two, width, factor, 3, 1)
    terms = [own] + near + [far]
    back = [back_two, shift(back_one, 0, -1, 0), shift(back_three, 0, -3, 0)]
    projected = (own_part + sum(b.astype(jnp.float32) for b in back)).astype(jnp.bfloat16)

    outer_delta = delta / replicas
    momentum = outer_beta * outer_momentum + outer_delta
    refreshed = global_fragment - outer_rate * (outer_delta + outer_beta * momentum)

    heads = weight_shard.shape[1] // global_fragment.shape[1]
    head_index = jnp.remainder(fragment_index, heads).astype(jnp.int32)
    merged, moment_one, moment_two = update(
        head_index,
        terms,
        weight_shard,
        adam_first[0],
        adam_second[0],
        refreshed,
    )
    return (
        projected[None],
        merged[None],
        moment_one[None],
        moment_two[None],
        momentum,
        refreshed,
    )


def solution(mesh):
    in_specs = (
        P("replica", "fsdp", None),
        P(),
        P("replica", "fsdp", None),
        P("replica", "fsdp", None),
        P("replica", "fsdp", None),
        P("replica", "fsdp", None),
        P("replica", "fsdp", None),
        P("replica", "fsdp"),
        P("fsdp", None),
        P("fsdp", None),
        P(),
    )
    out_specs = (
        P("replica", "fsdp", None),
        P("replica", "fsdp", None),
        P("replica", "fsdp", None),
        P("replica", "fsdp", None),
        P("fsdp", None),
        P("fsdp", None),
    )
    return jax.shard_map(
        per_device, mesh=mesh, in_specs=in_specs, out_specs=out_specs, check_vma=False
    )
```

time: 151 us -> 140 us (0.927)
  the two profiles are of different devices: /device:TPU:32 before, /device:TPU:6 now
where the time goes in v3:
time: 140 us; the launch traced here: 139 us
  waiting for transfers between devices  51.6 us (37%)
  Pallas kernels  36.5 us (26%)
  starting transfers between devices  35.4 us (25%)
  local copies, waits for them, and re-layouts  10.9 us (8%)
  other arithmetic  2.69 us (2%)
  between operations  1.73 us (1%)
    ppermute x17, waiting for transfers between devices, shift(): return lax.ppermute(value, 'fsdp', pairs)  34.7 us
    ppermute x17, starting transfers between devices, shift(): return lax.ppermute(value, 'fsdp', pairs)  21.8 us
    pallas_call x2, Pallas kernels, normalize(): pl.pallas_call(functools.partial(norm_kernel, width, blocks, relative, ex...  12.7 us
    unnamed x64, local copies, waits for them, and re-layouts  10.9 us
    all_to_all x1, waiting for transfers between devices, per_device(): lax.all_to_all(far, 'fsdp', 0, 0, axis_index_groups=along_y, tiled=True)  10.6 us
    all_to_all x1, starting transfers between devices, swap_x(): lax.all_to_all(value, 'fsdp', 0, 0, axis_index_groups=along_x, tiled=True)  7.2 us
    ppermute x3, waiting for transfers between devices, add_replica(): lax.ppermute(value, 'replica', [(r, r ^ step) for r in range(replicas)])  6.23 us
    pallas_call x2, Pallas kernels, near_gradient(): pl.pallas_call(functools.partial(near_gradient_kernel, factor, width, ski...  5.77 us
  transfers between devices with their start and end apart: 22, of which 9 were waited for; matrix products, arithmetic and copies ran while one was open for 2% of the time, Pallas kernels for 20%

profile of v3, /device:TPU:6, one launch (start us, length us, event | category | flops | bytes accessed | tf_op | source)
XLA Modules:
  0.0 138.8 jit_solution(1695608405013988080)
XLA Ops:
  0.6 6.6 %norm.2 = bf16[4,256,2048]{2,1,0:T(8,128)(2,1)} custom-call(bf16[256,12288]{1,0:T(8,128)(2,1)} %bitcast.33, bf16[96,128]{1,0:T(8,128)(2,1)} %bitcast.37, bf16[256,512]{1,0:T(8,128)(2,1)} %bitcast.35), custom_call_target="tpu_custom_call" | custom-call | flops 1 | bytes 1 | tf_op jit(solution)/shard_map/norm/pallas_call | solution.py:137
  7.3 7.2 %all-to-all-start = ((bf16[4,256,2048]{2,1,0:T(8,128)(2,1)}), bf16[4,256,2048]{2,1,0:T(8,128)(2,1)}, u32[]{:S(2)}, u32[]{:S(2)}) async-start(bf16[4,256,2048]{2,1,0:T(8,128)(2,1)} %norm.2), calls=%async_computation | async-start | bytes 8388608 | tf_op jit(solution)/shard_map/all_to_all | solution.py:392
  14.7 5.5 %collective-permute-start = (bf16[384,512]{1,0:T(8,128)(2,1)S(1)}, bf16[384,512]{1,0:T(8,128)(2,1)S(1)}, u32[]{:S(2)}, u32[]{:S(2)}) collective-permute-start(bf16[384,512]{1,0:T(8,128)(2,1)S(1)} %bitcast.24), channel_id=1, source_target_pairs={{0,1},{1,0},{2,3},{3,2},{4,5},{5,4},{6,7},{7,6},{8,9},{9,8},{10,11... | collective-permute-start | bytes 1179656 | tf_op jit(solution)/shard_map/ppermute | solution.py:38
  20.3 3.0 %collective-permute-start.2 = (bf16[384,512]{1,0:T(8,128)(2,1)S(1)}, bf16[384,512]{1,0:T(8,128)(2,1)S(1)}, u32[]{:S(2)}, u32[]{:S(2)}) collective-permute-start(bf16[384,512]{1,0:T(8,128)(2,1)S(1)} %bitcast.25), channel_id=1, source_target_pairs={{0,24},{1,25},{2,26},{3,27},{4,28},{5,29},{6,30},{7,31},{8,0},{9,1... | collective-permute-start | bytes 1179656 | tf_op jit(solution)/shard_map/ppermute | solution.py:38
  25.0 7.5 %collective-permute-done.refs_0_ = bf16[384,512]{1,0:T(8,128)(2,1)S(1)} collective-permute-done((bf16[384,512]{1,0:T(8,128)(2,1)S(1)}, bf16[384,512]{1,0:T(8,128)(2,1)S(1)}, u32[]{:S(2)}, u32[]{:S(2)}) %collective-permute-start) | collective-permute-done | bytes 393248 | tf_op jit(solution)/shard_map/ppermute | solution.py:38
  32.5 7.9 %collective-permute-done.2.refs_6_.refs_2_ = bf16[384,512]{1,0:T(8,128)(2,1)S(1)} collective-permute-done((bf16[384,512]{1,0:T(8,128)(2,1)S(1)}, bf16[384,512]{1,0:T(8,128)(2,1)S(1)}, u32[]{:S(2)}, u32[]{:S(2)}) %collective-permute-start.2) | collective-permute-done | bytes 393248 | tf_op jit(solution)/shard_map/ppermute | solution.py:38
  41.9 2.2 %collective-permute-done.4.refs_8_.refs_4_ = bf16[384,512]{1,0:T(8,128)(2,1)S(1)} collective-permute-done((bf16[384,512]{1,0:T(8,128)(2,1)S(1)}, bf16[384,512]{1,0:T(8,128)(2,1)S(1)}, u32[]{:S(2)}, u32[]{:S(2)}) %collective-permute-start.4) | collective-permute-done | bytes 393248 | tf_op jit(solution)/shard_map/ppermute | solution.py:38
  49.0 2.8 %collective-permute-done.8 = f32[384,128]{1,0:T(8,128)S(1)} collective-permute-done((f32[384,128]{1,0:T(8,128)S(1)}, f32[384,128]{1,0:T(8,128)S(1)}, u32[]{:S(2)}, u32[]{:S(2)}) %collective-permute-start.8) | collective-permute-done | bytes 196640 | tf_op jit(solution)/shard_map/ppermute | solution.py:380
  53.5 6.1 %norm.3 = (bf16[256,1536]{1,0:T(8,128)(2,1)}, bf16[256,1536]{1,0:T(8,128)(2,1)}, bf16[256,1536]{1,0:T(8,128)(2,1)}, bf16[256,1536]{1,0:T(8,128)(2,1)}) custom-call(bf16[256,12288]{1,0:T(8,128)(2,1)} %bitcast.34, bf16[96,128]{1,0:T(8,128)(2,1)} %bitcast.38, bf16[256,512]{1,0:T(8,128)(2,1)} %bitcast.36), custom_call_target="tpu_custom_call" | custom-call | flops 1 | bytes 1 | tf_op jit(solution)/shard_map/norm/pallas_call | solution.py:137
  59.8 3.4 %collective-permute-done.9 = f32[384,128]{1,0:T(8,128)S(1)} collective-permute-done((f32[384,128]{1,0:T(8,128)S(1)}, f32[384,128]{1,0:T(8,128)S(1)}, u32[]{:S(2)}, u32[]{:S(2)}) %collective-permute-start.9) | collective-permute-done | bytes 196640 | tf_op jit(solution)/shard_map/ppermute | solution.py:380
  65.2 2.0 %collective-permute-done.7.refs_3_ = bf16[384,512]{1,0:T(8,128)(2,1)S(1)} collective-permute-done((bf16[384,512]{1,0:T(8,128)(2,1)S(1)}, bf16[384,512]{1,0:T(8,128)(2,1)S(1)}, u32[]{:S(2)}, u32[]{:S(2)}) %collective-permute-start.7) | collective-permute-done | bytes 393248 | tf_op jit(solution)/shard_map/ppermute | solution.py:38
  67.2 5.5 %far_gradient.1 = (bf16[4,512,384]{2,1,0:T(8,128)(2,1)}, bf16[512,1024]{1,0:T(8,128)(2,1)S(1)}) custom-call(s32[4]{0:T(128)S(1)} %pad_add_fusion.targets_ref, bf16[4,256,2048]{2,1,0:T(8,128)(2,1)} %all-to-all-done.chunk), custom_call_target="tpu_custom_call" | custom-call | flops 99999997952 | bytes 1 | tf_op jit(solution)/shard_map/far_gradient/pallas_call | solution.py:191
  73.7 3.7 %all-to-all-start.1 = ((bf16[4,512,384]{2,1,0:T(8,128)(2,1)}), bf16[4,512,384]{2,1,0:T(8,128)(2,1)S(1)}, u32[]{:S(2)}, u32[]{:S(2)}) async-start(bf16[4,512,384]{2,1,0:T(8,128)(2,1)} %get-tuple-element.58), calls=%async_computation.1 | async-start | bytes 3145728 | tf_op jit(solution)/shard_map/all_to_all | solution.py:422
  81.4 4.6 %far_project.1 = (f32[256,512]{1,0:T(8,128)S(1)}, f32[256,512]{1,0:T(8,128)S(1)}, f32[256,512]{1,0:T(8,128)S(1)}, f32[256,512]{1,0:T(8,128)S(1)}) custom-call(s32[4]{0:T(128)S(1)} %pad_add_fusion.1.sources_ref, bf16[4,256,2048]{2,1,0:T(8,128)(2,1)} %all-to-all-done.chunk, bf16[384,512]{1,0:T(8,128)(2,1)S(1)} %copy-done.17, bf16[384,512]{1,0:T(8,128)(2,1)S(1)} %copy-done.19, ...), custom_call_target="tpu_custom_call" | custom-call | flops 99999997952 | bytes 1 | tf_op jit(solution)/shard_map/far_project/pallas_call | solution.py:244
  87.8 10.6 %all-to-all-done.1.terms = bf16[4,512,384]{2,1,0:T(8,128)(2,1)S(1)} async-done(((bf16[4,512,384]{2,1,0:T(8,128)(2,1)}), bf16[4,512,384]{2,1,0:T(8,128)(2,1)S(1)}, u32[]{:S(2)}, u32[]{:S(2)}) %all-to-all-start.1) | async-done | bytes 1572896 | tf_op jit(solution)/shard_map/all_to_all | solution.py:422
  98.7 3.4 %collective-permute-start.10 = (bf16[512,384]{1,0:T(8,128)(2,1)S(1)}, bf16[512,384]{1,0:T(8,128)(2,1)S(1)}, u32[]{:S(2)}, u32[]{:S(2)}) collective-permute-start(bf16[512,384]{1,0:T(8,128)(2,1)S(1)} %add_up.1), channel_id=1, source_target_pairs={{0,1},{1,0},{2,3},{3,2},{4,5},{5,4},{6,7},{7,6},{8,9},{9,8},{10,11... | collective-permute-start | bytes 1179656 | tf_op jit(solution)/shard_map/ppermute | solution.py:38
  103.3 3.4 %near_gradient.2 = (bf16[512,384]{1,0:T(8,128)(2,1)S(1)}, bf16[512,384]{1,0:T(8,128)(2,1)S(1)}, bf16[512,384]{1,0:T(8,128)(2,1)S(1)}) custom-call(s32[4]{0:T(128)S(1)} %pad_add_fusion.1.sources_ref, bf16[512,1024]{1,0:T(8,128)(2,1)S(1)} %copy-done.25, bf16[256,1536]{1,0:T(8,128)(2,1)S(1)} %copy-done.11, ...), custom_call_target="tpu_custom_call" | custom-call | flops 99999997952 | bytes 1 | tf_op jit(solution)/shard_map/near_gradient/pallas_call | solution.py:271
  106.8 3.3 %near_project.2 = (f32[256,512]{1,0:T(8,128)S(1)}, bf16[256,512]{1,0:T(8,128)(2,1)S(1)}, bf16[256,512]{1,0:T(8,128)(2,1)S(1)}) custom-call(f32[256,512]{1,0:T(8,128)S(1)} %get-tuple-element.75.refs_0_, f32[256,512]{1,0:T(8,128)S(1)} %copy-done.13, f32[256,512]{1,0:T(8,128)S(1)} %copy-done.15, bf16[256,1536]{1,0:T(8,128)(2,1)S(1)} %copy-done.11, ...), custom_call_target="tpu_custom_call" | custom-call | flops 1 | bytes 1 | tf_op jit(solution)/shard_map/near_project/pallas_call | solution.py:298
  112.3 2.1 %collective-permute-start.18 = (bf16[512,384]{1,0:T(8,128)(2,1)S(1)}, bf16[512,384]{1,0:T(8,128)(2,1)S(1)}, u32[]{:S(2)}, u32[]{:S(2)}) collective-permute-start(bf16[512,384]{1,0:T(8,128)(2,1)S(1)} %get-tuple-element.73), channel_id=1, source_target_pairs={{0,16},{1,17},{2,18},{3,19},{4,20},{5,21},{6,22},{7,23},{8,24},{9,... | collective-permute-start | bytes 1179656 | tf_op jit(solution)/shard_map/ppermute | solution.py:38
  115.0 1.8 %near_project.3 = bf16[256,512]{1,0:T(8,128)(2,1)S(1)} custom-call(f32[256,512]{1,0:T(8,128)S(1)} %get-tuple-element.84.refs_0_, bf16[256,1536]{1,0:T(8,128)(2,1)} %collective-permute-done.12.refs_2_.refs_1_, bf16[384,512]{1,0:T(8,128)(2,1)S(1)} %copy-done.3, bf16[384,512]{1,0:T(8,128)(2,1)S(1)} %copy-done.5, bf16[384,512]{1,0:T(8,128)(2,1)S(1)} %copy-done.7, ...), custom_call_target="tpu_custom_call" | custom-call | flops 1 | bytes 1 | tf_op jit(solution)/shard_map/near_project/pallas_call | solution.py:298
  116.8 4.7 %collective-permute-done.10.far = bf16[512,384]{1,0:T(8,128)(2,1)S(1)} collective-permute-done((bf16[512,384]{1,0:T(8,128)(2,1)S(1)}, bf16[512,384]{1,0:T(8,128)(2,1)S(1)}, u32[]{:S(2)}, u32[]{:S(2)}) %collective-permute-start.10) | collective-permute-done | bytes 393248 | tf_op jit(solution)/shard_map/ppermute | solution.py:38
  122.6 2.4 %near_gradient.3.own = bf16[512,384]{1,0:T(8,128)(2,1)S(1)} custom-call(s32[4]{0:T(128)S(1)} %pad_add_fusion.1.sources_ref, bf16[512,1024]{1,0:T(8,128)(2,1)S(1)} %copy-done.26, bf16[256,1536]{1,0:T(8,128)(2,1)S(1)} %copy-done.11, bf16[256,1536]{1,0:T(8,128)(2,1)} %collective-permute-done.11.refs_1_.refs_4_, ...), custom_call_target="tpu_custom_call" | custom-call | flops 99999997952 | bytes 1 | tf_op jit(solution)/shard_map/near_gradient/pallas_call | solution.py:271
  125.0 10.4 %collective-permute-done.15 = bf16[256,512]{1,0:T(8,128)(2,1)S(1)} collective-permute-done((bf16[256,512]{1,0:T(8,128)(2,1)S(1)}, bf16[256,512]{1,0:T(8,128)(2,1)S(1)}, u32[]{:S(2)}, u32[]{:S(2)}) %collective-permute-start.15) | collective-permute-done | bytes 262176 | tf_op jit(solution)/shard_map/ppermute | solution.py:38
  136.2 2.6 %update.1 = (bf16[384,512]{1,0:T(8,128)(2,1)}, f32[384,512]{1,0:T(8,128)}, f32[384,512]{1,0:T(8,128)}) custom-call(s32[1]{0:T(128)S(6)} %select_n.63.offset_ref, bf16[512,384]{1,0:T(8,128)(2,1)S(1)} %near_gradient.3.own, bf16[512,384]{1,0:T(8,128)(2,1)S(1)} %collective-permute-done.17.one, bf16[512,384]{1,0:T(8,128)(2,1)S(1)} %collective-permute-done.18.two, ...), custom_call_target="tpu_custom_call" | custom-call | flops 1 | bytes 1 | tf_op jit(solution)/shard_map/update/pallas_call | solution.py:336
  (103 shorter events, 24.3 us)
Async XLA Ops:
  7.3 59.9 %all-to-all-start = ((bf16[4,256,2048]{2,1,0:T(8,128)(2,1)}), bf16[4,256,2048]{2,1,0:T(8,128)(2,1)}, u32[]{:S(2)}, u32[]{:S(2)}) async-start(bf16[4,256,2048]{2,1,0:T(8,128)(2,1)} %norm.2), calls=%async_computation | async-start | bytes 8388608 | tf_op jit(solution)/shard_map/all_to_all | solution.py:392
  14.6 10.3 %collective-permute-start.1 = (f32[384,128]{1,0:T(8,128)S(1)}, f32[384,128]{1,0:T(8,128)S(1)}, u32[]{:S(2)}, u32[]{:S(2)}) collective-permute-start(f32[384,128]{1,0:T(8,128)S(1)} %convert_multiply_fusion), channel_id=1, source_target_pairs={{0,32},{32,0},{64,96},{96,64},{128,160},{160,128},{192,224},{224,1... | collective-permute-start | bytes 589832 | tf_op jit(solution)/shard_map/ppermute | solution.py:380
  14.7 17.8 %collective-permute-start = (bf16[384,512]{1,0:T(8,128)(2,1)S(1)}, bf16[384,512]{1,0:T(8,128)(2,1)S(1)}, u32[]{:S(2)}, u32[]{:S(2)}) collective-permute-start(bf16[384,512]{1,0:T(8,128)(2,1)S(1)} %bitcast.24), channel_id=1, source_target_pairs={{0,1},{1,0},{2,3},{3,2},{4,5},{5,4},{6,7},{7,6},{8,9},{9,8},{10,11... | collective-permute-start | bytes 1179656 | tf_op jit(solution)/shard_map/ppermute | solution.py:38
  20.3 20.1 %collective-permute-start.2 = (bf16[384,512]{1,0:T(8,128)(2,1)S(1)}, bf16[384,512]{1,0:T(8,128)(2,1)S(1)}, u32[]{:S(2)}, u32[]{:S(2)}) collective-permute-start(bf16[384,512]{1,0:T(8,128)(2,1)S(1)} %bitcast.25), channel_id=1, source_target_pairs={{0,24},{1,25},{2,26},{3,27},{4,28},{5,29},{6,30},{7,31},{8,0},{9,1... | collective-permute-start | bytes 1179656 | tf_op jit(solution)/shard_map/ppermute | solution.py:38
  23.3 17.9 %collective-permute-start.3 = (bf16[384,512]{1,0:T(8,128)(2,1)S(1)}, bf16[384,512]{1,0:T(8,128)(2,1)S(1)}, u32[]{:S(2)}, u32[]{:S(2)}) collective-permute-start(bf16[384,512]{1,0:T(8,128)(2,1)S(1)} %bitcast.26), channel_id=1, source_target_pairs={{0,16},{1,17},{2,18},{3,19},{4,20},{5,21},{6,22},{7,23},{8,24},{9,... | collective-permute-start | bytes 1179656 | tf_op jit(solution)/shard_map/ppermute | solution.py:38
  23.9 20.2 %collective-permute-start.4 = (bf16[384,512]{1,0:T(8,128)(2,1)S(1)}, bf16[384,512]{1,0:T(8,128)(2,1)S(1)}, u32[]{:S(2)}, u32[]{:S(2)}) collective-permute-start(bf16[384,512]{1,0:T(8,128)(2,1)S(1)} %bitcast.27), channel_id=1, source_target_pairs={{0,8},{1,9},{2,10},{3,11},{4,12},{5,13},{6,14},{7,15},{8,16},{9,17... | collective-permute-start | bytes 1179656 | tf_op jit(solution)/shard_map/ppermute | solution.py:38
  44.8 6.9 %collective-permute-start.8 = (f32[384,128]{1,0:T(8,128)S(1)}, f32[384,128]{1,0:T(8,128)S(1)}, u32[]{:S(2)}, u32[]{:S(2)}) collective-permute-start(f32[384,128]{1,0:T(8,128)S(1)} %fusion.1), channel_id=1, source_target_pairs={{0,64},{32,96},{64,0},{96,32},{128,192},{160,224},{192,128},{224,1... | collective-permute-start | bytes 589832 | tf_op jit(solution)/shard_map/ppermute | solution.py:380
  45.9 19.3 %collective-permute-start.5 = (bf16[384,512]{1,0:T(8,128)(2,1)S(1)}, bf16[384,512]{1,0:T(8,128)(2,1)S(1)}, u32[]{:S(2)}, u32[]{:S(2)}) collective-permute-start(bf16[384,512]{1,0:T(8,128)(2,1)S(1)} %collective-permute-done.refs_0_), channel_id=1, source_target_pairs={{0,24},{1,25},{2,26},{3,27},{4,28},{5,29},{6,30},{7,31},{8,0},{9,1... | collective-permute-start | bytes 1179656 | tf_op jit(solution)/shard_map/ppermute | solution.py:38
  47.4 17.8 %collective-permute-start.6 = (bf16[384,512]{1,0:T(8,128)(2,1)S(1)}, bf16[384,512]{1,0:T(8,128)(2,1)S(1)}, u32[]{:S(2)}, u32[]{:S(2)}) collective-permute-start(bf16[384,512]{1,0:T(8,128)(2,1)S(1)} %collective-permute-done.refs_0_), channel_id=1, source_target_pairs={{0,16},{1,17},{2,18},{3,19},{4,20},{5,21},{6,22},{7,23},{8,24},{9,... | collective-permute-start | bytes 1179656 | tf_op jit(solution)/shard_map/ppermute | solution.py:38
  47.4 19.8 %collective-permute-start.7 = (bf16[384,512]{1,0:T(8,128)(2,1)S(1)}, bf16[384,512]{1,0:T(8,128)(2,1)S(1)}, u32[]{:S(2)}, u32[]{:S(2)}) collective-permute-start(bf16[384,512]{1,0:T(8,128)(2,1)S(1)} %collective-permute-done.refs_0_), channel_id=1, source_target_pairs={{0,8},{1,9},{2,10},{3,11},{4,12},{5,13},{6,14},{7,15},{8,16},{9,17... | collective-permute-start | bytes 1179656 | tf_op jit(solution)/shard_map/ppermute | solution.py:38
  51.8 11.4 %collective-permute-start.9 = (f32[384,128]{1,0:T(8,128)S(1)}, f32[384,128]{1,0:T(8,128)S(1)}, u32[]{:S(2)}, u32[]{:S(2)}) collective-permute-start(f32[384,128]{1,0:T(8,128)S(1)} %add.80), channel_id=1, source_target_pairs={{0,128},{32,160},{64,192},{96,224},{128,0},{160,32},{192,64},{224,... | collective-permute-start | bytes 589832 | tf_op jit(solution)/shard_map/ppermute | solution.py:380
  59.6 42.4 %collective-permute-start.11 = (bf16[256,1536]{1,0:T(8,128)(2,1)}, bf16[256,1536]{1,0:T(8,128)(2,1)}, u32[]{:S(2)}, u32[]{:S(2)}) collective-permute-start(bf16[256,1536]{1,0:T(8,128)(2,1)} %get-tuple-element.51), channel_id=1, source_target_pairs={{0,2},{1,3},{2,4},{3,5},{4,6},{5,7},{6,0},{7,1},{8,10},{9,11},{10,... | collective-permute-start | bytes 2359304 | tf_op jit(solution)/shard_map/ppermute | solution.py:38
  63.2 38.9 %collective-permute-start.12 = (bf16[256,1536]{1,0:T(8,128)(2,1)}, bf16[256,1536]{1,0:T(8,128)(2,1)}, u32[]{:S(2)}, u32[]{:S(2)}) collective-permute-start(bf16[256,1536]{1,0:T(8,128)(2,1)} %get-tuple-element.52), channel_id=1, source_target_pairs={{0,4},{1,5},{2,6},{3,7},{4,0},{5,1},{6,2},{7,3},{8,12},{9,13},{10,... | collective-permute-start | bytes 2359304 | tf_op jit(solution)/shard_map/ppermute | solution.py:38
  65.1 36.9 %collective-permute-start.13 = (bf16[256,1536]{1,0:T(8,128)(2,1)}, bf16[256,1536]{1,0:T(8,128)(2,1)}, u32[]{:S(2)}, u32[]{:S(2)}) collective-permute-start(bf16[256,1536]{1,0:T(8,128)(2,1)} %get-tuple-element.53), channel_id=1, source_target_pairs={{0,6},{1,7},{2,0},{3,1},{4,2},{5,3},{6,4},{7,5},{8,14},{9,15},{10,... | collective-permute-start | bytes 2359304 | tf_op jit(solution)/shard_map/ppermute | solution.py:38
  73.7 24.7 %all-to-all-start.1 = ((bf16[4,512,384]{2,1,0:T(8,128)(2,1)}), bf16[4,512,384]{2,1,0:T(8,128)(2,1)S(1)}, u32[]{:S(2)}, u32[]{:S(2)}) async-start(bf16[4,512,384]{2,1,0:T(8,128)(2,1)} %get-tuple-element.58), calls=%async_computation.1 | async-start | bytes 3145728 | tf_op jit(solution)/shard_map/all_to_all | solution.py:422
  81.4 20.6 %copy-start.11 = (bf16[256,1536]{1,0:T(8,128)(2,1)S(1)}, bf16[256,1536]{1,0:T(8,128)(2,1)}, u32[]{:S(2)}) copy-start(bf16[256,1536]{1,0:T(8,128)(2,1)} %get-tuple-element.50.refs_0_.refs_3_) | copy-start | bytes 2359300
  98.7 22.8 %collective-permute-start.10 = (bf16[512,384]{1,0:T(8,128)(2,1)S(1)}, bf16[512,384]{1,0:T(8,128)(2,1)S(1)}, u32[]{:S(2)}, u32[]{:S(2)}) collective-permute-start(bf16[512,384]{1,0:T(8,128)(2,1)S(1)} %add_up.1), channel_id=1, source_target_pairs={{0,1},{1,0},{2,3},{3,2},{4,5},{5,4},{6,7},{7,6},{8,9},{9,8},{10,11... | collective-permute-start | bytes 1179656 | tf_op jit(solution)/shard_map/ppermute | solution.py:38
  110.2 12.0 %collective-permute-start.16 = (bf16[256,512]{1,0:T(8,128)(2,1)S(1)}, bf16[256,512]{1,0:T(8,128)(2,1)S(1)}, u32[]{:S(2)}, u32[]{:S(2)}) collective-permute-start(bf16[256,512]{1,0:T(8,128)(2,1)S(1)} %get-tuple-element.85), channel_id=1, source_target_pairs={{0,2},{1,3},{2,4},{3,5},{4,6},{5,7},{6,0},{7,1},{8,10},{9,11},{10,... | collective-permute-start | bytes 786440 | tf_op jit(solution)/shard_map/ppermute | solution.py:38
  111.7 24.5 %copy-start.8 = (f32[384,128]{1,0:T(8,128)}, f32[384,128]{1,0:T(8,128)S(1)}, u32[]{:S(2)}) copy-start(f32[384,128]{1,0:T(8,128)S(1)} %get-tuple-element.92.fresh) | copy-start | bytes 589828
  111.7 24.5 %collective-permute-start.17 = (bf16[512,384]{1,0:T(8,128)(2,1)S(1)}, bf16[512,384]{1,0:T(8,128)(2,1)S(1)}, u32[]{:S(2)}, u32[]{:S(2)}) collective-permute-start(bf16[512,384]{1,0:T(8,128)(2,1)S(1)} %get-tuple-element.72), channel_id=1, source_target_pairs={{0,8},{1,9},{2,10},{3,11},{4,12},{5,13},{6,14},{7,15},{8,16},{9,17... | collective-permute-start | bytes 1179656 | tf_op jit(solution)/shard_map/ppermute | solution.py:38
  112.3 23.9 %collective-permute-start.18 = (bf16[512,384]{1,0:T(8,128)(2,1)S(1)}, bf16[512,384]{1,0:T(8,128)(2,1)S(1)}, u32[]{:S(2)}, u32[]{:S(2)}) collective-permute-start(bf16[512,384]{1,0:T(8,128)(2,1)S(1)} %get-tuple-element.73), channel_id=1, source_target_pairs={{0,16},{1,17},{2,18},{3,19},{4,20},{5,21},{6,22},{7,23},{8,24},{9,... | collective-permute-start | bytes 1179656 | tf_op jit(solution)/shard_map/ppermute | solution.py:38
  114.4 21.8 %collective-permute-start.19 = (bf16[512,384]{1,0:T(8,128)(2,1)S(1)}, bf16[512,384]{1,0:T(8,128)(2,1)S(1)}, u32[]{:S(2)}, u32[]{:S(2)}) collective-permute-start(bf16[512,384]{1,0:T(8,128)(2,1)S(1)} %get-tuple-element.74), channel_id=1, source_target_pairs={{0,24},{1,25},{2,26},{3,27},{4,28},{5,29},{6,30},{7,31},{8,0},{9,1... | collective-permute-start | bytes 1179656 | tf_op jit(solution)/shard_map/ppermute | solution.py:38
  121.5 13.9 %collective-permute-start.15 = (bf16[256,512]{1,0:T(8,128)(2,1)S(1)}, bf16[256,512]{1,0:T(8,128)(2,1)S(1)}, u32[]{:S(2)}, u32[]{:S(2)}) collective-permute-start(bf16[256,512]{1,0:T(8,128)(2,1)S(1)} %get-tuple-element.82), channel_id=1, source_target_pairs={{0,6},{1,7},{2,0},{3,1},{4,2},{5,3},{6,4},{7,5},{8,14},{9,15},{10,... | collective-permute-start | bytes 786440 | tf_op jit(solution)/shard_map/ppermute | solution.py:38
  122.2 13.2 %collective-permute-start.14 = (bf16[256,512]{1,0:T(8,128)(2,1)S(1)}, bf16[256,512]{1,0:T(8,128)(2,1)S(1)}, u32[]{:S(2)}, u32[]{:S(2)}) collective-permute-start(bf16[256,512]{1,0:T(8,128)(2,1)S(1)} %near_project.3), channel_id=1, source_target_pairs={{0,4},{1,5},{2,6},{3,7},{4,0},{5,1},{6,2},{7,3},{8,12},{9,13},{10,... | collective-permute-start | bytes 786440 | tf_op jit(solution)/shard_map/ppermute | solution.py:38
  (30 other events, 159.0 us)

commit v4 on v3

--- a/solution.py
+++ b/solution.py
@@ -49,10 +49,10 @@
     )
 
 
-def norm_kernel(width, blocks, relative, extra, rows_hbm, gain_ref, cot_hbm, *refs):
+def norm_kernel(width, groups, relative, extra, rows_hbm, gain_ref, cot_hbm, *refs):
     outs, (held, ready, cot, gains, came, gone, cot_came, cot_gone) = refs[:-8], refs[-8:]
     tokens, features = held.shape
-    depth = width * len(blocks)
+    blocks = [block for group in groups for block in group]
     lanes = 128
     bands = tokens // ROWS
     me = lax.axis_index("fsdp")
@@ -62,13 +62,20 @@
         rows = pl.ds(pl.multiple_of(band * ROWS, ROWS), ROWS)
         return pltpu.make_async_copy(rows_hbm.at[rows], held.at[rows], came.at[band])
 
-    def store(band, x):
+    def stores(band, x):
         rows = pl.ds(pl.multiple_of(band * ROWS, ROWS), ROWS)
-        if len(outs) == 1:
-            target = outs[0].at[x, rows, pl.ds(0, depth)]
-        else:
-            target = outs[x].at[rows]
-        return pltpu.make_async_copy(ready.at[x, rows], target, gone.at[band, x])
+        low, copies = 0, []
+        for number, group in enumerate(groups):
+            span = pl.ds(low, width * len(group))
+            if relative:
+                target = outs[number * NX + x].at[rows]
+            else:
+                target = outs[number].at[x, rows, span]
+            copies.append(
+                pltpu.make_async_copy(ready.at[x, rows, span], target, gone.at[band, x, number])
+            )
+            low += width * len(group)
+        return copies
 
     for band in range(AHEAD):
         fetch(band).start()
@@ -77,7 +84,7 @@
         cot_fetch = pltpu.make_async_copy(cot_hbm, cot, cot_came)
         cot_fetch.start()
         cot_copies = [
-            pltpu.make_async_copy(cot, outs[0].at[x, :, pl.ds(depth, extra)], cot_gone.at[x])
+            pltpu.make_async_copy(cot, outs[0].at[x, :, pl.ds(width * len(blocks), extra)], cot_gone.at[x])
             for x in range(NX)
         ]
     gains[...] = gain_ref[...].astype(jnp.float32)
@@ -113,7 +120,8 @@
                     gain = gains[pl.ds(tile, 1), :]
                     low = position * width + k * lanes
                     ready[x, rows, low : low + lanes] = (part * scale * gain).astype(jnp.bfloat16)
-            store(band, x).start()
+            for copy in stores(band, x):
+                copy.start()
 
     if extra:
         cot_fetch.wait()
@@ -123,19 +131,22 @@
             copy.wait()
     for band in range(bands):
         for x in range(NX):
-            store(band, x).wait()
-
-
-def normalize(token_rows, gain, cot, blocks, relative, width, extra):
+            for copy in stores(band, x):
+                copy.wait()
+
+
+def normalize(token_rows, gain, cot, groups, relative, width, extra):
     tokens, features = token_rows.shape
-    depth = width * len(blocks)
+    depths = [width * len(group) for group in groups]
     bands = tokens // ROWS
-    if extra:
-        out_shape = [jax.ShapeDtypeStruct((NX, tokens, depth + extra), jnp.bfloat16)]
+    if relative:
+        out_shape = [
+            jax.ShapeDtypeStruct((tokens, depth), jnp.bfloat16) for depth in depths for _ in range(NX)
+        ]
     else:
-        out_shape = [jax.ShapeDtypeStruct((tokens, depth), jnp.bfloat16)] * NX
+        out_shape = [jax.ShapeDtypeStruct((NX, tokens, depths[0] + extra), jnp.bfloat16)]
     return pl.pallas_call(
-        functools.partial(norm_kernel, width, blocks, relative, extra),
+        functools.partial(norm_kernel, width, groups, relative, extra),
         in_specs=[
             pl.BlockSpec(memory_space=pl.ANY),
             pl.BlockSpec(memory_space=pltpu.VMEM),
@@ -145,11 +156,11 @@
         out_shape=out_shape,
         scratch_shapes=[
             pltpu.VMEM((tokens, features), jnp.bfloat16),
-            pltpu.VMEM((NX, tokens, depth), jnp.bfloat16),
+            pltpu.VMEM((NX, tokens, sum(depths)), jnp.bfloat16),
             pltpu.VMEM(cot.shape, jnp.bfloat16),
             pltpu.VMEM(gain.shape, jnp.float32),
             pltpu.SemaphoreType.DMA((bands,)),
-            pltpu.SemaphoreType.DMA((bands, NX)),
+            pltpu.SemaphoreType.DMA((bands, NX, len(groups))),
             pltpu.SemaphoreType.DMA,
             pltpu.SemaphoreType.DMA((NX,)),
         ],
@@ -223,134 +234,233 @@
     )(terms)
 
 
+def fetch_weights(weights_hbm, weights, came):
+    width = weights.shape[0] // len(weights_hbm)
+    copies = [
+        pltpu.make_async_copy(weight, weights.at[pl.ds(j * width, width)], came.at[j])
+        for j, weight in enumerate(weights_hbm)
+    ]
+    for copy in copies:
+        copy.start()
+    return copies
+
+
 def far_project_kernel(sources_ref, chunk, *refs):
-    weights, outs = refs[:-NX], refs[-NX:]
-    width = weights[0].shape[0]
-    for out_number, out in enumerate(outs):
-        total = None
-        for j, weight in enumerate(weights):
-            term = jnp.dot(
-                chunk[sources_ref[out_number], :, j * width : (j + 1) * width],
-                weight[...],
-                preferred_element_type=jnp.float32,
-            )
-            total = term if total is None else total + term
-        out[...] = total
+    weights_hbm, (out, weights, came, ready, gone) = refs[:-5], refs[-5:]
+    for copy in fetch_weights(weights_hbm, weights, came):
+        copy.wait()
+    copies = []
+    for d in range(NX):
+        ready[d] = jnp.dot(
+            chunk[sources_ref[d], :, : weights.shape[0]],
+            weights[...],
+            preferred_element_type=jnp.float32,
+        )
+        copies.append(pltpu.make_async_copy(ready.at[d], out.at[d], gone.at[d]))
+        copies[d].start()
+    for copy in copies:
+        copy.wait()
 
 
 def far_project(sources, chunk, weights):
     count, tokens, _ = chunk.shape
-    keys = weights[0].shape[1]
+    width, keys = weights[0].shape
+    shape = (count, tokens, keys)
     return pl.pallas_call(
         far_project_kernel,
-        in_specs=[SMEM] + [VMEM] * (1 + len(weights)),
-        out_specs=[VMEM] * count,
-        out_shape=[jax.ShapeDtypeStruct((tokens, keys), jnp.float32)] * count,
+        in_specs=[SMEM, VMEM] + in_memory(len(weights)),
+        out_specs=pl.BlockSpec(memory_space=pl.ANY),
+        out_shape=jax.ShapeDtypeStruct(shape, jnp.float32),
+        scratch_shapes=[
+            pltpu.VMEM((width * len(weights), keys), jnp.bfloat16),
+            pltpu.SemaphoreType.DMA((len(weights),)),
+            pltpu.VMEM(shape, jnp.float32),
+            pltpu.SemaphoreType.DMA((count,)),
+        ],
         name="far_project",
         **call_options(HEAVY, VMEM_LIMIT // 3),
     )(sources, chunk, *weights)
 
 
-def near_gradient_kernel(factor, width, skip, sources_ref, cots, *refs):
-    rows, outs = refs[:NX], refs[NX:]
+def near_project_kernel(factor, pieces, start_hbm, *refs):
+    rows_hbm, own_hbm, refs = refs[:NX], refs[NX : 2 * NX], refs[2 * NX :]
+    weights_hbm, refs = refs[:pieces], refs[pieces:]
+    outs, (weights, came, start, rows, start_came, rows_came) = refs[:NX], refs[NX:]
+    depth = rows_hbm[0].shape[1]
+    own_depth = own_hbm[0].shape[1]
+    copies = fetch_weights(weights_hbm, weights, came)
+    fetches = []
+    for d in range(NX):
+        fetches.append(
+            [
+                pltpu.make_async_copy(
+                    rows_hbm[d], rows.at[d, :, pl.ds(0, depth)], rows_came.at[d, 0]
+                ),
+                pltpu.make_async_copy(
+                    own_hbm[d], rows.at[d, :, pl.ds(depth, own_depth)], rows_came.at[d, 1]
+                ),
+                pltpu.make_async_copy(start_hbm.at[d], start.at[d], start_came.at[d]),
+            ]
+        )
+        for copy in fetches[d]:
+            copy.start()
+    for copy in copies:
+        copy.wait()
+    for d in range(NX):
+        for copy in fetches[d]:
+            copy.wait()
+        total = start[d] + jnp.dot(rows[d], weights[...], preferred_element_type=jnp.float32)
+        outs[d][...] = (factor * total).astype(outs[d].dtype)
+
+
+def near_project(start, rows, own_rows, weights, out_types, factor):
+    width, keys = weights[0].shape
+    count, tokens, _ = start.shape
+    depth = width * len(weights)
+    return pl.pallas_call(
+        functools.partial(near_project_kernel, factor, len(weights)),
+        in_specs=in_memory(1 + 2 * NX + len(weights)),
+        out_specs=[VMEM] * NX,
+        out_shape=[jax.ShapeDtypeStruct((tokens, keys), t) for t in out_types],
+        scratch_shapes=[
+            pltpu.VMEM((depth, keys), jnp.bfloat16),
+            pltpu.SemaphoreType.DMA((len(weights),)),
+            pltpu.VMEM(start.shape, jnp.float32),
+            pltpu.VMEM((count, tokens, depth), jnp.bfloat16),
+            pltpu.SemaphoreType.DMA((count,)),
+            pltpu.SemaphoreType.DMA((count, 2)),
+        ],
+        name="near_project",
+        **call_options(HEAVY),
+    )(start, *rows, *own_rows, *weights)
+
+
+def near_gradient_kernel(factor, width, stacked, sources_ref, targets_ref, cots, *refs):
+    rows, refs = refs[:NX], refs[NX:]
+    out = refs[0]
     keys, all_tokens = cots.shape
     tokens = all_tokens // NX
-    for j, out in enumerate(outs):
-        span = slice((skip + j) * width, (skip + j + 1) * width)
+    copies = []
+    for j in range(rows[0].shape[1] // width):
         total = None
         for number, row in enumerate(rows):
             left = cots[:, pl.ds(pl.multiple_of(sources_ref[number] * tokens, 128), tokens)]
-            term = jnp.dot(left, row[:, span], preferred_element_type=jnp.float32)
+            term = jnp.dot(
+                left, row[:, j * width : (j + 1) * width], preferred_element_type=jnp.float32
+            )
             total = term if total is None else total + term
-        out[...] = (factor * total).astype(jnp.bfloat16)
-
-
-def near_gradient(sources, cots, rows, width, factor, skip, count):
+        total = (factor * total).astype(jnp.bfloat16)
+        if stacked:
+            ready, gone = refs[1:]
+            ready[j] = total
+            copies.append(
+                pltpu.make_async_copy(ready.at[j], out.at[targets_ref[j + 1]], gone.at[j])
+            )
+            copies[j].start()
+        else:
+            out[...] = total
+    if stacked:
+        ready[NY - 1] = jnp.zeros((keys, width), jnp.bfloat16)
+        copies.append(
+            pltpu.make_async_copy(ready.at[NY - 1], out.at[targets_ref[0]], gone.at[NY - 1])
+        )
+        copies[NY - 1].start()
+    for copy in copies:
+        copy.wait()
+
+
+def near_gradient(sources, targets, cots, rows, width, factor, stacked):
     keys = cots.shape[0]
-    vmem = pl.BlockSpec(memory_space=pltpu.VMEM)
+    shape = (NY, keys, width) if stacked else (keys, width)
+    scratch = [pltpu.VMEM(shape, jnp.bfloat16), pltpu.SemaphoreType.DMA((NY,))]
     return pl.pallas_call(
-        functools.partial(near_gradient_kernel, factor, width, skip),
-        in_specs=[pl.BlockSpec(memory_space=pltpu.SMEM)] + [vmem] * (1 + NX),
-        out_specs=[vmem] * count,
-        out_shape=[jax.ShapeDtypeStruct((keys, width), jnp.bfloat16)] * count,
+        functools.partial(near_gradient_kernel, factor, width, stacked),
+        in_specs=[SMEM, SMEM] + [VMEM] * (1 + NX),
+        out_specs=pl.BlockSpec(memory_space=pl.ANY) if stacked else VMEM,
+        out_shape=jax.ShapeDtypeStruct(shape, jnp.bfloat16),
+        scratch_shapes=scratch if stacked else [],
         name="near_gradient",
-        **call_options(HEAVY, VMEM_LIMIT // 3),
-    )(sources, cots, *rows)
-
-
-def near_project_kernel(factor, count, *refs):
-    starts, rows, refs = refs[:count], refs[count : 2 * count], refs[2 * count :]
-    weights, outs = refs[:-count], refs[-count:]
-    width = weights[0].shape[0]
-    for start, row, out in zip(starts, rows, outs):
-        total = start[...]
-        for j, weight in enumerate(weights):
-            total = total + jnp.dot(
-                row[:, j * width : (j + 1) * width],
-                weight[...],
-                preferred_element_type=jnp.float32,
-            )
-        out[...] = (factor * total).astype(out.dtype)
-
-
-def near_project(starts, rows, weights, out_types, factor):
-    count = len(rows)
-    return pl.pallas_call(
-        functools.partial(near_project_kernel, factor, count),
-        in_specs=[VMEM] * (2 * count + len(weights)),
-        out_specs=[VMEM] * count,
-        out_shape=[jax.ShapeDtypeStruct(starts[0].shape, t) for t in out_types],
-        name="near_project",
-        **call_options(1, VMEM_LIMIT // 3),
-    )(*starts, *rows, *weights)
-
-
-def update_kernel(
-    offset_ref, own, one, two, three, far, weight, first, second, fresh, merged_out, first_out, second_out
-):
-    summed = own[...].astype(jnp.float32)
-    for other in (one, two, three, far):
-        summed = summed + other[...].astype(jnp.float32)
-    gradient = summed.T
-    moment_one = beta_one * first[...] + (1.0 - beta_one) * gradient
-    moment_two = beta_two * second[...] + (1.0 - beta_two) * gradient * gradient
-    first_out[...] = moment_one
-    second_out[...] = moment_two
-    master = weight[...].astype(jnp.float32)
-    stepped = master - inner_rate * (
-        moment_one / (jnp.sqrt(moment_two) + adam_epsilon) + decay_rate * master
-    )
-    head = fresh.shape[1]
-    for position in range(master.shape[1] // head):
-        part = stepped[:, position * head : (position + 1) * head]
-        blended = mix_weight * part + (1.0 - mix_weight) * fresh[...]
-        merged_out[:, position * head : (position + 1) * head] = jnp.where(
-            offset_ref[0] == position, blended, part
-        ).astype(jnp.bfloat16)
-
-
-def update(head_index, terms, weight, first, second, fresh):
+        **call_options(HEAVY if stacked else 1, VMEM_LIMIT // 3),
+    )(sources, targets, cots, *rows)
+
+
+def update_kernel(offset_ref, *refs):
+    sums_hbm, ins, outs, refs = refs[:4], refs[4:7], refs[7:10], refs[10:]
+    weight, first, second, merged, first_new, second_new = refs[:6]
+    near, own, far, fresh, came, gone, sums_came = refs[6:]
     rows, keys = weight.shape
     head = fresh.shape[1]
     block = 128
+    sums = [
+        pltpu.make_async_copy(source, target, sums_came.at[n])
+        for n, (source, target) in enumerate(zip(sums_hbm, (near, own, far, fresh)))
+    ]
+    for copy in sums:
+        copy.start()
+    fetches, stores = [], []
+    for i in range(rows // block):
+        span = pl.ds(i * block, block)
+        fetches.append(
+            [
+                pltpu.make_async_copy(source.at[span], target.at[span], came.at[i, n])
+                for n, (source, target) in enumerate(zip(ins, (weight, first, second)))
+            ]
+        )
+        stores.append(
+            [
+                pltpu.make_async_copy(source.at[span], target.at[span], gone.at[i, n])
+                for n, (source, target) in enumerate(zip((merged, first_new, second_new), outs))
+            ]
+        )
+        for copy in fetches[i]:
+            copy.start()
+    for copy in sums:
+        copy.wait()
+    for i in range(rows // block):
+        low, high = i * block, (i + 1) * block
+        summed = own[:, low:high].astype(jnp.float32) + far[:, low:high].astype(jnp.float32)
+        for number in range(near.shape[0]):
+            summed = summed + near[number, :, low:high].astype(jnp.float32)
+        gradient = summed.T
+        for copy in fetches[i]:
+            copy.wait()
+        moment_one = beta_one * first[low:high, :] + (1.0 - beta_one) * gradient
+        moment_two = beta_two * second[low:high, :] + (1.0 - beta_two) * gradient * gradient
+        first_new[low:high, :] = moment_one
+        second_new[low:high, :] = moment_two
+        master = weight[low:high, :].astype(jnp.float32)
+        stepped = master - inner_rate * (
+            moment_one / (jnp.sqrt(moment_two) + adam_epsilon) + decay_rate * master
+        )
+        for position in range(keys // head):
+            span = slice(position * head, (position + 1) * head)
+            part = stepped[:, span]
+            blended = mix_weight * part + (1.0 - mix_weight) * fresh[low:high, :]
+            merged[low:high, span] = jnp.where(
+                offset_ref[0] == position, blended, part
+            ).astype(jnp.bfloat16)
+        for copy in stores[i]:
+            copy.start()
+    for copies in stores:
+        for copy in copies:
+            copy.wait()
+
+
+def update(head_index, terms, weight, first, second, fresh):
+    rows, keys = weight.shape
+    types = [jnp.bfloat16, jnp.float32, jnp.float32]
     return pl.pallas_call(
         update_kernel,
-        grid_spec=pltpu.PrefetchScalarGridSpec(
-            num_scalar_prefetch=1,
-            grid=(rows // block,),
-            in_specs=[pl.BlockSpec((keys, block), lambda i, o: (0, i))] * 5
-            + [pl.BlockSpec((block, keys), lambda i, o: (i, 0))] * 3
-            + [pl.BlockSpec((block, head), lambda i, o: (i, 0))],
-            out_specs=[pl.BlockSpec((block, keys), lambda i, o: (i, 0))] * 3,
-        ),
-        out_shape=[
-            jax.ShapeDtypeStruct((rows, keys), jnp.bfloat16),
-            jax.ShapeDtypeStruct((rows, keys), jnp.float32),
-            jax.ShapeDtypeStruct((rows, keys), jnp.float32),
-        ],
+        in_specs=[SMEM] + in_memory(7),
+        out_specs=in_memory(3),
+        out_shape=[jax.ShapeDtypeStruct((rows, keys), t) for t in types],
+        scratch_shapes=[pltpu.VMEM((rows, keys), t) for t in types + types]
+        + [pltpu.VMEM(term.shape, term.dtype) for term in (*terms, fresh)]
+        + [pltpu.SemaphoreType.DMA((rows // 128, 3))] * 2
+        + [pltpu.SemaphoreType.DMA((4,))],
         name="update",
-        **call_options(limit=VMEM_LIMIT // 4),
-    )(head_index, *terms, weight, first, second, fresh)
+        **call_options(),
+    )(head_index, *terms, fresh, weight, first, second)
 
 
 def per_device(
@@ -397,8 +507,8 @@
     sources = jnp.stack([(my_x - d) % NX for d in range(NX)]).astype(jnp.int32)
     targets = jnp.stack([(my_y + e) % NY for e in range(NY)]).astype(jnp.int32)
 
-    blocks = [(e, 1) for e in range(NY)]
-    (part_one,) = normalize(token_rows, gain, cot, blocks, False, width, keys)
+    groups = [[(e, 1) for e in range(NY)]]
+    (part_one,) = normalize(token_rows, gain, cot, groups, False, width, keys)
     chunk_one = swap_x(part_one)
 
     near_weights = [weight_shard] + [shift(weight_shard, -e, 0, 0) for e in range(1, NY)]
@@ -409,8 +519,9 @@
     token_rows, far_weight, delta, near_weights = lax.optimization_barrier(
         (token_rows, far_weight, delta, near_weights)
     )
-    blocks = [(1, 0), (2, 0), (3, 0), (0, 0)]
-    part_two = normalize(token_rows, gain, cot, blocks, True, width, 0)
+    groups = [[(e, 0) for e in range(1, NY)], [(0, 0)]]
+    part_two = normalize(token_rows, gain, cot, groups, True, width, 0)
+    part_two, part_own = part_two[:NX], part_two[NX:]
     far_weights = [far_weight] + [shift(far_weight, -e, 0, 0) for e in range(1, NY)]
     delta = add_replica(add_replica(delta, 2), 4)
     chunk_two = [part_two[0]] + [shift(part_two[d], 0, d, 0) for d in range(1, NX)]
@@ -421,28 +532,24 @@
     far, cots = far_gradient(targets, chunk_one, keys, width, factor)
     far = lax.all_to_all(far, "fsdp", 0, 0, axis_index_groups=along_y, tiled=True)
     partial = far_project(sources, chunk_one, far_weights)
-    far = add_up(far)
-    cots, far, partial = lax.optimization_barrier((cots, far, partial))
-    far = shift(far, 0, 0, 1)
-    second = near_gradient(sources, cots, chunk_two, width, factor, 0, 3)
-    near = [shift(second[e - 1], e, 0, 0) for e in range(1, NY)]
-
-    weights = near_weights[1:] + [weight_shard]
-    (back_two,) = near_project([partial[2]], [chunk_two[2]], weights, [jnp.bfloat16], factor)
-    back_two = shift(back_two, 0, -2, 0)
-    rest, _ = lax.optimization_barrier(([partial[d] for d in (0, 1, 3)], second))
-    own_part, back_one, back_three = near_project(
-        rest,
-        [chunk_two[d] for d in (0, 1, 3)],
-        weights,
-        [jnp.float32, jnp.bfloat16, jnp.bfloat16],
+    part_own, cots = lax.optimization_barrier((part_own, cots))
+    chunk_own = [part_own[0]] + [shift(part_own[d], 0, d, 0) for d in range(1, NX)]
+    near = near_gradient(sources, targets, cots, chunk_two, width, factor, True)
+    far, near, partial = lax.optimization_barrier((far, near, partial))
+    far = shift(add_up(far), 0, 0, 1)
+    near = lax.all_to_all(near, "fsdp", 0, 0, axis_index_groups=along_y, tiled=True)
+
+    own_part, *back = near_project(
+        partial,
+        chunk_two,
+        chunk_own,
+        near_weights[1:] + [weight_shard],
+        [jnp.float32] + [jnp.bfloat16] * (NX - 1),
         factor,
     )
-    cots, far, own_part, _ = lax.optimization_barrier((cots, far, own_part, back_one))
-    (own,) = near_gradient(sources, cots, chunk_two, width, factor, 3, 1)
-    terms = [own] + near + [far]
-    back = [back_two, shift(back_one, 0, -1, 0), shift(back_three, 0, -3, 0)]
-    projected = (own_part + sum(b.astype(jnp.float32) for b in back)).astype(jnp.bfloat16)
+    own = near_gradient(sources, targets, cots, chunk_own, width, factor, False)
+    terms = [near, own, far]
+    back = [shift(back[d - 1], 0, -d, 0) for d in range(1, NX)]
 
     outer_delta = delta / replicas
     momentum = outer_beta * outer_momentum + outer_delta
@@ -458,6 +565,8 @@
         adam_second[0],
         refreshed,
     )
+    own_part, moment_one = lax.optimization_barrier((own_part, moment_one))
+    projected = (own_part + sum(b.astype(jnp.float32) for b in back)).astype(jnp.bfloat16)
     return (
         projected[None],
         merged[None],

time: 140 us -> 134 us (0.957)
  the two profiles are of different devices: /device:TPU:6 before, /device:TPU:32 now
where the time goes in v4:
time: 134 us; the launch traced here: 132 us
  starting transfers between devices  46 us (34%)
  Pallas kernels  41.8 us (31%)
  waiting for transfers between devices  36 us (27%)
  local copies, waits for them, and re-layouts  3.75 us (3%)
  other arithmetic  2.76 us (2%)
  between operations  1.64 us (1%)
    ppermute x17, starting transfers between devices, shift(): return lax.ppermute(value, 'fsdp', pairs)  29.6 us
    ppermute x17, waiting for transfers between devices, shift(): return lax.ppermute(value, 'fsdp', pairs)  23.9 us
    pallas_call x2, Pallas kernels, normalize(): pl.pallas_call(functools.partial(norm_kernel, width, groups, relative, ex...  13 us
    pallas_call x2, Pallas kernels, near_gradient(): pl.pallas_call(functools.partial(near_gradient_kernel, factor, width, sta...  5.9 us
    pallas_call x1, Pallas kernels, near_project(): pl.pallas_call(functools.partial(near_project_kernel, factor, len(weights...  5.88 us
    pallas_call x1, Pallas kernels, far_project(): pl.pallas_call(far_project_kernel, in_specs=[SMEM, VMEM] + in_memory(len(...  5.53 us
    pallas_call x1, Pallas kernels, far_gradient(): pl.pallas_call(functools.partial(far_gradient_kernel, factor, width), in_...  5.37 us
    all_to_all x1, waiting for transfers between devices, per_device(): lax.all_to_all(far, 'fsdp', 0, 0, axis_index_groups=along_y, tiled=True)  5.25 us
  transfers between devices with their start and end apart: 23, of which 9 were waited for; matrix products, arithmetic and copies ran while one was open for 1% of the time, Pallas kernels for 27%

profile of v4, /device:TPU:32, one launch (start us, length us, event | category | flops | bytes accessed | tf_op | source)
XLA Modules:
  0.0 131.9 jit_solution(1052395004958161502)
XLA Ops:
  0.6 6.6 %norm.2 = bf16[4,256,2048]{2,1,0:T(8,128)(2,1)} custom-call(bf16[256,12288]{1,0:T(8,128)(2,1)} %bitcast.24, bf16[96,128]{1,0:T(8,128)(2,1)} %bitcast.36, bf16[256,512]{1,0:T(8,128)(2,1)} %bitcast.26), custom_call_target="tpu_custom_call" | custom-call | flops 1 | bytes 1 | tf_op jit(solution)/shard_map/norm/pallas_call | solution.py:148
  7.3 5.0 %all-to-all-start = ((bf16[4,256,2048]{2,1,0:T(8,128)(2,1)}), bf16[4,256,2048]{2,1,0:T(8,128)(2,1)}, u32[]{:S(2)}, u32[]{:S(2)}) async-start(bf16[4,256,2048]{2,1,0:T(8,128)(2,1)} %norm.2), calls=%async_computation | async-start | bytes 8388608 | tf_op jit(solution)/shard_map/all_to_all | solution.py:502
  12.6 6.4 %collective-permute-start = (bf16[384,512]{1,0:T(8,128)(2,1)S(1)}, bf16[384,512]{1,0:T(8,128)(2,1)S(1)}, u32[]{:S(2)}, u32[]{:S(2)}) collective-permute-start(bf16[384,512]{1,0:T(8,128)(2,1)S(1)} %bitcast.32), channel_id=1, source_target_pairs={{0,1},{1,0},{2,3},{3,2},{4,5},{5,4},{6,7},{7,6},{8,9},{9,8},{10,11... | collective-permute-start | bytes 1179656 | tf_op jit(solution)/shard_map/ppermute | solution.py:38
  18.9 3.0 %collective-permute-start.2 = (bf16[384,512]{1,0:T(8,128)(2,1)S(1)}, bf16[384,512]{1,0:T(8,128)(2,1)S(1)}, u32[]{:S(2)}, u32[]{:S(2)}) collective-permute-start(bf16[384,512]{1,0:T(8,128)(2,1)S(1)} %bitcast.33), channel_id=1, source_target_pairs={{0,24},{1,25},{2,26},{3,27},{4,28},{5,29},{6,30},{7,31},{8,0},{9,1... | collective-permute-start | bytes 1179656 | tf_op jit(solution)/shard_map/ppermute | solution.py:38
  23.7 13.5 %collective-permute-done.refs_0_ = bf16[384,512]{1,0:T(8,128)(2,1)S(1)} collective-permute-done((bf16[384,512]{1,0:T(8,128)(2,1)S(1)}, bf16[384,512]{1,0:T(8,128)(2,1)S(1)}, u32[]{:S(2)}, u32[]{:S(2)}) %collective-permute-start) | collective-permute-done | bytes 393248 | tf_op jit(solution)/shard_map/ppermute | solution.py:38
  37.1 1.9 %collective-permute-done.2.refs_8_ = bf16[384,512]{1,0:T(8,128)(2,1)S(1)} collective-permute-done((bf16[384,512]{1,0:T(8,128)(2,1)S(1)}, bf16[384,512]{1,0:T(8,128)(2,1)S(1)}, u32[]{:S(2)}, u32[]{:S(2)}) %collective-permute-start.2) | collective-permute-done | bytes 393248 | tf_op jit(solution)/shard_map/ppermute | solution.py:38
  39.1 3.7 %collective-permute-done.4.refs_10_ = bf16[384,512]{1,0:T(8,128)(2,1)S(1)} collective-permute-done((bf16[384,512]{1,0:T(8,128)(2,1)S(1)}, bf16[384,512]{1,0:T(8,128)(2,1)S(1)}, u32[]{:S(2)}, u32[]{:S(2)}) %collective-permute-start.4) | collective-permute-done | bytes 393248 | tf_op jit(solution)/shard_map/ppermute | solution.py:38
  45.9 3.8 %collective-permute-done.8 = f32[384,128]{1,0:T(8,128)S(1)} collective-permute-done((f32[384,128]{1,0:T(8,128)S(1)}, f32[384,128]{1,0:T(8,128)S(1)}, u32[]{:S(2)}, u32[]{:S(2)}) %collective-permute-start.8) | collective-permute-done | bytes 196640 | tf_op jit(solution)/shard_map/ppermute | solution.py:490
  51.5 6.4 %norm.3 = (bf16[256,1152]{1,0:T(8,128)(2,1)}, bf16[256,1152]{1,0:T(8,128)(2,1)}, bf16[256,1152]{1,0:T(8,128)(2,1)}, bf16[256,1152]{1,0:T(8,128)(2,1)}, bf16[256,...) custom-call(bf16[256,12288]{1,0:T(8,128)(2,1)} %bitcast.25, ...), custom_call_target="tpu_custom_call" | custom-call | flops 1 | bytes 1 | tf_op jit(solution)/shard_map/norm/pallas_call | solution.py:148
  57.9 1.9 %collective-permute-start.10 = (bf16[256,1152]{1,0:T(8,128)(2,1)}, bf16[256,1152]{1,0:T(8,128)(2,1)}, u32[]{:S(2)}, u32[]{:S(2)}) collective-permute-start(bf16[256,1152]{1,0:T(8,128)(2,1)} %get-tuple-element.47), channel_id=1, source_target_pairs={{0,2},{1,3},{2,4},{3,5},{4,6},{5,7},{6,0},{7,1},{8,10},{9,11},{10,... | collective-permute-start | bytes 1769480 | tf_op jit(solution)/shard_map/ppermute | solution.py:38
  59.8 2.8 %collective-permute-start.11 = (bf16[256,1152]{1,0:T(8,128)(2,1)}, bf16[256,1152]{1,0:T(8,128)(2,1)}, u32[]{:S(2)}, u32[]{:S(2)}) collective-permute-start(bf16[256,1152]{1,0:T(8,128)(2,1)} %get-tuple-element.48), channel_id=1, source_target_pairs={{0,4},{1,5},{2,6},{3,7},{4,0},{5,1},{6,2},{7,3},{8,12},{9,13},{10,... | collective-permute-start | bytes 1769480 | tf_op jit(solution)/shard_map/ppermute | solution.py:38
  64.7 5.4 %far_gradient.1 = (bf16[4,512,384]{2,1,0:T(8,128)(2,1)}, bf16[512,1024]{1,0:T(8,128)(2,1)S(1)}) custom-call(s32[4]{0:T(128)S(1)} %pad_add_fusion.targets_ref, bf16[4,256,2048]{2,1,0:T(8,128)(2,1)} %all-to-all-done.chunk), custom_call_target="tpu_custom_call" | custom-call | flops 99999997952 | bytes 1 | tf_op jit(solution)/shard_map/far_gradient/pallas_call | solution.py:202
  70.0 2.0 %collective-permute-start.13 = (bf16[256,384]{1,0:T(8,128)(2,1)}, bf16[256,384]{1,0:T(8,128)(2,1)}, u32[]{:S(2)}, u32[]{:S(2)}) collective-permute-start(bf16[256,384]{1,0:T(8,128)(2,1)} %get-tuple-element.66), channel_id=1, source_target_pairs={{0,2},{1,3},{2,4},{3,5},{4,6},{5,7},{6,0},{7,1},{8,10},{9,11},{10,... | collective-permute-start | bytes 589832 | tf_op jit(solution)/shard_map/ppermute | solution.py:38
  72.1 2.8 %collective-permute-start.14 = (bf16[256,384]{1,0:T(8,128)(2,1)}, bf16[256,384]{1,0:T(8,128)(2,1)}, u32[]{:S(2)}, u32[]{:S(2)}) collective-permute-start(bf16[256,384]{1,0:T(8,128)(2,1)} %get-tuple-element.67), channel_id=1, source_target_pairs={{0,4},{1,5},{2,6},{3,7},{4,0},{5,1},{6,2},{7,3},{8,12},{9,13},{10,... | collective-permute-start | bytes 589832 | tf_op jit(solution)/shard_map/ppermute | solution.py:38
  74.9 4.4 %all-to-all-start.1 = ((bf16[4,512,384]{2,1,0:T(8,128)(2,1)}), bf16[4,512,384]{2,1,0:T(8,128)(2,1)}, u32[]{:S(2)}, u32[]{:S(2)}) async-start(bf16[4,512,384]{2,1,0:T(8,128)(2,1)} %get-tuple-element.53), calls=%async_computation.1 | async-start | bytes 3145728 | tf_op jit(solution)/shard_map/all_to_all | solution.py:533
  79.3 5.5 %far_project.1.start_hbm = f32[4,256,512]{2,1,0:T(8,128)S(1)} custom-call(s32[4]{0:T(128)S(1)} %pad_add_fusion.1.sources_ref, bf16[4,256,2048]{2,1,0:T(8,128)(2,1)} %all-to-all-done.chunk, bf16[384,512]{1,0:T(8,128)(2,1)S(1)} %collective-permute-done.refs_0_, bf16[384,512]{1,0:T(8,128)(2,1)S(1)} %collective-permute-done.5.refs_1_, ...), custom_call_target="tpu_custom_call" | custom-call | flops 99999997952 | bytes 1 | tf_op jit(solution)/shard_map/far_project/pallas_call | solution.py:269
  87.5 2.3 %collective-permute-done.11.refs_2_ = bf16[256,1152]{1,0:T(8,128)(2,1)} collective-permute-done((bf16[256,1152]{1,0:T(8,128)(2,1)}, bf16[256,1152]{1,0:T(8,128)(2,1)}, u32[]{:S(2)}, u32[]{:S(2)}) %collective-permute-start.11) | collective-permute-done | bytes 589856 | tf_op jit(solution)/shard_map/ppermute | solution.py:38
  90.5 4.2 %near_gradient.2 = bf16[4,512,384]{2,1,0:T(8,128)(2,1)} custom-call(s32[4]{0:T(128)S(1)} %pad_add_fusion.1.sources_ref, s32[4]{0:T(128)S(1)} %pad_add_fusion.targets_ref, bf16[512,1024]{1,0:T(8,128)(2,1)S(1)} %get-tuple-element.59.cots, bf16[256,1152]{1,0:T(8,128)(2,1)S(1)} %copy-done.4, bf16[256,1152]{1,0:T(8,128)(2,1)} %collective-permute-done.10.refs_1_, ...), custom_call_target="tpu_custom_call" | custom-call | flops 99999997952 | bytes 1 | tf_op jit(solution)/shard_map/near_gradient/pallas_call | solution.py:376
  94.7 5.2 %all-to-all-done.1.terms = bf16[4,512,384]{2,1,0:T(8,128)(2,1)} async-done(((bf16[4,512,384]{2,1,0:T(8,128)(2,1)}), bf16[4,512,384]{2,1,0:T(8,128)(2,1)}, u32[]{:S(2)}, u32[]{:S(2)}) %all-to-all-start.1) | async-done | bytes 1572896 | tf_op jit(solution)/shard_map/all_to_all | solution.py:533
  101.5 1.9 %collective-permute-start.16 = (bf16[512,384]{1,0:T(8,128)(2,1)S(1)}, bf16[512,384]{1,0:T(8,128)(2,1)S(1)}, u32[]{:S(2)}, u32[]{:S(2)}) collective-permute-start(bf16[512,384]{1,0:T(8,128)(2,1)S(1)} %add_up.1), channel_id=1, source_target_pairs={{0,1},{1,0},{2,3},{3,2},{4,5},{5,4},{6,7},{7,6},{8,9},{9,8},{10,11... | collective-permute-start | bytes 1179656 | tf_op jit(solution)/shard_map/ppermute | solution.py:38
  103.4 4.4 %all-to-all-start.2 = ((bf16[4,512,384]{2,1,0:T(8,128)(2,1)}), bf16[4,512,384]{2,1,0:T(8,128)(2,1)}, u32[]{:S(2)}, u32[]{:S(2)}) async-start(bf16[4,512,384]{2,1,0:T(8,128)(2,1)} %near_gradient.2), calls=%async_computation.2 | async-start | bytes 3145728 | tf_op jit(solution)/shard_map/all_to_all | solution.py:540
  108.5 5.9 %near_project.1 = (f32[256,512]{1,0:T(8,128)}, bf16[256,512]{1,0:T(8,128)(2,1)}, bf16[256,512]{1,0:T(8,128)(2,1)}, bf16[256,512]{1,0:T(8,128)(2,1)}) custom-call(f32[4,256,512]{2,1,0:T(8,128)} %copy-done.5, bf16[256,1152]{1,0:T(8,128)(2,1)} %get-tuple-element.46.refs_0_, bf16[256,1152]{1,0:T(8,128)(2,1)} %collective-permute-done.10.refs_1_, ...), custom_call_target="tpu_custom_call" | custom-call | flops 99999997952 | bytes 1 | tf_op jit(solution)/shard_map/near_project/pallas_call | solution.py:320
  123.5 3.0 %all-to-all-done.2.refs_0_ = bf16[4,512,384]{2,1,0:T(8,128)(2,1)} async-done(((bf16[4,512,384]{2,1,0:T(8,128)(2,1)}), bf16[4,512,384]{2,1,0:T(8,128)(2,1)}, u32[]{:S(2)}, u32[]{:S(2)}) %all-to-all-start.2) | async-done | bytes 1572896 | tf_op jit(solution)/shard_map/all_to_all | solution.py:540
  126.5 4.5 %update.1 = (bf16[384,512]{1,0:T(8,128)(2,1)}, f32[384,512]{1,0:T(8,128)}, f32[384,512]{1,0:T(8,128)}) custom-call(s32[1]{0:T(128)S(6)} %select_n.63.offset_ref, bf16[4,512,384]{2,1,0:T(8,128)(2,1)} %all-to-all-done.2.refs_0_, bf16[512,384]{1,0:T(8,128)(2,1)} %copy-done, bf16[512,384]{1,0:T(8,128)(2,1)} %copy-done.9, f32[384,128]{1,0:T(8,128)} %get-tuple-element.84.refs_3_, ...), custom_call_target="tpu_custom_call" | custom-call | flops 1 | bytes 1 | tf_op jit(solution)/shard_map/update/pallas_call | solution.py:452
  (76 shorter events, 23.9 us)
Async XLA Ops:
  7.3 57.4 %all-to-all-start = ((bf16[4,256,2048]{2,1,0:T(8,128)(2,1)}), bf16[4,256,2048]{2,1,0:T(8,128)(2,1)}, u32[]{:S(2)}, u32[]{:S(2)}) async-start(bf16[4,256,2048]{2,1,0:T(8,128)(2,1)} %norm.2), calls=%async_computation | async-start | bytes 8388608 | tf_op jit(solution)/shard_map/all_to_all | solution.py:502
  12.5 11.1 %collective-permute-start.1 = (f32[384,128]{1,0:T(8,128)S(1)}, f32[384,128]{1,0:T(8,128)S(1)}, u32[]{:S(2)}, u32[]{:S(2)}) collective-permute-start(f32[384,128]{1,0:T(8,128)S(1)} %convert_multiply_fusion), channel_id=1, source_target_pairs={{0,32},{32,0},{64,96},{96,64},{128,160},{160,128},{192,224},{224,1... | collective-permute-start | bytes 589832 | tf_op jit(solution)/shard_map/ppermute | solution.py:490
  12.6 24.6 %collective-permute-start = (bf16[384,512]{1,0:T(8,128)(2,1)S(1)}, bf16[384,512]{1,0:T(8,128)(2,1)S(1)}, u32[]{:S(2)}, u32[]{:S(2)}) collective-permute-start(bf16[384,512]{1,0:T(8,128)(2,1)S(1)} %bitcast.32), channel_id=1, source_target_pairs={{0,1},{1,0},{2,3},{3,2},{4,5},{5,4},{6,7},{7,6},{8,9},{9,8},{10,11... | collective-permute-start | bytes 1179656 | tf_op jit(solution)/shard_map/ppermute | solution.py:38
  18.9 20.1 %collective-permute-start.2 = (bf16[384,512]{1,0:T(8,128)(2,1)S(1)}, bf16[384,512]{1,0:T(8,128)(2,1)S(1)}, u32[]{:S(2)}, u32[]{:S(2)}) collective-permute-start(bf16[384,512]{1,0:T(8,128)(2,1)S(1)} %bitcast.33), channel_id=1, source_target_pairs={{0,24},{1,25},{2,26},{3,27},{4,28},{5,29},{6,30},{7,31},{8,0},{9,1... | collective-permute-start | bytes 1179656 | tf_op jit(solution)/shard_map/ppermute | solution.py:38
  22.0 17.1 %collective-permute-start.3 = (bf16[384,512]{1,0:T(8,128)(2,1)S(1)}, bf16[384,512]{1,0:T(8,128)(2,1)S(1)}, u32[]{:S(2)}, u32[]{:S(2)}) collective-permute-start(bf16[384,512]{1,0:T(8,128)(2,1)S(1)} %bitcast.34), channel_id=1, source_target_pairs={{0,16},{1,17},{2,18},{3,19},{4,20},{5,21},{6,22},{7,23},{8,24},{9,... | collective-permute-start | bytes 1179656 | tf_op jit(solution)/shard_map/ppermute | solution.py:38
  22.6 20.2 %collective-permute-start.4 = (bf16[384,512]{1,0:T(8,128)(2,1)S(1)}, bf16[384,512]{1,0:T(8,128)(2,1)S(1)}, u32[]{:S(2)}, u32[]{:S(2)}) collective-permute-start(bf16[384,512]{1,0:T(8,128)(2,1)S(1)} %bitcast.35), channel_id=1, source_target_pairs={{0,8},{1,9},{2,10},{3,11},{4,12},{5,13},{6,14},{7,15},{8,16},{9,17... | collective-permute-start | bytes 1179656 | tf_op jit(solution)/shard_map/ppermute | solution.py:38
  42.8 6.9 %collective-permute-start.8 = (f32[384,128]{1,0:T(8,128)S(1)}, f32[384,128]{1,0:T(8,128)S(1)}, u32[]{:S(2)}, u32[]{:S(2)}) collective-permute-start(f32[384,128]{1,0:T(8,128)S(1)} %fusion.1), channel_id=1, source_target_pairs={{0,64},{32,96},{64,0},{96,32},{128,192},{160,224},{192,128},{224,1... | collective-permute-start | bytes 589832 | tf_op jit(solution)/shard_map/ppermute | solution.py:490
  43.8 19.5 %collective-permute-start.5 = (bf16[384,512]{1,0:T(8,128)(2,1)S(1)}, bf16[384,512]{1,0:T(8,128)(2,1)S(1)}, u32[]{:S(2)}, u32[]{:S(2)}) collective-permute-start(bf16[384,512]{1,0:T(8,128)(2,1)S(1)} %collective-permute-done.refs_0_), channel_id=1, source_target_pairs={{0,24},{1,25},{2,26},{3,27},{4,28},{5,29},{6,30},{7,31},{8,0},{9,1... | collective-permute-start | bytes 1179656 | tf_op jit(solution)/shard_map/ppermute | solution.py:38
  44.4 20.2 %collective-permute-start.6 = (bf16[384,512]{1,0:T(8,128)(2,1)S(1)}, bf16[384,512]{1,0:T(8,128)(2,1)S(1)}, u32[]{:S(2)}, u32[]{:S(2)}) collective-permute-start(bf16[384,512]{1,0:T(8,128)(2,1)S(1)} %collective-permute-done.refs_0_), channel_id=1, source_target_pairs={{0,16},{1,17},{2,18},{3,19},{4,20},{5,21},{6,22},{7,23},{8,24},{9,... | collective-permute-start | bytes 1179656 | tf_op jit(solution)/shard_map/ppermute | solution.py:38
  45.0 19.6 %collective-permute-start.7 = (bf16[384,512]{1,0:T(8,128)(2,1)S(1)}, bf16[384,512]{1,0:T(8,128)(2,1)S(1)}, u32[]{:S(2)}, u32[]{:S(2)}) collective-permute-start(bf16[384,512]{1,0:T(8,128)(2,1)S(1)} %collective-permute-done.refs_0_), channel_id=1, source_target_pairs={{0,8},{1,9},{2,10},{3,11},{4,12},{5,13},{6,14},{7,15},{8,16},{9,17... | collective-permute-start | bytes 1179656 | tf_op jit(solution)/shard_map/ppermute | solution.py:38
  49.7 10.1 %collective-permute-start.9 = (f32[384,128]{1,0:T(8,128)S(1)}, f32[384,128]{1,0:T(8,128)S(1)}, u32[]{:S(2)}, u32[]{:S(2)}) collective-permute-start(f32[384,128]{1,0:T(8,128)S(1)} %add.80), channel_id=1, source_target_pairs={{0,128},{32,160},{64,192},{96,224},{128,0},{160,32},{192,64},{224,... | collective-permute-start | bytes 589832 | tf_op jit(solution)/shard_map/ppermute | solution.py:490
  57.9 28.3 %collective-permute-start.10 = (bf16[256,1152]{1,0:T(8,128)(2,1)}, bf16[256,1152]{1,0:T(8,128)(2,1)}, u32[]{:S(2)}, u32[]{:S(2)}) collective-permute-start(bf16[256,1152]{1,0:T(8,128)(2,1)} %get-tuple-element.47), channel_id=1, source_target_pairs={{0,2},{1,3},{2,4},{3,5},{4,6},{5,7},{6,0},{7,1},{8,10},{9,11},{10,... | collective-permute-start | bytes 1769480 | tf_op jit(solution)/shard_map/ppermute | solution.py:38
  59.8 30.0 %collective-permute-start.11 = (bf16[256,1152]{1,0:T(8,128)(2,1)}, bf16[256,1152]{1,0:T(8,128)(2,1)}, u32[]{:S(2)}, u32[]{:S(2)}) collective-permute-start(bf16[256,1152]{1,0:T(8,128)(2,1)} %get-tuple-element.48), channel_id=1, source_target_pairs={{0,4},{1,5},{2,6},{3,7},{4,0},{5,1},{6,2},{7,3},{8,12},{9,13},{10,... | collective-permute-start | bytes 1769480 | tf_op jit(solution)/shard_map/ppermute | solution.py:38
  63.3 27.2 %collective-permute-start.12 = (bf16[256,1152]{1,0:T(8,128)(2,1)}, bf16[256,1152]{1,0:T(8,128)(2,1)}, u32[]{:S(2)}, u32[]{:S(2)}) collective-permute-start(bf16[256,1152]{1,0:T(8,128)(2,1)} %get-tuple-element.49), channel_id=1, source_target_pairs={{0,6},{1,7},{2,0},{3,1},{4,2},{5,3},{6,4},{7,5},{8,14},{9,15},{10,... | collective-permute-start | bytes 1769480 | tf_op jit(solution)/shard_map/ppermute | solution.py:38
  70.0 37.8 %collective-permute-start.13 = (bf16[256,384]{1,0:T(8,128)(2,1)}, bf16[256,384]{1,0:T(8,128)(2,1)}, u32[]{:S(2)}, u32[]{:S(2)}) collective-permute-start(bf16[256,384]{1,0:T(8,128)(2,1)} %get-tuple-element.66), channel_id=1, source_target_pairs={{0,2},{1,3},{2,4},{3,5},{4,6},{5,7},{6,0},{7,1},{8,10},{9,11},{10,... | collective-permute-start | bytes 589832 | tf_op jit(solution)/shard_map/ppermute | solution.py:38
  72.1 35.7 %collective-permute-start.14 = (bf16[256,384]{1,0:T(8,128)(2,1)}, bf16[256,384]{1,0:T(8,128)(2,1)}, u32[]{:S(2)}, u32[]{:S(2)}) collective-permute-start(bf16[256,384]{1,0:T(8,128)(2,1)} %get-tuple-element.67), channel_id=1, source_target_pairs={{0,4},{1,5},{2,6},{3,7},{4,0},{5,1},{6,2},{7,3},{8,12},{9,13},{10,... | collective-permute-start | bytes 589832 | tf_op jit(solution)/shard_map/ppermute | solution.py:38
  74.9 25.0 %all-to-all-start.1 = ((bf16[4,512,384]{2,1,0:T(8,128)(2,1)}), bf16[4,512,384]{2,1,0:T(8,128)(2,1)}, u32[]{:S(2)}, u32[]{:S(2)}) async-start(bf16[4,512,384]{2,1,0:T(8,128)(2,1)} %get-tuple-element.53), calls=%async_computation.1 | async-start | bytes 3145728 | tf_op jit(solution)/shard_map/all_to_all | solution.py:533
  79.3 11.2 %copy-start.4 = (bf16[256,1152]{1,0:T(8,128)(2,1)S(1)}, bf16[256,1152]{1,0:T(8,128)(2,1)}, u32[]{:S(2)}) copy-start(bf16[256,1152]{1,0:T(8,128)(2,1)} %get-tuple-element.46.refs_0_) | copy-start | bytes 1769476
  86.2 21.7 %collective-permute-start.15 = (bf16[256,384]{1,0:T(8,128)(2,1)S(1)}, bf16[256,384]{1,0:T(8,128)(2,1)S(1)}, u32[]{:S(2)}, u32[]{:S(2)}) collective-permute-start(bf16[256,384]{1,0:T(8,128)(2,1)S(1)} %copy-done.17), channel_id=1, source_target_pairs={{0,6},{1,7},{2,0},{3,1},{4,2},{5,3},{6,4},{7,5},{8,14},{9,15},{10,... | collective-permute-start | bytes 589832 | tf_op jit(solution)/shard_map/ppermute | solution.py:38
  101.5 22.0 %collective-permute-start.16 = (bf16[512,384]{1,0:T(8,128)(2,1)S(1)}, bf16[512,384]{1,0:T(8,128)(2,1)S(1)}, u32[]{:S(2)}, u32[]{:S(2)}) collective-permute-start(bf16[512,384]{1,0:T(8,128)(2,1)S(1)} %add_up.1), channel_id=1, source_target_pairs={{0,1},{1,0},{2,3},{3,2},{4,5},{5,4},{6,7},{7,6},{8,9},{9,8},{10,11... | collective-permute-start | bytes 1179656 | tf_op jit(solution)/shard_map/ppermute | solution.py:38
  103.4 23.1 %all-to-all-start.2 = ((bf16[4,512,384]{2,1,0:T(8,128)(2,1)}), bf16[4,512,384]{2,1,0:T(8,128)(2,1)}, u32[]{:S(2)}, u32[]{:S(2)}) async-start(bf16[4,512,384]{2,1,0:T(8,128)(2,1)} %near_gradient.2), calls=%async_computation.2 | async-start | bytes 3145728 | tf_op jit(solution)/shard_map/all_to_all | solution.py:540
  114.4 16.6 %collective-permute-start.17 = (bf16[256,512]{1,0:T(8,128)(2,1)}, bf16[256,512]{1,0:T(8,128)(2,1)S(1)}, u32[]{:S(2)}, u32[]{:S(2)}) collective-permute-start(bf16[256,512]{1,0:T(8,128)(2,1)} %get-tuple-element.78), channel_id=1, source_target_pairs={{0,6},{1,7},{2,0},{3,1},{4,2},{5,3},{6,4},{7,5},{8,14},{9,15},{10,... | collective-permute-start | bytes 786440 | tf_op jit(solution)/shard_map/ppermute | solution.py:38
  115.8 15.2 %collective-permute-start.18 = (bf16[256,512]{1,0:T(8,128)(2,1)}, bf16[256,512]{1,0:T(8,128)(2,1)S(1)}, u32[]{:S(2)}, u32[]{:S(2)}) collective-permute-start(bf16[256,512]{1,0:T(8,128)(2,1)} %get-tuple-element.79), channel_id=1, source_target_pairs={{0,4},{1,5},{2,6},{3,7},{4,0},{5,1},{6,2},{7,3},{8,12},{9,13},{10,... | collective-permute-start | bytes 786440 | tf_op jit(solution)/shard_map/ppermute | solution.py:38
  116.3 14.7 %collective-permute-start.19 = (bf16[256,512]{1,0:T(8,128)(2,1)}, bf16[256,512]{1,0:T(8,128)(2,1)S(1)}, u32[]{:S(2)}, u32[]{:S(2)}) collective-permute-start(bf16[256,512]{1,0:T(8,128)(2,1)} %get-tuple-element.80), channel_id=1, source_target_pairs={{0,2},{1,3},{2,4},{3,5},{4,6},{5,7},{6,0},{7,1},{8,10},{9,11},{10,... | collective-permute-start | bytes 786440 | tf_op jit(solution)/shard_map/ppermute | solution.py:38
  (17 other events, 87.6 us)

commit v5 on v4

--- a/solution.py
+++ b/solution.py
@@ -19,7 +19,7 @@
 
 NY, NX, NZ = 4, 4, 2
 ROWS = 32
-AHEAD = 3
+AHEAD = 7
 VMEM_LIMIT = 60 * 1024 * 1024
 HEAVY = 10**11
 
@@ -391,12 +391,6 @@
     rows, keys = weight.shape
     head = fresh.shape[1]
     block = 128
-    sums = [
-        pltpu.make_async_copy(source, target, sums_came.at[n])
-        for n, (source, target) in enumerate(zip(sums_hbm, (near, own, far, fresh)))
-    ]
-    for copy in sums:
-        copy.start()
     fetches, stores = [], []
     for i in range(rows // block):
         span = pl.ds(i * block, block)
@@ -404,6 +398,18 @@
             [
                 pltpu.make_async_copy(source.at[span], target.at[span], came.at[i, n])
                 for n, (source, target) in enumerate(zip(ins, (weight, first, second)))
+            ]
+            + [
+                pltpu.make_async_copy(
+                    sums_hbm[0].at[:, :, span], near.at[:, :, span], sums_came.at[i, 0]
+                ),
+                pltpu.make_async_copy(
+                    sums_hbm[1].at[:, span], own.at[:, span], sums_came.at[i, 1]
+                ),
+                pltpu.make_async_copy(
+                    sums_hbm[2].at[:, span], far.at[:, span], sums_came.at[i, 2]
+                ),
+                pltpu.make_async_copy(sums_hbm[3].at[span], fresh.at[span], sums_came.at[i, 3]),
             ]
         )
         stores.append(
@@ -414,16 +420,14 @@
         )
         for copy in fetches[i]:
             copy.start()
-    for copy in sums:
-        copy.wait()
     for i in range(rows // block):
         low, high = i * block, (i + 1) * block
+        for copy in fetches[i]:
+            copy.wait()
         summed = own[:, low:high].astype(jnp.float32) + far[:, low:high].astype(jnp.float32)
         for number in range(near.shape[0]):
             summed = summed + near[number, :, low:high].astype(jnp.float32)
         gradient = summed.T
-        for copy in fetches[i]:
-            copy.wait()
         moment_one = beta_one * first[low:high, :] + (1.0 - beta_one) * gradient
         moment_two = beta_two * second[low:high, :] + (1.0 - beta_two) * gradient * gradient
         first_new[low:high, :] = moment_one
@@ -457,7 +461,7 @@
         scratch_shapes=[pltpu.VMEM((rows, keys), t) for t in types + types]
         + [pltpu.VMEM(term.shape, term.dtype) for term in (*terms, fresh)]
         + [pltpu.SemaphoreType.DMA((rows // 128, 3))] * 2
-        + [pltpu.SemaphoreType.DMA((4,))],
+        + [pltpu.SemaphoreType.DMA((rows // 128, 4))],
         name="update",
         **call_options(),
     )(head_index, *terms, fresh, weight, first, second)

time: 134 us -> 132 us (0.985)
  Pallas kernels: 41.8 us -> 39.9 us
  transfers between devices with their start and end apart: 23 -> 23, of which waited for: 9 -> 10; matrix products, arithmetic and copies ran while one was open for 1% -> 1% of each run, Pallas kernels for 27% -> 26%
where the time goes in v5:
time: 132 us; the launch traced here: 131 us
  starting transfers between devices  46.3 us (35%)
  Pallas kernels  39.9 us (30%)
  waiting for transfers between devices  36.2 us (27%)
  local copies, waits for them, and re-layouts  3.75 us (3%)
  other arithmetic  2.76 us (2%)
  between operations  1.64 us (1%)
    ppermute x17, starting transfers between devices, shift(): return lax.ppermute(value, 'fsdp', pairs)  29.9 us
    ppermute x17, waiting for transfers between devices, shift(): return lax.ppermute(value, 'fsdp', pairs)  24.1 us
    pallas_call x2, Pallas kernels, normalize(): pl.pallas_call(functools.partial(norm_kernel, width, groups, relative, ex...  11.9 us
    pallas_call x2, Pallas kernels, near_gradient(): pl.pallas_call(functools.partial(near_gradient_kernel, factor, width, sta...  5.9 us
    pallas_call x1, Pallas kernels, near_project(): pl.pallas_call(functools.partial(near_project_kernel, factor, len(weights...  5.88 us
    pallas_call x1, Pallas kernels, far_project(): pl.pallas_call(far_project_kernel, in_specs=[SMEM, VMEM] + in_memory(len(...  5.53 us
    pallas_call x1, Pallas kernels, far_gradient(): pl.pallas_call(functools.partial(far_gradient_kernel, factor, width), in_...  5.37 us
    all_to_all x1, waiting for transfers between devices, per_device(): lax.all_to_all(far, 'fsdp', 0, 0, axis_index_groups=along_y, tiled=True)  5.25 us
  transfers between devices with their start and end apart: 23, of which 10 were waited for; matrix products, arithmetic and copies ran while one was open for 1% of the time, Pallas kernels for 26%

profile of v5, /device:TPU:32, one launch (start us, length us, event | category | flops | bytes accessed | tf_op | source)
XLA Modules:
  0.0 130.5 jit_solution(11465508856018193014)
XLA Ops:
  0.6 6.0 %norm.2 = bf16[4,256,2048]{2,1,0:T(8,128)(2,1)} custom-call(bf16[256,12288]{1,0:T(8,128)(2,1)} %bitcast.24, bf16[96,128]{1,0:T(8,128)(2,1)} %bitcast.36, bf16[256,512]{1,0:T(8,128)(2,1)} %bitcast.26), custom_call_target="tpu_custom_call" | custom-call | flops 1 | bytes 1 | tf_op jit(solution)/shard_map/norm/pallas_call | solution.py:148
  6.7 5.0 %all-to-all-start = ((bf16[4,256,2048]{2,1,0:T(8,128)(2,1)}), bf16[4,256,2048]{2,1,0:T(8,128)(2,1)}, u32[]{:S(2)}, u32[]{:S(2)}) async-start(bf16[4,256,2048]{2,1,0:T(8,128)(2,1)} %norm.2), calls=%async_computation | async-start | bytes 8388608 | tf_op jit(solution)/shard_map/all_to_all | solution.py:506
  12.0 6.4 %collective-permute-start = (bf16[384,512]{1,0:T(8,128)(2,1)S(1)}, bf16[384,512]{1,0:T(8,128)(2,1)S(1)}, u32[]{:S(2)}, u32[]{:S(2)}) collective-permute-start(bf16[384,512]{1,0:T(8,128)(2,1)S(1)} %bitcast.32), channel_id=1, source_target_pairs={{0,1},{1,0},{2,3},{3,2},{4,5},{5,4},{6,7},{7,6},{8,9},{9,8},{10,11... | collective-permute-start | bytes 1179656 | tf_op jit(solution)/shard_map/ppermute | solution.py:38
  18.4 3.0 %collective-permute-start.2 = (bf16[384,512]{1,0:T(8,128)(2,1)S(1)}, bf16[384,512]{1,0:T(8,128)(2,1)S(1)}, u32[]{:S(2)}, u32[]{:S(2)}) collective-permute-start(bf16[384,512]{1,0:T(8,128)(2,1)S(1)} %bitcast.33), channel_id=1, source_target_pairs={{0,24},{1,25},{2,26},{3,27},{4,28},{5,29},{6,30},{7,31},{8,0},{9,1... | collective-permute-start | bytes 1179656 | tf_op jit(solution)/shard_map/ppermute | solution.py:38
  23.1 13.5 %collective-permute-done.refs_0_ = bf16[384,512]{1,0:T(8,128)(2,1)S(1)} collective-permute-done((bf16[384,512]{1,0:T(8,128)(2,1)S(1)}, bf16[384,512]{1,0:T(8,128)(2,1)S(1)}, u32[]{:S(2)}, u32[]{:S(2)}) %collective-permute-start) | collective-permute-done | bytes 393248 | tf_op jit(solution)/shard_map/ppermute | solution.py:38
  36.6 1.9 %collective-permute-done.2.refs_8_ = bf16[384,512]{1,0:T(8,128)(2,1)S(1)} collective-permute-done((bf16[384,512]{1,0:T(8,128)(2,1)S(1)}, bf16[384,512]{1,0:T(8,128)(2,1)S(1)}, u32[]{:S(2)}, u32[]{:S(2)}) %collective-permute-start.2) | collective-permute-done | bytes 393248 | tf_op jit(solution)/shard_map/ppermute | solution.py:38
  38.5 3.7 %collective-permute-done.4.refs_10_ = bf16[384,512]{1,0:T(8,128)(2,1)S(1)} collective-permute-done((bf16[384,512]{1,0:T(8,128)(2,1)S(1)}, bf16[384,512]{1,0:T(8,128)(2,1)S(1)}, u32[]{:S(2)}, u32[]{:S(2)}) %collective-permute-start.4) | collective-permute-done | bytes 393248 | tf_op jit(solution)/shard_map/ppermute | solution.py:38
  45.3 3.8 %collective-permute-done.8 = f32[384,128]{1,0:T(8,128)S(1)} collective-permute-done((f32[384,128]{1,0:T(8,128)S(1)}, f32[384,128]{1,0:T(8,128)S(1)}, u32[]{:S(2)}, u32[]{:S(2)}) %collective-permute-start.8) | collective-permute-done | bytes 196640 | tf_op jit(solution)/shard_map/ppermute | solution.py:494
  50.9 5.9 %norm.3 = (bf16[256,1152]{1,0:T(8,128)(2,1)}, bf16[256,1152]{1,0:T(8,128)(2,1)}, bf16[256,1152]{1,0:T(8,128)(2,1)}, bf16[256,1152]{1,0:T(8,128)(2,1)}, bf16[256,...) custom-call(bf16[256,12288]{1,0:T(8,128)(2,1)} %bitcast.25, ...), custom_call_target="tpu_custom_call" | custom-call | flops 1 | bytes 1 | tf_op jit(solution)/shard_map/norm/pallas_call | solution.py:148
  56.8 1.9 %collective-permute-start.10 = (bf16[256,1152]{1,0:T(8,128)(2,1)}, bf16[256,1152]{1,0:T(8,128)(2,1)}, u32[]{:S(2)}, u32[]{:S(2)}) collective-permute-start(bf16[256,1152]{1,0:T(8,128)(2,1)} %get-tuple-element.47), channel_id=1, source_target_pairs={{0,2},{1,3},{2,4},{3,5},{4,6},{5,7},{6,0},{7,1},{8,10},{9,11},{10,... | collective-permute-start | bytes 1769480 | tf_op jit(solution)/shard_map/ppermute | solution.py:38
  58.7 3.2 %collective-permute-start.11 = (bf16[256,1152]{1,0:T(8,128)(2,1)}, bf16[256,1152]{1,0:T(8,128)(2,1)}, u32[]{:S(2)}, u32[]{:S(2)}) collective-permute-start(bf16[256,1152]{1,0:T(8,128)(2,1)} %get-tuple-element.48), channel_id=1, source_target_pairs={{0,4},{1,5},{2,6},{3,7},{4,0},{5,1},{6,2},{7,3},{8,12},{9,13},{10,... | collective-permute-start | bytes 1769480 | tf_op jit(solution)/shard_map/ppermute | solution.py:38
  64.0 5.4 %far_gradient.1 = (bf16[4,512,384]{2,1,0:T(8,128)(2,1)}, bf16[512,1024]{1,0:T(8,128)(2,1)S(1)}) custom-call(s32[4]{0:T(128)S(1)} %pad_add_fusion.targets_ref, bf16[4,256,2048]{2,1,0:T(8,128)(2,1)} %all-to-all-done.chunk), custom_call_target="tpu_custom_call" | custom-call | flops 99999997952 | bytes 1 | tf_op jit(solution)/shard_map/far_gradient/pallas_call | solution.py:202
  69.4 2.1 %collective-permute-start.13 = (bf16[256,384]{1,0:T(8,128)(2,1)}, bf16[256,384]{1,0:T(8,128)(2,1)}, u32[]{:S(2)}, u32[]{:S(2)}) collective-permute-start(bf16[256,384]{1,0:T(8,128)(2,1)} %get-tuple-element.66), channel_id=1, source_target_pairs={{0,2},{1,3},{2,4},{3,5},{4,6},{5,7},{6,0},{7,1},{8,10},{9,11},{10,... | collective-permute-start | bytes 589832 | tf_op jit(solution)/shard_map/ppermute | solution.py:38
  71.5 2.8 %collective-permute-start.14 = (bf16[256,384]{1,0:T(8,128)(2,1)}, bf16[256,384]{1,0:T(8,128)(2,1)}, u32[]{:S(2)}, u32[]{:S(2)}) collective-permute-start(bf16[256,384]{1,0:T(8,128)(2,1)} %get-tuple-element.67), channel_id=1, source_target_pairs={{0,4},{1,5},{2,6},{3,7},{4,0},{5,1},{6,2},{7,3},{8,12},{9,13},{10,... | collective-permute-start | bytes 589832 | tf_op jit(solution)/shard_map/ppermute | solution.py:38
  74.3 4.4 %all-to-all-start.1 = ((bf16[4,512,384]{2,1,0:T(8,128)(2,1)}), bf16[4,512,384]{2,1,0:T(8,128)(2,1)}, u32[]{:S(2)}, u32[]{:S(2)}) async-start(bf16[4,512,384]{2,1,0:T(8,128)(2,1)} %get-tuple-element.53), calls=%async_computation.1 | async-start | bytes 3145728 | tf_op jit(solution)/shard_map/all_to_all | solution.py:537
  78.7 5.5 %far_project.1.start_hbm = f32[4,256,512]{2,1,0:T(8,128)S(1)} custom-call(s32[4]{0:T(128)S(1)} %pad_add_fusion.1.sources_ref, bf16[4,256,2048]{2,1,0:T(8,128)(2,1)} %all-to-all-done.chunk, bf16[384,512]{1,0:T(8,128)(2,1)S(1)} %collective-permute-done.refs_0_, bf16[384,512]{1,0:T(8,128)(2,1)S(1)} %collective-permute-done.5.refs_1_, ...), custom_call_target="tpu_custom_call" | custom-call | flops 99999997952 | bytes 1 | tf_op jit(solution)/shard_map/far_project/pallas_call | solution.py:269
  89.9 4.2 %near_gradient.2 = bf16[4,512,384]{2,1,0:T(8,128)(2,1)} custom-call(s32[4]{0:T(128)S(1)} %pad_add_fusion.1.sources_ref, s32[4]{0:T(128)S(1)} %pad_add_fusion.targets_ref, bf16[512,1024]{1,0:T(8,128)(2,1)S(1)} %get-tuple-element.59.cots, bf16[256,1152]{1,0:T(8,128)(2,1)S(1)} %copy-done.4, bf16[256,1152]{1,0:T(8,128)(2,1)} %collective-permute-done.10.refs_1_, ...), custom_call_target="tpu_custom_call" | custom-call | flops 99999997952 | bytes 1 | tf_op jit(solution)/shard_map/near_gradient/pallas_call | solution.py:376
  94.1 5.2 %all-to-all-done.1.terms = bf16[4,512,384]{2,1,0:T(8,128)(2,1)} async-done(((bf16[4,512,384]{2,1,0:T(8,128)(2,1)}), bf16[4,512,384]{2,1,0:T(8,128)(2,1)}, u32[]{:S(2)}, u32[]{:S(2)}) %all-to-all-start.1) | async-done | bytes 1572896 | tf_op jit(solution)/shard_map/all_to_all | solution.py:537
  100.9 1.9 %collective-permute-start.16 = (bf16[512,384]{1,0:T(8,128)(2,1)S(1)}, bf16[512,384]{1,0:T(8,128)(2,1)S(1)}, u32[]{:S(2)}, u32[]{:S(2)}) collective-permute-start(bf16[512,384]{1,0:T(8,128)(2,1)S(1)} %add_up.1), channel_id=1, source_target_pairs={{0,1},{1,0},{2,3},{3,2},{4,5},{5,4},{6,7},{7,6},{8,9},{9,8},{10,11... | collective-permute-start | bytes 1179656 | tf_op jit(solution)/shard_map/ppermute | solution.py:38
  102.8 4.4 %all-to-all-start.2 = ((bf16[4,512,384]{2,1,0:T(8,128)(2,1)}), bf16[4,512,384]{2,1,0:T(8,128)(2,1)}, u32[]{:S(2)}, u32[]{:S(2)}) async-start(bf16[4,512,384]{2,1,0:T(8,128)(2,1)} %near_gradient.2), calls=%async_computation.2 | async-start | bytes 3145728 | tf_op jit(solution)/shard_map/all_to_all | solution.py:544
  107.9 5.9 %near_project.1 = (f32[256,512]{1,0:T(8,128)}, bf16[256,512]{1,0:T(8,128)(2,1)}, bf16[256,512]{1,0:T(8,128)(2,1)}, bf16[256,512]{1,0:T(8,128)(2,1)}) custom-call(f32[4,256,512]{2,1,0:T(8,128)} %copy-done.5, bf16[256,1152]{1,0:T(8,128)(2,1)} %get-tuple-element.46.refs_0_, bf16[256,1152]{1,0:T(8,128)(2,1)} %collective-permute-done.10.refs_1_, ...), custom_call_target="tpu_custom_call" | custom-call | flops 99999997952 | bytes 1 | tf_op jit(solution)/shard_map/near_project/pallas_call | solution.py:320
  121.1 1.8 %collective-permute-done.16.refs_2_ = bf16[512,384]{1,0:T(8,128)(2,1)S(1)} collective-permute-done((bf16[512,384]{1,0:T(8,128)(2,1)S(1)}, bf16[512,384]{1,0:T(8,128)(2,1)S(1)}, u32[]{:S(2)}, u32[]{:S(2)}) %collective-permute-start.16) | collective-permute-done | bytes 393248 | tf_op jit(solution)/shard_map/ppermute | solution.py:38
  122.9 3.0 %all-to-all-done.2.refs_0_ = bf16[4,512,384]{2,1,0:T(8,128)(2,1)} async-done(((bf16[4,512,384]{2,1,0:T(8,128)(2,1)}), bf16[4,512,384]{2,1,0:T(8,128)(2,1)}, u32[]{:S(2)}, u32[]{:S(2)}) %all-to-all-start.2) | async-done | bytes 1572896 | tf_op jit(solution)/shard_map/all_to_all | solution.py:544
  126.0 3.7 %update.1 = (bf16[384,512]{1,0:T(8,128)(2,1)}, f32[384,512]{1,0:T(8,128)}, f32[384,512]{1,0:T(8,128)}) custom-call(s32[1]{0:T(128)S(6)} %select_n.63.offset_ref, bf16[4,512,384]{2,1,0:T(8,128)(2,1)} %all-to-all-done.2.refs_0_, bf16[512,384]{1,0:T(8,128)(2,1)} %copy-done, bf16[512,384]{1,0:T(8,128)(2,1)} %copy-done.9, f32[384,128]{1,0:T(8,128)} %get-tuple-element.84.refs_3_, ...), custom_call_target="tpu_custom_call" | custom-call | flops 1 | bytes 1 | tf_op jit(solution)/shard_map/update/pallas_call | solution.py:456
  (76 shorter events, 24.4 us)
Async XLA Ops:
  6.7 57.3 %all-to-all-start = ((bf16[4,256,2048]{2,1,0:T(8,128)(2,1)}), bf16[4,256,2048]{2,1,0:T(8,128)(2,1)}, u32[]{:S(2)}, u32[]{:S(2)}) async-start(bf16[4,256,2048]{2,1,0:T(8,128)(2,1)} %norm.2), calls=%async_computation | async-start | bytes 8388608 | tf_op jit(solution)/shard_map/all_to_all | solution.py:506
  11.9 11.1 %collective-permute-start.1 = (f32[384,128]{1,0:T(8,128)S(1)}, f32[384,128]{1,0:T(8,128)S(1)}, u32[]{:S(2)}, u32[]{:S(2)}) collective-permute-start(f32[384,128]{1,0:T(8,128)S(1)} %convert_multiply_fusion), channel_id=1, source_target_pairs={{0,32},{32,0},{64,96},{96,64},{128,160},{160,128},{192,224},{224,1... | collective-permute-start | bytes 589832 | tf_op jit(solution)/shard_map/ppermute | solution.py:494
  12.0 24.6 %collective-permute-start = (bf16[384,512]{1,0:T(8,128)(2,1)S(1)}, bf16[384,512]{1,0:T(8,128)(2,1)S(1)}, u32[]{:S(2)}, u32[]{:S(2)}) collective-permute-start(bf16[384,512]{1,0:T(8,128)(2,1)S(1)} %bitcast.32), channel_id=1, source_target_pairs={{0,1},{1,0},{2,3},{3,2},{4,5},{5,4},{6,7},{7,6},{8,9},{9,8},{10,11... | collective-permute-start | bytes 1179656 | tf_op jit(solution)/shard_map/ppermute | solution.py:38
  18.4 20.1 %collective-permute-start.2 = (bf16[384,512]{1,0:T(8,128)(2,1)S(1)}, bf16[384,512]{1,0:T(8,128)(2,1)S(1)}, u32[]{:S(2)}, u32[]{:S(2)}) collective-permute-start(bf16[384,512]{1,0:T(8,128)(2,1)S(1)} %bitcast.33), channel_id=1, source_target_pairs={{0,24},{1,25},{2,26},{3,27},{4,28},{5,29},{6,30},{7,31},{8,0},{9,1... | collective-permute-start | bytes 1179656 | tf_op jit(solution)/shard_map/ppermute | solution.py:38
  21.4 17.1 %collective-permute-start.3 = (bf16[384,512]{1,0:T(8,128)(2,1)S(1)}, bf16[384,512]{1,0:T(8,128)(2,1)S(1)}, u32[]{:S(2)}, u32[]{:S(2)}) collective-permute-start(bf16[384,512]{1,0:T(8,128)(2,1)S(1)} %bitcast.34), channel_id=1, source_target_pairs={{0,16},{1,17},{2,18},{3,19},{4,20},{5,21},{6,22},{7,23},{8,24},{9,... | collective-permute-start | bytes 1179656 | tf_op jit(solution)/shard_map/ppermute | solution.py:38
  22.0 20.2 %collective-permute-start.4 = (bf16[384,512]{1,0:T(8,128)(2,1)S(1)}, bf16[384,512]{1,0:T(8,128)(2,1)S(1)}, u32[]{:S(2)}, u32[]{:S(2)}) collective-permute-start(bf16[384,512]{1,0:T(8,128)(2,1)S(1)} %bitcast.35), channel_id=1, source_target_pairs={{0,8},{1,9},{2,10},{3,11},{4,12},{5,13},{6,14},{7,15},{8,16},{9,17... | collective-permute-start | bytes 1179656 | tf_op jit(solution)/shard_map/ppermute | solution.py:38
  42.2 6.9 %collective-permute-start.8 = (f32[384,128]{1,0:T(8,128)S(1)}, f32[384,128]{1,0:T(8,128)S(1)}, u32[]{:S(2)}, u32[]{:S(2)}) collective-permute-start(f32[384,128]{1,0:T(8,128)S(1)} %fusion.1), channel_id=1, source_target_pairs={{0,64},{32,96},{64,0},{96,32},{128,192},{160,224},{192,128},{224,1... | collective-permute-start | bytes 589832 | tf_op jit(solution)/shard_map/ppermute | solution.py:494
  43.2 19.4 %collective-permute-start.5 = (bf16[384,512]{1,0:T(8,128)(2,1)S(1)}, bf16[384,512]{1,0:T(8,128)(2,1)S(1)}, u32[]{:S(2)}, u32[]{:S(2)}) collective-permute-start(bf16[384,512]{1,0:T(8,128)(2,1)S(1)} %collective-permute-done.refs_0_), channel_id=1, source_target_pairs={{0,24},{1,25},{2,26},{3,27},{4,28},{5,29},{6,30},{7,31},{8,0},{9,1... | collective-permute-start | bytes 1179656 | tf_op jit(solution)/shard_map/ppermute | solution.py:38
  43.8 20.0 %collective-permute-start.6 = (bf16[384,512]{1,0:T(8,128)(2,1)S(1)}, bf16[384,512]{1,0:T(8,128)(2,1)S(1)}, u32[]{:S(2)}, u32[]{:S(2)}) collective-permute-start(bf16[384,512]{1,0:T(8,128)(2,1)S(1)} %collective-permute-done.refs_0_), channel_id=1, source_target_pairs={{0,16},{1,17},{2,18},{3,19},{4,20},{5,21},{6,22},{7,23},{8,24},{9,... | collective-permute-start | bytes 1179656 | tf_op jit(solution)/shard_map/ppermute | solution.py:38
  44.5 19.6 %collective-permute-start.7 = (bf16[384,512]{1,0:T(8,128)(2,1)S(1)}, bf16[384,512]{1,0:T(8,128)(2,1)S(1)}, u32[]{:S(2)}, u32[]{:S(2)}) collective-permute-start(bf16[384,512]{1,0:T(8,128)(2,1)S(1)} %collective-permute-done.refs_0_), channel_id=1, source_target_pairs={{0,8},{1,9},{2,10},{3,11},{4,12},{5,13},{6,14},{7,15},{8,16},{9,17... | collective-permute-start | bytes 1179656 | tf_op jit(solution)/shard_map/ppermute | solution.py:38
  49.2 9.5 %collective-permute-start.9 = (f32[384,128]{1,0:T(8,128)S(1)}, f32[384,128]{1,0:T(8,128)S(1)}, u32[]{:S(2)}, u32[]{:S(2)}) collective-permute-start(f32[384,128]{1,0:T(8,128)S(1)} %add.80), channel_id=1, source_target_pairs={{0,128},{32,160},{64,192},{96,224},{128,0},{160,32},{192,64},{224,... | collective-permute-start | bytes 589832 | tf_op jit(solution)/shard_map/ppermute | solution.py:494
  56.8 28.8 %collective-permute-start.10 = (bf16[256,1152]{1,0:T(8,128)(2,1)}, bf16[256,1152]{1,0:T(8,128)(2,1)}, u32[]{:S(2)}, u32[]{:S(2)}) collective-permute-start(bf16[256,1152]{1,0:T(8,128)(2,1)} %get-tuple-element.47), channel_id=1, source_target_pairs={{0,2},{1,3},{2,4},{3,5},{4,6},{5,7},{6,0},{7,1},{8,10},{9,11},{10,... | collective-permute-start | bytes 1769480 | tf_op jit(solution)/shard_map/ppermute | solution.py:38
  58.7 30.0 %collective-permute-start.11 = (bf16[256,1152]{1,0:T(8,128)(2,1)}, bf16[256,1152]{1,0:T(8,128)(2,1)}, u32[]{:S(2)}, u32[]{:S(2)}) collective-permute-start(bf16[256,1152]{1,0:T(8,128)(2,1)} %get-tuple-element.48), channel_id=1, source_target_pairs={{0,4},{1,5},{2,6},{3,7},{4,0},{5,1},{6,2},{7,3},{8,12},{9,13},{10,... | collective-permute-start | bytes 1769480 | tf_op jit(solution)/shard_map/ppermute | solution.py:38
  62.6 27.3 %collective-permute-start.12 = (bf16[256,1152]{1,0:T(8,128)(2,1)}, bf16[256,1152]{1,0:T(8,128)(2,1)}, u32[]{:S(2)}, u32[]{:S(2)}) collective-permute-start(bf16[256,1152]{1,0:T(8,128)(2,1)} %get-tuple-element.49), channel_id=1, source_target_pairs={{0,6},{1,7},{2,0},{3,1},{4,2},{5,3},{6,4},{7,5},{8,14},{9,15},{10,... | collective-permute-start | bytes 1769480 | tf_op jit(solution)/shard_map/ppermute | solution.py:38
  69.4 37.8 %collective-permute-start.13 = (bf16[256,384]{1,0:T(8,128)(2,1)}, bf16[256,384]{1,0:T(8,128)(2,1)}, u32[]{:S(2)}, u32[]{:S(2)}) collective-permute-start(bf16[256,384]{1,0:T(8,128)(2,1)} %get-tuple-element.66), channel_id=1, source_target_pairs={{0,2},{1,3},{2,4},{3,5},{4,6},{5,7},{6,0},{7,1},{8,10},{9,11},{10,... | collective-permute-start | bytes 589832 | tf_op jit(solution)/shard_map/ppermute | solution.py:38
  71.5 35.7 %collective-permute-start.14 = (bf16[256,384]{1,0:T(8,128)(2,1)}, bf16[256,384]{1,0:T(8,128)(2,1)}, u32[]{:S(2)}, u32[]{:S(2)}) collective-permute-start(bf16[256,384]{1,0:T(8,128)(2,1)} %get-tuple-element.67), channel_id=1, source_target_pairs={{0,4},{1,5},{2,6},{3,7},{4,0},{5,1},{6,2},{7,3},{8,12},{9,13},{10,... | collective-permute-start | bytes 589832 | tf_op jit(solution)/shard_map/ppermute | solution.py:38
  74.3 25.0 %all-to-all-start.1 = ((bf16[4,512,384]{2,1,0:T(8,128)(2,1)}), bf16[4,512,384]{2,1,0:T(8,128)(2,1)}, u32[]{:S(2)}, u32[]{:S(2)}) async-start(bf16[4,512,384]{2,1,0:T(8,128)(2,1)} %get-tuple-element.53), calls=%async_computation.1 | async-start | bytes 3145728 | tf_op jit(solution)/shard_map/all_to_all | solution.py:537
  78.7 11.2 %copy-start.4 = (bf16[256,1152]{1,0:T(8,128)(2,1)S(1)}, bf16[256,1152]{1,0:T(8,128)(2,1)}, u32[]{:S(2)}) copy-start(bf16[256,1152]{1,0:T(8,128)(2,1)} %get-tuple-element.46.refs_0_) | copy-start | bytes 1769476
  85.6 21.7 %collective-permute-start.15 = (bf16[256,384]{1,0:T(8,128)(2,1)S(1)}, bf16[256,384]{1,0:T(8,128)(2,1)S(1)}, u32[]{:S(2)}, u32[]{:S(2)}) collective-permute-start(bf16[256,384]{1,0:T(8,128)(2,1)S(1)} %copy-done.17), channel_id=1, source_target_pairs={{0,6},{1,7},{2,0},{3,1},{4,2},{5,3},{6,4},{7,5},{8,14},{9,15},{10,... | collective-permute-start | bytes 589832 | tf_op jit(solution)/shard_map/ppermute | solution.py:38
  100.9 22.0 %collective-permute-start.16 = (bf16[512,384]{1,0:T(8,128)(2,1)S(1)}, bf16[512,384]{1,0:T(8,128)(2,1)S(1)}, u32[]{:S(2)}, u32[]{:S(2)}) collective-permute-start(bf16[512,384]{1,0:T(8,128)(2,1)S(1)} %add_up.1), channel_id=1, source_target_pairs={{0,1},{1,0},{2,3},{3,2},{4,5},{5,4},{6,7},{7,6},{8,9},{9,8},{10,11... | collective-permute-start | bytes 1179656 | tf_op jit(solution)/shard_map/ppermute | solution.py:38
  102.8 23.1 %all-to-all-start.2 = ((bf16[4,512,384]{2,1,0:T(8,128)(2,1)}), bf16[4,512,384]{2,1,0:T(8,128)(2,1)}, u32[]{:S(2)}, u32[]{:S(2)}) async-start(bf16[4,512,384]{2,1,0:T(8,128)(2,1)} %near_gradient.2), calls=%async_computation.2 | async-start | bytes 3145728 | tf_op jit(solution)/shard_map/all_to_all | solution.py:544
  113.8 15.8 %collective-permute-start.17 = (bf16[256,512]{1,0:T(8,128)(2,1)}, bf16[256,512]{1,0:T(8,128)(2,1)S(1)}, u32[]{:S(2)}, u32[]{:S(2)}) collective-permute-start(bf16[256,512]{1,0:T(8,128)(2,1)} %get-tuple-element.78), channel_id=1, source_target_pairs={{0,6},{1,7},{2,0},{3,1},{4,2},{5,3},{6,4},{7,5},{8,14},{9,15},{10,... | collective-permute-start | bytes 786440 | tf_op jit(solution)/shard_map/ppermute | solution.py:38
  115.3 14.4 %collective-permute-start.18 = (bf16[256,512]{1,0:T(8,128)(2,1)}, bf16[256,512]{1,0:T(8,128)(2,1)S(1)}, u32[]{:S(2)}, u32[]{:S(2)}) collective-permute-start(bf16[256,512]{1,0:T(8,128)(2,1)} %get-tuple-element.79), channel_id=1, source_target_pairs={{0,4},{1,5},{2,6},{3,7},{4,0},{5,1},{6,2},{7,3},{8,12},{9,13},{10,... | collective-permute-start | bytes 786440 | tf_op jit(solution)/shard_map/ppermute | solution.py:38
  115.8 13.9 %collective-permute-start.19 = (bf16[256,512]{1,0:T(8,128)(2,1)}, bf16[256,512]{1,0:T(8,128)(2,1)S(1)}, u32[]{:S(2)}, u32[]{:S(2)}) collective-permute-start(bf16[256,512]{1,0:T(8,128)(2,1)} %get-tuple-element.80), channel_id=1, source_target_pairs={{0,2},{1,3},{2,4},{3,5},{4,6},{5,7},{6,0},{7,1},{8,10},{9,11},{10,... | collective-permute-start | bytes 786440 | tf_op jit(solution)/shard_map/ppermute | solution.py:38
  (17 other events, 86.9 us)
